TPU v7x, 32 devices: a whole 2x2x4 slice. The times are simulated.
32 devices in a mesh: outer: 8 (over z, core), inner: 4 (over y, x).
Axes of the slice: x: 2, y: 2, z: 4, core: 2. Of those that a mesh axis runs over, the one named last changes fastest.
Arguments:
- queries: bfloat16 [4096, 32, 128], P(('outer', 'inner')), may hold values from -8 to 8
- keys: bfloat16 [4096, 4, 128], P(('outer', 'inner')), may hold values from -8 to 8
- values: bfloat16 [4096, 4, 128], P(('outer', 'inner')), may hold values from -6 to 6
- positions: int32 [4096], P(('outer', 'inner')), may hold values from 0 to 4095, as said below
Outputs:
- attended: bfloat16 [4096, 32, 128], P(('outer', 'inner'))
Inputs may be any that keep to these rules, and one draw needn't show every extreme that they name: positions is a permutation of the numbers 0 to 4095 made of runs of 64 consecutive ascending positions starting at multiples of 64; runs are laid out in an order drawn from the seed.
All inputs are finite; a program needn't handle non-finite values.
Results may differ from a plain program's by a relative error of at most 0.0045.
Values may be sent and summed in bfloat16 or wider, within the bound.
No kernel may reach another device: no remote copies, remote signals or barrier semaphores. Data moves between devices by JAX's collectives and lax.ppermute only.
A program may use at most 128 MiB of HBM per device.

v0:
```python
import functools
import math

import jax
import jax.numpy as jnp
from jax import lax
from jax.experimental import pallas as pl
from jax.experimental.pallas import tpu as pltpu
from jax.sharding import PartitionSpec as P

RUN = 64
TILE = 8
KEEP = 4
AXES = ("outer", "inner")


def flash(score, v, state, factor, live=None):
    top, mixed = state
    keys = score.shape[1]
    if isinstance(live, int):
        lane = lax.broadcasted_iota(jnp.int32, score.shape, 1)
        keys, live = live, lane < live
    if live is not None:
        score = jnp.where(live, score, -jnp.inf)
    parts = [score[:, c : c + 128] for c in range(0, score.shape[1], 128)]
    new = jnp.max(functools.reduce(jnp.maximum, parts), axis=1, keepdims=True)
    if top is None:
        new = jnp.broadcast_to(new, parts[0].shape)
    else:
        new = jnp.maximum(top, new)
    weights = [
        jnp.exp2((part - new) * factor).astype(jnp.bfloat16) for part in parts
    ]
    weights = jnp.concatenate(weights, axis=1)
    ones = jnp.ones((keys, 128), v.dtype)
    part_mixed = jnp.dot(
        weights[:, :keys],
        jnp.concatenate([v, ones], axis=1),
        preferred_element_type=jnp.float32,
    )
    if top is None:
        return new, part_mixed
    decay = jnp.exp2((top - new) * factor)
    halves = [
        mixed[:, c : c + 128] * decay + part_mixed[:, c : c + 128]
        for c in range(0, mixed.shape[1], 128)
    ]
    return new, jnp.concatenate(halves, axis=1)


def head_tile(q_ref, state_refs, a, keys, values, factor, live=None):
    def scores(h):
        return lax.dot_general(
            q_ref[a, h],
            keys(h),
            (((1,), (1,)), ((), ())),
            preferred_element_type=jnp.float32,
        )

    heads_kv = q_ref.shape[1]
    ahead = scores(0)
    for h in range(heads_kv):
        score = ahead
        if h + 1 < heads_kv:
            ahead = scores(h + 1)
        state = (None, None)
        if live is None or isinstance(live, int):
            state = tuple(ref[a, h] for ref in state_refs)
        state = flash(score, values(h), state, factor, live)
        for ref, value in zip(state_refs, state):
            ref[a, h] = value


def own_kernel(group, factor, half, q_ref, own_ref, meta_ref, *refs):
    heads_kv, rows, head_dim = q_ref.shape[1:]
    state_refs = refs[:2]
    run_rows = 2 * heads_kv * RUN

    ids = own_ref[2 * run_rows :].astype(jnp.float32)
    lane = lax.broadcasted_iota(jnp.int32, ids.shape, 1)
    numbers = [jnp.max(jnp.where(lane // RUN == a, ids, 0.0)) for a in range(2)]
    row = lax.broadcasted_iota(jnp.int32, meta_ref.shape, 0)
    meta_ref[...] = jnp.where(
        row == 0, numbers[0], jnp.where(row == 1, numbers[1], 0.0)
    )

    row_at = lax.broadcasted_iota(jnp.int32, (rows, 2 * RUN), 0) // group
    key_at = lax.broadcasted_iota(jnp.int32, (rows, 2 * RUN), 1)
    for a in range(2):
        mine, other = numbers[a], numbers[1 - a]
        seen = (other < mine) & ((other >= half) == (mine >= half))
        reach = jnp.where(seen, RUN, 0)
        if a == 0:
            live = (key_at <= row_at) | ((key_at >= RUN) & (key_at < RUN + reach))
        else:
            live = (key_at < reach) | ((key_at >= RUN) & (key_at - RUN <= row_at))

        def own(g):
            starts = [g * RUN, run_rows + g * RUN]
            return jnp.concatenate([own_ref[n : n + RUN] for n in starts])

        head_tile(q_ref, state_refs, a, own, lambda h: own(heads_kv + h), factor, live)


def attend_kernel(group, factor, half, last, keep, blocks, q_ref, *refs):
    heads_kv, rows, head_dim = q_ref.shape[1:]
    run_rows = 2 * heads_kv * RUN
    block_rows = 2 * run_rows + 16
    kv_refs, refs = refs[: len(blocks)], refs[len(blocks) :]
    refs = refs[4:]
    if last:
        out_ref, refs = refs[0], refs[1:]
    meta_ref, *state_refs, buf = refs[:4]

    meta = meta_ref[...]
    counts = tuple(
        jnp.max(meta[2 + a : 3 + a]).astype(jnp.int32) for a in range(2)
    )
    seen_bits = []
    for ref, (skip, end) in zip(kv_refs, blocks):
        assert end - skip <= 8
        ids = jnp.concatenate(
            [ref[n * block_rows - 16 : n * block_rows] for n in range(skip + 1, end + 1)]
        ).astype(jnp.float32)
        row = lax.broadcasted_iota(jnp.int32, ids.shape, 0)
        lane = lax.broadcasted_iota(jnp.int32, ids.shape, 1)
        bit = jnp.left_shift(1, 2 * (row // 16) + lane // RUN)
        bit = jnp.where((row % 16 == 0) & (lane % RUN == 0), bit, 0).astype(jnp.float32)
        found = []
        for a in range(2):
            mine = meta[a : a + 1]
            low = jnp.where(mine >= half, float(half), 0.0)
            seen = (ids < mine) & (ids >= low)
            found.append(jnp.sum(jnp.where(seen, bit, 0.0)).astype(jnp.int32))
        seen_bits.append(found)

    for ref, (skip, end), bits in zip(kv_refs, blocks, seen_bits):

        def gather(n, counts):
            at = pl.multiple_of((skip + n // 2) * block_rows + n % 2 * run_rows, 16)
            fresh = []
            for a in range(2):
                flag = (bits[a] >> n) & 1
                count = counts[a]

                @pl.when(flag == 1)
                def _():
                    buf[a, count] = ref[pl.ds(at, run_rows), :]

                fresh.append(count + flag)
            return tuple(fresh)

        counts = lax.fori_loop(0, 2 * (end - skip), gather, counts)

    def some_runs(a, start, runs):
        def rows_of(g):
            found = buf[a, pl.ds(start, runs), g * RUN : (g + 1) * RUN, :]
            return found.reshape(runs * RUN, -1)

        def keys(h):
            if runs > 1:
                return rows_of(h)
            return jnp.concatenate([rows_of(h), jnp.zeros((RUN, head_dim), buf.dtype)])

        live = RUN if runs == 1 else None
        head_tile(
            q_ref, state_refs, a, keys, lambda h: rows_of(heads_kv + h), factor, live
        )

    whole = [count // TILE for count in counts]

    def step(item, carry):
        a = (item >= whole[0]).astype(jnp.int32)
        some_runs(a, (item - a * whole[0]) * TILE, TILE)
        return carry

    lax.fori_loop(0, whole[0] + whole[1], step, 0)

    def remainder(a, carry):
        count = jnp.where(a == 0, counts[0], counts[1])
        start = count // TILE * TILE
        runs = TILE // 2
        while runs >= keep:

            @pl.when(count & runs != 0)
            def _():
                some_runs(a, start, runs)

            start = start + (count & runs)
            runs //= 2
        return carry

    lax.fori_loop(0, 2, remainder, 0)

    if not last:
        row = lax.broadcasted_iota(jnp.int32, meta.shape, 0)
        for a in range(2):
            start = counts[a] // keep * keep
            rest = counts[a] - start
            if keep > 1:

                @pl.when((start > 0) & (rest > 0))
                def _():
                    for n in range(keep - 1):
                        buf[a, n] = buf[a, start + n]

            meta = jnp.where(row == 2 + a, rest.astype(jnp.float32), meta)
        meta_ref[...] = meta
        return

    made, sems = refs[4:]
    copies = []
    for a in range(2):
        for h in range(0, heads_kv, 2):
            done = []
            for g in (h, h + 1):
                mixed = state_refs[1][a, g]
                part = mixed[:, :head_dim] * (1.0 / mixed[:, head_dim:])
                done.append(part.reshape(RUN, group, -1))
            place = (slice(a * RUN, (a + 1) * RUN), slice(h * group, (h + 2) * group))
            made[place] = jnp.concatenate(done, axis=1).astype(out_ref.dtype)
            copy = pltpu.make_async_copy(
                made.at[place], out_ref.at[place], sems.at[len(copies)]
            )
            copy.start()
            copies.append(copy)
    for copy in copies:
        copy.wait()


def pack_kernel(k_any, v_any, positions_any, own_ref, k_ref, v_ref, positions_ref, sems):
    pairs = ((k_any, k_ref), (v_any, v_ref), (positions_any, positions_ref))
    copies = [
        pltpu.make_async_copy(source, target, sems.at[n])
        for n, (source, target) in enumerate(pairs)
    ]
    for copy in copies:
        copy.start()
    heads_kv = k_ref.shape[0] // (2 * RUN)
    rows = heads_kv * RUN
    at = lax.broadcasted_iota(jnp.int32, (rows, rows), 0)
    origin = lax.broadcasted_iota(jnp.int32, (rows, rows), 1)
    move = at % RUN * heads_kv + at // RUN == origin
    move = jnp.where(move, 1.0, 0.0).astype(k_ref.dtype)
    for n, ref in enumerate((k_ref, v_ref)):
        copies[n].wait()
        for r in range(2):
            moved = jnp.dot(
                move,
                ref[r * rows : (r + 1) * rows],
                preferred_element_type=jnp.float32,
            )
            start = (2 * r + n) * rows
            own_ref[start : start + rows] = moved.astype(own_ref.dtype)
    copies[2].wait()
    numbers = (positions_ref[...] // RUN).astype(jnp.float32)
    numbers = jnp.broadcast_to(numbers, (16, numbers.shape[1]))
    own_ref[4 * rows :] = numbers.astype(own_ref.dtype)


class Attention:
    def __init__(self, q, group, half, room):
        self.q, self.group, self.half = q, group, half
        self.factor = math.log2(math.e) / math.sqrt(q.shape[3])
        heads_kv, rows, head_dim = q.shape[1:]
        self.block_rows = 4 * heads_kv * RUN + 16
        slots = 2 * room + TILE
        self.carried = [jax.ShapeDtypeStruct((8, 128), jnp.float32)]
        self.carried += [
            jax.ShapeDtypeStruct((2, heads_kv, rows, n), jnp.float32)
            for n in (128, head_dim + 128)
        ]
        self.carried.append(
            jax.ShapeDtypeStruct((2, slots, 2 * heads_kv * RUN, head_dim), q.dtype)
        )

    def call(self, kernel, operands, shapes, aliases, count, name, out=None):
        vmem = pl.BlockSpec(memory_space=pltpu.VMEM)
        out_specs = [vmem] * len(shapes)
        scratch = []
        if out is not None:
            shapes = [out, *shapes]
            out_specs.insert(0, pl.BlockSpec(memory_space=pl.ANY))
            scratch = [pltpu.VMEM(out.shape, out.dtype), pltpu.SemaphoreType.DMA((8,))]
        return pl.pallas_call(
            kernel,
            out_shape=shapes,
            in_specs=[vmem] * len(operands),
            out_specs=out_specs,
            scratch_shapes=scratch,
            input_output_aliases=aliases,
            compiler_params=pltpu.CompilerParams(vmem_limit_bytes=28 * 1024 * 1024),
            cost_estimate=pl.CostEstimate(
                flops=count * RUN * self.q.size * 4,
                bytes_accessed=self.q.size * 8,
                transcendentals=0,
            ),
            name=name,
        )(*operands)

    def start(self, own):
        kernel = functools.partial(own_kernel, self.group, self.factor, self.half)
        return self.call(kernel, [self.q, own], self.carried, {}, 2, "attend_own")

    def add(self, state, kvs, keep=KEEP, out=None):
        kvs = [x if isinstance(x, tuple) else (x, 0) for x in kvs]
        blocks = [(skip, x.shape[0] // self.block_rows) for x, skip in kvs]
        count = sum(end - skip for skip, end in blocks)
        operands = [self.q, *(x for x, _ in kvs), *state]
        first, ahead = 1 + len(kvs), int(out is not None)
        aliases = {first + n: ahead + n for n in range(len(state))}
        kernel = functools.partial(
            attend_kernel, self.group, self.factor, self.half, ahead, keep, blocks
        )
        results = self.call(kernel, operands, self.carried, aliases, count, "attend", out)
        return results[0] if ahead else results


def per_device(queries, keys, values, positions):
    outer, inner = lax.axis_size("outer"), lax.axis_size("inner")
    tokens, heads_q, head_dim = queries.shape
    heads_kv = keys.shape[1]
    group = heads_q // heads_kv
    half = tokens // RUN * outer * inner // 2

    chips = outer // 2
    bits = inner.bit_length() - 1
    ring = [0] + list(range(1, chips, 2)) + list(range(2, chips, 2))[::-1]
    after = {ring[n]: ring[(n + 1) % chips] for n in range(chips)}

    def permute(x, to):
        pairs = []
        for z in range(chips):
            for core in range(2):
                for place in range(inner):
                    nz, ncore, nplace = to(z, core, place)
                    pairs.append(
                        (
                            (2 * z + core) * inner + place,
                            (2 * nz + ncore) * inner + nplace,
                        )
                    )
        return lax.ppermute(x, AXES, pairs)

    def along_z(x):
        return permute(x, lambda z, core, place: (after[z], core, place))

    def over_place(x, step):
        def to(z, core, place):
            return z, core, place ^ (1 << (bits - 1 - step if core else step))

        return permute(x, to)

    def other_core(x):
        return permute(x, lambda z, core, place: (z, 1 - core, place))

    def tied(x, *others):
        return lax.optimization_barrier((x, *others))[0]

    flat = jax.ShapeDtypeStruct((tokens * heads_kv, head_dim), keys.dtype)
    own = pl.pallas_call(
        pack_kernel,
        out_shape=jax.ShapeDtypeStruct(
            (2 * tokens * heads_kv + 16, head_dim), keys.dtype
        ),
        in_specs=[pl.BlockSpec(memory_space=pltpu.HBM)] * 3,
        out_specs=pl.BlockSpec(memory_space=pltpu.VMEM),
        scratch_shapes=[
            pltpu.VMEM(flat.shape, flat.dtype),
            pltpu.VMEM(flat.shape, flat.dtype),
            pltpu.VMEM((1, tokens), jnp.int32),
            pltpu.SemaphoreType.DMA((3,)),
        ],
        compiler_params=pltpu.CompilerParams(vmem_limit_bytes=60 * 1024 * 1024),
        name="pack",
    )(keys.reshape(flat.shape), values.reshape(flat.shape), positions.reshape(1, tokens))
    q = (
        queries.reshape(2, RUN, heads_kv, group, head_dim)
        .transpose(0, 2, 1, 3, 4)
        .reshape(2, heads_kv, RUN * group, head_dim)
    )

    attention = Attention(q, group, half, 2 * inner)
    state = attention.start(own)

    stage, waiting = own, None
    for n in range(chips - 1):
        following = along_z(stage)
        held = stage
        for step in range(bits):
            if n == 0 and step + 1 == bits:
                held = tied(held, state[0])
            held = jnp.concatenate([held, over_place(held, step)])
        if waiting:
            state = attention.add(state, waiting)
            held = tied(held, state[0])
        waiting = [(held, int(n == 0)), other_core(held)]
        stage = following

    found = [stage]
    for step in range(bits):
        found += [over_place(x, step) for x in found]
    *most, final = found
    most = jnp.concatenate(most)
    theirs = other_core(most)
    state = attention.add(state, waiting)
    state = attention.add(state, [most, theirs])
    final = tied(final, state[0])
    theirs = other_core(final)
    state = attention.add(state, [final], keep=1)
    out = jax.ShapeDtypeStruct(queries.shape, queries.dtype)
    return attention.add(state, [theirs], keep=1, out=out)


def solution(mesh):
    in_specs = (
        P(("outer", "inner"), None, None),
        P(("outer", "inner"), None, None),
        P(("outer", "inner"), None, None),
        P(("outer", "inner")),
    )
    out_specs = P(("outer", "inner"), None, None)
    return jax.shard_map(
        per_device, mesh=mesh, in_specs=in_specs, out_specs=out_specs, check_vma=False
    )
```

profile of v0, /device:TPU:1, one launch (start us, length us, event | category | flops | bytes accessed | tf_op | source)
XLA Modules:
  0.0 62.7 jit_solution(5258379118644053868)
XLA Ops:
  0.0 2.1 %pack.1.own_ref = bf16[1040,128]{1,0:T(8,128)(2,1)} custom-call(bf16[512,128]{1,0:T(8,128)(2,1)} %bitcast.17, bf16[512,128]{1,0:T(8,128)(2,1)} %bitcast.18, s32[1,128]{1,0:T(1,128)} %bitcast.19), custom_call_target="tpu_custom_call" | custom-call | tf_op jit(solution)/shard_map/pack/pallas_call | solution.py:361
  2.1 0.0 copy-start
  2.1 2.1 %collective-permute-start.11 = (bf16[1040,128]{1,0:T(8,128)(2,1)}, bf16[1040,128]{1,0:T(8,128)(2,1)S(1)}, u32[]{:S(2)}, u32[]{:S(2)}) collective-permute-start(bf16[1040,128]{1,0:T(8,128)(2,1)} %pack.1.own_ref), channel_id=1, source_target_pairs={{0,1},{1,0},{2,3},{3,2},{4,6},{5,7},{6,4},{7,5},{8,9},{9,8},{10,11... | collective-permute-start | bytes 798728 | tf_op jit(solution)/shard_map/ppermute | solution.py:343
  4.2 1.3 %collective-permute-start = (bf16[1040,128]{1,0:T(8,128)(2,1)}, bf16[1040,128]{1,0:T(8,128)(2,1)S(1)}, u32[]{:S(2)}, u32[]{:S(2)}) collective-permute-start(bf16[1040,128]{1,0:T(8,128)(2,1)} %pack.1.own_ref), channel_id=1, source_target_pairs={{0,8},{1,9},{2,10},{3,11},{4,12},{5,13},{6,14},{7,15},{8,24},{9,25... | collective-permute-start | bytes 798728 | tf_op jit(solution)/shard_map/ppermute | solution.py:343
  5.5 1.4 %copy.31 = bf16[2,64,4,8,128]{4,3,1,2,0:T(8,128)(2,1)S(1)} copy(bf16[2,64,4,8,128]{4,3,2,1,0:T(8,128)(2,1)} %bitcast.16) | data formatting | bytes 2097152 | tf_op jit(solution)/shard_map/reshape | solution.py:378
  6.9 0.0 copy-done
  7.0 1.5 %attend_own.1 = (f32[8,128]{1,0:T(8,128)S(1)}, f32[2,4,512,128]{3,2,1,0:T(8,128)S(1)}, f32[2,4,512,256]{3,2,1,0:T(8,128)S(1)}, bf16[2,24,512,128]{3,2,1,0:T(8,128)(2,1)S(1)}) custom-call(bf16[2,4,512,128]{3,2,1,0:T(8,128)(2,1)S(1)} %bitcast.9, bf16[1040,128]{1,0:T(8,128)(2,1)S(1)} %copy-done), custom_call_target="tpu_custom_call" | custom-call | flops 268435456 | bytes 4194304 | tf_op jit(solution)/shard_map/attend_own/pallas_call | solution.py:285
  8.4 0.1 collective-permute-done.11
  8.6 1.5 %collective-permute-start.12 = (bf16[2080,128]{1,0:T(8,128)(2,1)S(1)}, bf16[2080,128]{1,0:T(8,128)(2,1)S(1)}, u32[]{:S(2)}, u32[]{:S(2)}) collective-permute-start(bf16[2080,128]{1,0:T(8,128)(2,1)S(1)} %pad_maximum_fusion.4), channel_id=1, source_target_pairs={{0,2},{1,3},{2,0},{3,1},{4,5},{5,4},{6,7},{7,6},{8,10},{9,11},{10,... | collective-permute-start | bytes 1597448 | tf_op jit(solution)/shard_map/ppermute | solution.py:343
  10.1 2.3 %collective-permute-done = bf16[1040,128]{1,0:T(8,128)(2,1)S(1)} collective-permute-done((bf16[1040,128]{1,0:T(8,128)(2,1)}, bf16[1040,128]{1,0:T(8,128)(2,1)S(1)}, u32[]{:S(2)}, u32[]{:S(2)}) %collective-permute-start) | collective-permute-done | bytes 266272 | tf_op jit(solution)/shard_map/ppermute | solution.py:343
  12.4 0.0 collective-permute-start.9
  12.4 0.6 collective-permute-start.1
  13.0 7.8 %collective-permute-done.9 = bf16[1040,128]{1,0:T(8,128)(2,1)S(1)} collective-permute-done((bf16[1040,128]{1,0:T(8,128)(2,1)S(1)}, bf16[1040,128]{1,0:T(8,128)(2,1)S(1)}, u32[]{:S(2)}, u32[]{:S(2)}) %collective-permute-start.9) | collective-permute-done | bytes 266272 | tf_op jit(solution)/shard_map/ppermute | solution.py:343
  20.9 2.6 %collective-permute-start.10 = (bf16[2080,128]{1,0:T(8,128)(2,1)S(1)}, bf16[2080,128]{1,0:T(8,128)(2,1)S(1)}, u32[]{:S(2)}, u32[]{:S(2)}) collective-permute-start(bf16[2080,128]{1,0:T(8,128)(2,1)S(1)} %pad_maximum_fusion.3), channel_id=1, source_target_pairs={{0,2},{1,3},{2,0},{3,1},{4,5},{5,4},{6,7},{7,6},{8,10},{9,11},{10,... | collective-permute-start | bytes 1597448 | tf_op jit(solution)/shard_map/ppermute | solution.py:343
  23.4 0.0 collective-permute-done.1
  23.4 0.0 collective-permute-start.7
  23.5 0.0 collective-permute-done.12
  23.5 0.1 constant_dynamic-update-slice_fusion.3.refs_0_
  23.5 1.6 %collective-permute-start.13 = (bf16[4160,128]{1,0:T(8,128)(2,1)S(1)}, bf16[4160,128]{1,0:T(8,128)(2,1)S(1)}, u32[]{:S(2)}, u32[]{:S(2)}) collective-permute-start(bf16[4160,128]{1,0:T(8,128)(2,1)S(1)} %constant_dynamic-update-slice_fusion.3.refs_0_), channel_id=1, source_target_pairs={{0,4},{1,5},{2,6},{3,7},{4,0},{5,1},{6,2},{7,3},{8,12},{9,13},{10,... | collective-permute-start | bytes 3194888 | tf_op jit(solution)/shard_map/ppermute | solution.py:343
  25.1 0.3 collective-permute-start.2
  25.3 6.6 %collective-permute-done.7 = bf16[1040,128]{1,0:T(8,128)(2,1)S(1)} collective-permute-done((bf16[1040,128]{1,0:T(8,128)(2,1)S(1)}, bf16[1040,128]{1,0:T(8,128)(2,1)S(1)}, u32[]{:S(2)}, u32[]{:S(2)}) %collective-permute-start.7) | collective-permute-done | bytes 266272 | tf_op jit(solution)/shard_map/ppermute | solution.py:343
  32.0 0.7 %collective-permute-start.8 = (bf16[2080,128]{1,0:T(8,128)(2,1)S(1)}, bf16[2080,128]{1,0:T(8,128)(2,1)S(1)}, u32[]{:S(2)}, u32[]{:S(2)}) collective-permute-start(bf16[2080,128]{1,0:T(8,128)(2,1)S(1)} %pad_maximum_fusion.2), channel_id=1, source_target_pairs={{0,2},{1,3},{2,0},{3,1},{4,5},{5,4},{6,7},{7,6},{8,10},{9,11},{10,... | collective-permute-start | bytes 1597448 | tf_op jit(solution)/shard_map/ppermute | solution.py:343
  32.6 0.6 collective-permute-done.10
  33.2 0.1 pad_maximum_fusion.1.refs_0_
  33.3 0.0 collective-permute-done.13.refs_1_
  33.3 2.8 %attend.6 = (f32[8,128]{1,0:T(8,128)S(1)}, f32[2,4,512,128]{3,2,1,0:T(8,128)S(1)}, f32[2,4,512,256]{3,2,1,0:T(8,128)S(1)}, bf16[2,24,512,128]{3,2,1,0:T(8,128)(2,1)S(1)}) custom-call(bf16[2,4,512,128]{3,2,1,0:T(8,128)(2,1)S(1)} %bitcast.10, ...), custom_call_target="tpu_custom_call", output_to_operand_aliasing={{0}: (3, {}), {1}: (4, {}), {2}: (5, {}), {3}: (6, {})} | custom-call | flops 939524096 | bytes 4194304 | tf_op jit(solution)/shard_map/attend/pallas_call | solution.py:285
  36.1 0.1 collective-permute-start.14
  36.2 0.0 collective-permute-done.2
  36.2 1.6 %collective-permute-start.3 = (bf16[1040,128]{1,0:T(8,128)(2,1)S(1)}, bf16[1040,128]{1,0:T(8,128)(2,1)S(1)}, u32[]{:S(2)}, u32[]{:S(2)}) collective-permute-start(bf16[1040,128]{1,0:T(8,128)(2,1)S(1)} %collective-permute-done.2), channel_id=1, source_target_pairs={{0,1},{1,0},{2,3},{3,2},{4,6},{5,7},{6,4},{7,5},{8,9},{9,8},{10,11... | collective-permute-start | bytes 798728 | tf_op jit(solution)/shard_map/ppermute | solution.py:343
  37.8 0.0 collective-permute-start.5
  37.9 3.1 %collective-permute-done.8 = bf16[2080,128]{1,0:T(8,128)(2,1)S(1)} collective-permute-done((bf16[2080,128]{1,0:T(8,128)(2,1)S(1)}, bf16[2080,128]{1,0:T(8,128)(2,1)S(1)}, u32[]{:S(2)}, u32[]{:S(2)}) %collective-permute-start.8) | collective-permute-done | bytes 532512 | tf_op jit(solution)/shard_map/ppermute | solution.py:343
  41.0 0.1 pad_maximum_fusion.refs_0_
  41.0 0.0 collective-permute-done.14.refs_1_
  41.0 2.9 %attend.7 = (f32[8,128]{1,0:T(8,128)S(1)}, f32[2,4,512,128]{3,2,1,0:T(8,128)S(1)}, f32[2,4,512,256]{3,2,1,0:T(8,128)S(1)}, bf16[2,24,512,128]{3,2,1,0:T(8,128)(2,1)S(1)}) custom-call(bf16[2,4,512,128]{3,2,1,0:T(8,128)(2,1)S(1)} %bitcast.11, ...), custom_call_target="tpu_custom_call", output_to_operand_aliasing={{0}: (3, {}), {1}: (4, {}), {2}: (5, {}), {3}: (6, {})} | custom-call | flops 1073741824 | bytes 4194304 | tf_op jit(solution)/shard_map/attend/pallas_call | solution.py:285
  44.0 3.2 %collective-permute-start.15 = (bf16[4160,128]{1,0:T(8,128)(2,1)S(1)}, bf16[4160,128]{1,0:T(8,128)(2,1)S(1)}, u32[]{:S(2)}, u32[]{:S(2)}) collective-permute-start(bf16[4160,128]{1,0:T(8,128)(2,1)S(1)} %pad_maximum_fusion.refs_0_), channel_id=1, source_target_pairs={{0,4},{1,5},{2,6},{3,7},{4,0},{5,1},{6,2},{7,3},{8,12},{9,13},{10,... | collective-permute-start | bytes 3194888 | tf_op jit(solution)/shard_map/ppermute | solution.py:343
  47.1 0.0 collective-permute-done.3
  47.2 0.0 collective-permute-done.5
  47.2 0.3 collective-permute-start.6
  47.6 1.6 %collective-permute-start.4 = (bf16[1040,128]{1,0:T(8,128)(2,1)S(1)}, bf16[1040,128]{1,0:T(8,128)(2,1)S(1)}, u32[]{:S(2)}, u32[]{:S(2)}) collective-permute-start(bf16[1040,128]{1,0:T(8,128)(2,1)S(1)} %collective-permute-done.3), channel_id=1, source_target_pairs={{0,2},{1,3},{2,0},{3,1},{4,5},{5,4},{6,7},{7,6},{8,10},{9,11},{10,... | collective-permute-start | bytes 798728 | tf_op jit(solution)/shard_map/ppermute | solution.py:343
  49.2 0.3 collective-permute-done.15.refs_1_
  49.5 3.7 %attend.8 = (f32[8,128]{1,0:T(8,128)S(1)}, f32[2,4,512,128]{3,2,1,0:T(8,128)S(1)}, f32[2,4,512,256]{3,2,1,0:T(8,128)S(1)}, bf16[2,24,512,128]{3,2,1,0:T(8,128)(2,1)S(1)}) custom-call(bf16[2,4,512,128]{3,2,1,0:T(8,128)(2,1)S(1)} %bitcast.12, ...), custom_call_target="tpu_custom_call", output_to_operand_aliasing={{0}: (3, {}), {1}: (4, {}), {2}: (5, {}), {3}: (6, {})} | custom-call | flops 1073741824 | bytes 4194304 | tf_op jit(solution)/shard_map/attend/pallas_call | solution.py:285
  53.2 0.0 collective-permute-done.6.refs_1_
  53.2 1.7 %attend.9 = (f32[8,128]{1,0:T(8,128)S(1)}, f32[2,4,512,128]{3,2,1,0:T(8,128)S(1)}, f32[2,4,512,256]{3,2,1,0:T(8,128)S(1)}, bf16[2,24,512,128]{3,2,1,0:T(8,128)(2,1)S(1)}) custom-call(bf16[2,4,512,128]{3,2,1,0:T(8,128)(2,1)S(1)} %bitcast.13, ...), custom_call_target="tpu_custom_call", output_to_operand_aliasing={{0}: (3, {}), {1}: (4, {}), {2}: (5, {}), {3}: (6, {})} | custom-call | flops 805306368 | bytes 4194304 | tf_op jit(solution)/shard_map/attend/pallas_call | solution.py:285
  54.9 0.0 collective-permute-done.4.refs_0_
  54.9 2.2 %collective-permute-start.16 = (bf16[1040,128]{1,0:T(8,128)(2,1)S(1)}, bf16[1040,128]{1,0:T(8,128)(2,1)S(1)}, u32[]{:S(2)}, u32[]{:S(2)}) collective-permute-start(bf16[1040,128]{1,0:T(8,128)(2,1)S(1)} %collective-permute-done.4.refs_0_), channel_id=1, source_target_pairs={{0,4},{1,5},{2,6},{3,7},{4,0},{5,1},{6,2},{7,3},{8,12},{9,13},{10,... | collective-permute-start | bytes 798728 | tf_op jit(solution)/shard_map/ppermute | solution.py:343
  57.1 3.2 %attend.10 = (f32[8,128]{1,0:T(8,128)S(1)}, f32[2,4,512,128]{3,2,1,0:T(8,128)S(1)}, f32[2,4,512,256]{3,2,1,0:T(8,128)S(1)}, bf16[2,24,512,128]{3,2,1,0:T(8,128)(2,1)S(1)}) custom-call(bf16[2,4,512,128]{3,2,1,0:T(8,128)(2,1)S(1)} %bitcast.14, ...), custom_call_target="tpu_custom_call", output_to_operand_aliasing={{0}: (2, {}), {1}: (3, {}), {2}: (4, {}), {3}: (5, {})} | custom-call | flops 134217728 | bytes 4194304 | tf_op jit(solution)/shard_map/attend/pallas_call | solution.py:285
  60.3 0.0 collective-permute-done.16.refs_0_
  60.3 2.3 %attend.11 = (bf16[128,32,128]{2,1,0:T(8,128)(2,1)}, f32[8,128]{1,0:T(8,128)S(1)}, f32[2,4,512,128]{3,2,1,0:T(8,128)S(1)}, f32[2,4,512,256]{3,2,1,0:T(8,128)S(1)}, bf16[2,24,512,128]{3,2,1,0:T(8,128)(2,1)S(1)}) custom-call(bf16[2,4,512,128]{3,2,1,0:T(8,128)(2,1)S(1)} %bitcast.15, ...), custom_call_target="tpu_custom_call", output_to_operand_aliasing={{1}: (2, {}), {2}: (3, {}), {3}: (4, {}), {4}: (5, {})} | custom-call | flops 134217728 | bytes 4194304 | tf_op jit(solution)/shard_map/attend/pallas_call | solution.py:285
  (7 shorter events, 0.2 us)
Async XLA Ops:
  2.1 4.9 %copy-start = (bf16[1040,128]{1,0:T(8,128)(2,1)S(1)}, bf16[1040,128]{1,0:T(8,128)(2,1)}, u32[]{:S(2)}) copy-start(bf16[1040,128]{1,0:T(8,128)(2,1)} %pack.1.own_ref) | copy-start | bytes 798724
  2.1 6.4 %collective-permute-start.11 = (bf16[1040,128]{1,0:T(8,128)(2,1)}, bf16[1040,128]{1,0:T(8,128)(2,1)S(1)}, u32[]{:S(2)}, u32[]{:S(2)}) collective-permute-start(bf16[1040,128]{1,0:T(8,128)(2,1)} %pack.1.own_ref), channel_id=1, source_target_pairs={{0,1},{1,0},{2,3},{3,2},{4,6},{5,7},{6,4},{7,5},{8,9},{9,8},{10,11... | collective-permute-start | bytes 798728 | tf_op jit(solution)/shard_map/ppermute | solution.py:343
  4.2 8.1 %collective-permute-start = (bf16[1040,128]{1,0:T(8,128)(2,1)}, bf16[1040,128]{1,0:T(8,128)(2,1)S(1)}, u32[]{:S(2)}, u32[]{:S(2)}) collective-permute-start(bf16[1040,128]{1,0:T(8,128)(2,1)} %pack.1.own_ref), channel_id=1, source_target_pairs={{0,8},{1,9},{2,10},{3,11},{4,12},{5,13},{6,14},{7,15},{8,24},{9,25... | collective-permute-start | bytes 798728 | tf_op jit(solution)/shard_map/ppermute | solution.py:343
  8.6 14.9 %collective-permute-start.12 = (bf16[2080,128]{1,0:T(8,128)(2,1)S(1)}, bf16[2080,128]{1,0:T(8,128)(2,1)S(1)}, u32[]{:S(2)}, u32[]{:S(2)}) collective-permute-start(bf16[2080,128]{1,0:T(8,128)(2,1)S(1)} %pad_maximum_fusion.4), channel_id=1, source_target_pairs={{0,2},{1,3},{2,0},{3,1},{4,5},{5,4},{6,7},{7,6},{8,10},{9,11},{10,... | collective-permute-start | bytes 1597448 | tf_op jit(solution)/shard_map/ppermute | solution.py:343
  12.4 8.5 %collective-permute-start.9 = (bf16[1040,128]{1,0:T(8,128)(2,1)S(1)}, bf16[1040,128]{1,0:T(8,128)(2,1)S(1)}, u32[]{:S(2)}, u32[]{:S(2)}) collective-permute-start(bf16[1040,128]{1,0:T(8,128)(2,1)S(1)} %collective-permute-done), channel_id=1, source_target_pairs={{0,1},{1,0},{2,3},{3,2},{4,6},{5,7},{6,4},{7,5},{8,9},{9,8},{10,11... | collective-permute-start | bytes 798728 | tf_op jit(solution)/shard_map/ppermute | solution.py:343
  12.4 11.0 %collective-permute-start.1 = (bf16[1040,128]{1,0:T(8,128)(2,1)S(1)}, bf16[1040,128]{1,0:T(8,128)(2,1)S(1)}, u32[]{:S(2)}, u32[]{:S(2)}) collective-permute-start(bf16[1040,128]{1,0:T(8,128)(2,1)S(1)} %collective-permute-done), channel_id=1, source_target_pairs={{0,8},{1,9},{2,10},{3,11},{4,12},{5,13},{6,14},{7,15},{8,24},{9,25... | collective-permute-start | bytes 798728 | tf_op jit(solution)/shard_map/ppermute | solution.py:343
  20.9 12.4 %collective-permute-start.10 = (bf16[2080,128]{1,0:T(8,128)(2,1)S(1)}, bf16[2080,128]{1,0:T(8,128)(2,1)S(1)}, u32[]{:S(2)}, u32[]{:S(2)}) collective-permute-start(bf16[2080,128]{1,0:T(8,128)(2,1)S(1)} %pad_maximum_fusion.3), channel_id=1, source_target_pairs={{0,2},{1,3},{2,0},{3,1},{4,5},{5,4},{6,7},{7,6},{8,10},{9,11},{10,... | collective-permute-start | bytes 1597448 | tf_op jit(solution)/shard_map/ppermute | solution.py:343
  23.4 8.5 %collective-permute-start.7 = (bf16[1040,128]{1,0:T(8,128)(2,1)S(1)}, bf16[1040,128]{1,0:T(8,128)(2,1)S(1)}, u32[]{:S(2)}, u32[]{:S(2)}) collective-permute-start(bf16[1040,128]{1,0:T(8,128)(2,1)S(1)} %collective-permute-done.1), channel_id=1, source_target_pairs={{0,1},{1,0},{2,3},{3,2},{4,6},{5,7},{6,4},{7,5},{8,9},{9,8},{10,11... | collective-permute-start | bytes 798728 | tf_op jit(solution)/shard_map/ppermute | solution.py:343
  23.5 9.8 %collective-permute-start.13 = (bf16[4160,128]{1,0:T(8,128)(2,1)S(1)}, bf16[4160,128]{1,0:T(8,128)(2,1)S(1)}, u32[]{:S(2)}, u32[]{:S(2)}) collective-permute-start(bf16[4160,128]{1,0:T(8,128)(2,1)S(1)} %constant_dynamic-update-slice_fusion.3.refs_0_), channel_id=1, source_target_pairs={{0,4},{1,5},{2,6},{3,7},{4,0},{5,1},{6,2},{7,3},{8,12},{9,13},{10,... | collective-permute-start | bytes 3194888 | tf_op jit(solution)/shard_map/ppermute | solution.py:343
  25.1 11.1 %collective-permute-start.2 = (bf16[1040,128]{1,0:T(8,128)(2,1)S(1)}, bf16[1040,128]{1,0:T(8,128)(2,1)S(1)}, u32[]{:S(2)}, u32[]{:S(2)}) collective-permute-start(bf16[1040,128]{1,0:T(8,128)(2,1)S(1)} %collective-permute-done.1), channel_id=1, source_target_pairs={{0,8},{1,9},{2,10},{3,11},{4,12},{5,13},{6,14},{7,15},{8,24},{9,25... | collective-permute-start | bytes 798728 | tf_op jit(solution)/shard_map/ppermute | solution.py:343
  32.0 9.0 %collective-permute-start.8 = (bf16[2080,128]{1,0:T(8,128)(2,1)S(1)}, bf16[2080,128]{1,0:T(8,128)(2,1)S(1)}, u32[]{:S(2)}, u32[]{:S(2)}) collective-permute-start(bf16[2080,128]{1,0:T(8,128)(2,1)S(1)} %pad_maximum_fusion.2), channel_id=1, source_target_pairs={{0,2},{1,3},{2,0},{3,1},{4,5},{5,4},{6,7},{7,6},{8,10},{9,11},{10,... | collective-permute-start | bytes 1597448 | tf_op jit(solution)/shard_map/ppermute | solution.py:343
  36.1 4.9 %collective-permute-start.14 = (bf16[4160,128]{1,0:T(8,128)(2,1)S(1)}, bf16[4160,128]{1,0:T(8,128)(2,1)S(1)}, u32[]{:S(2)}, u32[]{:S(2)}) collective-permute-start(bf16[4160,128]{1,0:T(8,128)(2,1)S(1)} %pad_maximum_fusion.1.refs_0_), channel_id=1, source_target_pairs={{0,4},{1,5},{2,6},{3,7},{4,0},{5,1},{6,2},{7,3},{8,12},{9,13},{10,... | collective-permute-start | bytes 3194888 | tf_op jit(solution)/shard_map/ppermute | solution.py:343
  36.2 11.0 %collective-permute-start.3 = (bf16[1040,128]{1,0:T(8,128)(2,1)S(1)}, bf16[1040,128]{1,0:T(8,128)(2,1)S(1)}, u32[]{:S(2)}, u32[]{:S(2)}) collective-permute-start(bf16[1040,128]{1,0:T(8,128)(2,1)S(1)} %collective-permute-done.2), channel_id=1, source_target_pairs={{0,1},{1,0},{2,3},{3,2},{4,6},{5,7},{6,4},{7,5},{8,9},{9,8},{10,11... | collective-permute-start | bytes 798728 | tf_op jit(solution)/shard_map/ppermute | solution.py:343
  37.8 9.4 %collective-permute-start.5 = (bf16[1040,128]{1,0:T(8,128)(2,1)S(1)}, bf16[1040,128]{1,0:T(8,128)(2,1)S(1)}, u32[]{:S(2)}, u32[]{:S(2)}) collective-permute-start(bf16[1040,128]{1,0:T(8,128)(2,1)S(1)} %collective-permute-done.2), channel_id=1, source_target_pairs={{0,2},{1,3},{2,0},{3,1},{4,5},{5,4},{6,7},{7,6},{8,10},{9,11},{10,... | collective-permute-start | bytes 798728 | tf_op jit(solution)/shard_map/ppermute | solution.py:343
  44.0 5.5 %collective-permute-start.15 = (bf16[4160,128]{1,0:T(8,128)(2,1)S(1)}, bf16[4160,128]{1,0:T(8,128)(2,1)S(1)}, u32[]{:S(2)}, u32[]{:S(2)}) collective-permute-start(bf16[4160,128]{1,0:T(8,128)(2,1)S(1)} %pad_maximum_fusion.refs_0_), channel_id=1, source_target_pairs={{0,4},{1,5},{2,6},{3,7},{4,0},{5,1},{6,2},{7,3},{8,12},{9,13},{10,... | collective-permute-start | bytes 3194888 | tf_op jit(solution)/shard_map/ppermute | solution.py:343
  47.2 5.9 %collective-permute-start.6 = (bf16[3120,128]{1,0:T(8,128)(2,1)S(1)}, bf16[3120,128]{1,0:T(8,128)(2,1)S(1)}, u32[]{:S(2)}, u32[]{:S(2)}) collective-permute-start(bf16[3120,128]{1,0:T(8,128)(2,1)S(1)} %constant_dynamic-update-slice_fusion.refs_0_), channel_id=1, source_target_pairs={{0,4},{1,5},{2,6},{3,7},{4,0},{5,1},{6,2},{7,3},{8,12},{9,13},{10,... | collective-permute-start | bytes 2396168 | tf_op jit(solution)/shard_map/ppermute | solution.py:343
  47.6 7.3 %collective-permute-start.4 = (bf16[1040,128]{1,0:T(8,128)(2,1)S(1)}, bf16[1040,128]{1,0:T(8,128)(2,1)S(1)}, u32[]{:S(2)}, u32[]{:S(2)}) collective-permute-start(bf16[1040,128]{1,0:T(8,128)(2,1)S(1)} %collective-permute-done.3), channel_id=1, source_target_pairs={{0,2},{1,3},{2,0},{3,1},{4,5},{5,4},{6,7},{7,6},{8,10},{9,11},{10,... | collective-permute-start | bytes 798728 | tf_op jit(solution)/shard_map/ppermute | solution.py:343
  54.9 5.4 %collective-permute-start.16 = (bf16[1040,128]{1,0:T(8,128)(2,1)S(1)}, bf16[1040,128]{1,0:T(8,128)(2,1)S(1)}, u32[]{:S(2)}, u32[]{:S(2)}) collective-permute-start(bf16[1040,128]{1,0:T(8,128)(2,1)S(1)} %collective-permute-done.4.refs_0_), channel_id=1, source_target_pairs={{0,4},{1,5},{2,6},{3,7},{4,0},{5,1},{6,2},{7,3},{8,12},{9,13},{10,... | collective-permute-start | bytes 798728 | tf_op jit(solution)/shard_map/ppermute | solution.py:343
where the time goes:
time: 62.7 us
  waiting for transfers between devices  20.8 us (33%)
  Pallas kernels  20.1 us (32%)
  starting transfers between devices  19.6 us (31%)
  local copies, waits for them, and re-layouts  1.61 us (3%)
    ppermute x17, waiting for transfers between devices, permute(): return lax.ppermute(x, AXES, pairs)  20.8 us
    ppermute x17, starting transfers between devices, permute(): return lax.ppermute(x, AXES, pairs)  19.6 us
    pallas_call x7, Pallas kernels, call(): pl.pallas_call(kernel, out_shape=shapes, in_specs=[vmem] * len(operands),...  18.1 us
    pallas_call x1, Pallas kernels, per_device(): pl.pallas_call(pack_kernel, out_shape=jax.ShapeDtypeStruct((2 * tokens *...  2.08 us
    reshape x1, local copies, waits for them, and re-layouts, per_device(): queries.reshape(2, RUN, heads_kv, group, head_dim).transpose(0, 2, 1, 3, 4)  1.41 us
  transfers between devices with their start and end apart: 17, of which 7 were waited for; matrix products, arithmetic and copies ran while one was open for 3% of the time, Pallas kernels for 25%

commit v1 on v0

--- a/solution.py
+++ b/solution.py
@@ -383,18 +383,35 @@
     attention = Attention(q, group, half, 2 * inner)
     state = attention.start(own)
 
-    stage, waiting = own, None
+    stage = own
+    halves, theirs = [], []
     for n in range(chips - 1):
         following = along_z(stage)
         held = stage
         for step in range(bits):
             if n == 0 and step + 1 == bits:
+                first = held
                 held = tied(held, state[0])
-            held = jnp.concatenate([held, over_place(held, step)])
-        if waiting:
-            state = attention.add(state, waiting)
+            there = over_place(held, step)
+            if n and step == 0:
+                if n == 1:
+                    kvs = [(halves[0][0], 1), theirs[0][0]]
+                else:
+                    kvs = [halves[n - 2][1], halves[n - 1][0], theirs[n - 2][-1]]
+                state = attention.add(state, kvs)
+                there = tied(there, state[0])
+            if step + 1 < bits:
+                held = jnp.concatenate([held, there])
+        halves.append((held, there))
+        if n == 0:
+            theirs.append([other_core(tied(first, following)), other_core(there)])
+            stage = following
+            continue
+        held = jnp.concatenate([held, there])
+        if n + 2 == chips:
+            state = attention.add(state, [halves[n - 1][1], theirs[n - 1][-1], halves[n][0]])
             held = tied(held, state[0])
-        waiting = [(held, int(n == 0)), other_core(held)]
+        theirs.append([other_core(held)])
         stage = following
 
     found = [stage]
@@ -402,9 +419,9 @@
         found += [over_place(x, step) for x in found]
     *most, final = found
     most = jnp.concatenate(most)
-    theirs = other_core(most)
-    state = attention.add(state, waiting)
-    state = attention.add(state, [most, theirs])
+    their_most = other_core(most)
+    state = attention.add(state, [halves[-1][1], theirs[-1][-1]])
+    state = attention.add(state, [most, their_most])
     final = tied(final, state[0])
     theirs = other_core(final)
     state = attention.add(state, [final], keep=1)

time: 62.7 us -> 62.7 us (level)
  the two profiles are of different devices: /device:TPU:1 before, /device:TPU:9 now
where the time goes in v1:
time: 62.7 us; the launch traced here: 61.7 us
  starting transfers between devices  24.4 us (39%)
  Pallas kernels  21.6 us (34%)
  waiting for transfers between devices  13.5 us (22%)
  local copies, waits for them, and re-layouts  1.62 us (3%)
    ppermute x18, starting transfers between devices, permute(): return lax.ppermute(x, AXES, pairs)  24.4 us
    pallas_call x8, Pallas kernels, call(): pl.pallas_call(kernel, out_shape=shapes, in_specs=[vmem] * len(operands),...  19.5 us
    ppermute x18, waiting for transfers between devices, permute(): return lax.ppermute(x, AXES, pairs)  13.5 us
    pallas_call x1, Pallas kernels, per_device(): pl.pallas_call(pack_kernel, out_shape=jax.ShapeDtypeStruct((2 * tokens *...  2.08 us
    reshape x1, local copies, waits for them, and re-layouts, per_device(): queries.reshape(2, RUN, heads_kv, group, head_dim).transpose(0, 2, 1, 3, 4)  1.41 us
  transfers between devices with their start and end apart: 18, of which 6 were waited for; matrix products, arithmetic and copies ran while one was open for 3% of the time, Pallas kernels for 28%

profile of v1, /device:TPU:9, one launch (start us, length us, event | category | flops | bytes accessed | tf_op | source)
XLA Modules:
  0.0 61.7 jit_solution(239899278656299430)
XLA Ops:
  0.0 2.1 %pack.1.own_ref = bf16[1040,128]{1,0:T(8,128)(2,1)} custom-call(bf16[512,128]{1,0:T(8,128)(2,1)} %bitcast.18, bf16[512,128]{1,0:T(8,128)(2,1)} %bitcast.19, s32[1,128]{1,0:T(1,128)} %bitcast.20), custom_call_target="tpu_custom_call" | custom-call | tf_op jit(solution)/shard_map/pack/pallas_call | solution.py:361
  2.1 0.0 copy-start
  2.1 1.3 %collective-permute-start.8 = (bf16[1040,128]{1,0:T(8,128)(2,1)}, bf16[1040,128]{1,0:T(8,128)(2,1)S(1)}, u32[]{:S(2)}, u32[]{:S(2)}) collective-permute-start(bf16[1040,128]{1,0:T(8,128)(2,1)} %pack.1.own_ref), channel_id=1, source_target_pairs={{0,1},{1,0},{2,3},{3,2},{4,6},{5,7},{6,4},{7,5},{8,9},{9,8},{10,11... | collective-permute-start | bytes 798728 | tf_op jit(solution)/shard_map/ppermute | solution.py:343
  3.4 2.3 %collective-permute-start = (bf16[1040,128]{1,0:T(8,128)(2,1)}, bf16[1040,128]{1,0:T(8,128)(2,1)S(1)}, u32[]{:S(2)}, u32[]{:S(2)}) collective-permute-start(bf16[1040,128]{1,0:T(8,128)(2,1)} %pack.1.own_ref), channel_id=1, source_target_pairs={{0,8},{1,9},{2,10},{3,11},{4,12},{5,13},{6,14},{7,15},{8,24},{9,25... | collective-permute-start | bytes 798728 | tf_op jit(solution)/shard_map/ppermute | solution.py:343
  5.7 1.4 %copy.35 = bf16[2,64,4,8,128]{4,3,1,2,0:T(8,128)(2,1)S(1)} copy(bf16[2,64,4,8,128]{4,3,2,1,0:T(8,128)(2,1)} %bitcast.17) | data formatting | bytes 2097152 | tf_op jit(solution)/shard_map/reshape | solution.py:378
  7.1 1.5 %attend_own.1 = (f32[8,128]{1,0:T(8,128)S(1)}, f32[2,4,512,128]{3,2,1,0:T(8,128)S(1)}, f32[2,4,512,256]{3,2,1,0:T(8,128)S(1)}, bf16[2,24,512,128]{3,2,1,0:T(8,128)(2,1)S(1)}) custom-call(bf16[2,4,512,128]{3,2,1,0:T(8,128)(2,1)S(1)} %bitcast.9, bf16[1040,128]{1,0:T(8,128)(2,1)S(1)} %copy-done), custom_call_target="tpu_custom_call" | custom-call | flops 268435456 | bytes 4194304 | tf_op jit(solution)/shard_map/attend_own/pallas_call | solution.py:285
  8.6 0.0 collective-permute-done.8
  8.7 1.3 %collective-permute-start.9 = (bf16[2080,128]{1,0:T(8,128)(2,1)S(1)}, bf16[2080,128]{1,0:T(8,128)(2,1)S(1)}, u32[]{:S(2)}, u32[]{:S(2)}) collective-permute-start(bf16[2080,128]{1,0:T(8,128)(2,1)S(1)} %pad_maximum_fusion.2.refs_0_), channel_id=1, source_target_pairs={{0,2},{1,3},{2,0},{3,1},{4,5},{5,4},{6,7},{7,6},{8,10},{9,11},{10,... | collective-permute-start | bytes 1597448 | tf_op jit(solution)/shard_map/ppermute | solution.py:343
  10.0 0.8 %collective-permute-done = bf16[1040,128]{1,0:T(8,128)(2,1)S(1)} collective-permute-done((bf16[1040,128]{1,0:T(8,128)(2,1)}, bf16[1040,128]{1,0:T(8,128)(2,1)S(1)}, u32[]{:S(2)}, u32[]{:S(2)}) %collective-permute-start) | collective-permute-done | bytes 266272 | tf_op jit(solution)/shard_map/ppermute | solution.py:343
  10.8 1.8 %collective-permute-start.11 = (bf16[2080,128]{1,0:T(8,128)(2,1)S(1)}, bf16[2080,128]{1,0:T(8,128)(2,1)S(1)}, u32[]{:S(2)}, u32[]{:S(2)}) collective-permute-start(bf16[2080,128]{1,0:T(8,128)(2,1)S(1)} %pad_maximum_fusion.2.refs_0_), channel_id=1, source_target_pairs={{0,4},{1,5},{2,6},{3,7},{4,0},{5,1},{6,2},{7,3},{8,12},{9,13},{10,... | collective-permute-start | bytes 1597448 | tf_op jit(solution)/shard_map/ppermute | solution.py:343
  12.6 3.0 %collective-permute-start.1 = (bf16[1040,128]{1,0:T(8,128)(2,1)S(1)}, bf16[1040,128]{1,0:T(8,128)(2,1)S(1)}, u32[]{:S(2)}, u32[]{:S(2)}) collective-permute-start(bf16[1040,128]{1,0:T(8,128)(2,1)S(1)} %collective-permute-done), channel_id=1, source_target_pairs={{0,8},{1,9},{2,10},{3,11},{4,12},{5,13},{6,14},{7,15},{8,24},{9,25... | collective-permute-start | bytes 798728 | tf_op jit(solution)/shard_map/ppermute | solution.py:343
  15.6 0.2 collective-permute-start.10
  15.9 1.3 %collective-permute-done.9.refs_0_ = bf16[2080,128]{1,0:T(8,128)(2,1)S(1)} collective-permute-done((bf16[2080,128]{1,0:T(8,128)(2,1)S(1)}, bf16[2080,128]{1,0:T(8,128)(2,1)S(1)}, u32[]{:S(2)}, u32[]{:S(2)}) %collective-permute-start.9) | collective-permute-done | bytes 532512 | tf_op jit(solution)/shard_map/ppermute | solution.py:343
  17.2 2.5 %collective-permute-start.12 = (bf16[2080,128]{1,0:T(8,128)(2,1)S(1)}, bf16[2080,128]{1,0:T(8,128)(2,1)S(1)}, u32[]{:S(2)}, u32[]{:S(2)}) collective-permute-start(bf16[2080,128]{1,0:T(8,128)(2,1)S(1)} %collective-permute-done.9.refs_0_), channel_id=1, source_target_pairs={{0,4},{1,5},{2,6},{3,7},{4,0},{5,1},{6,2},{7,3},{8,12},{9,13},{10,... | collective-permute-start | bytes 1597448 | tf_op jit(solution)/shard_map/ppermute | solution.py:343
  19.7 1.8 %collective-permute-done.1 = bf16[1040,128]{1,0:T(8,128)(2,1)S(1)} collective-permute-done((bf16[1040,128]{1,0:T(8,128)(2,1)S(1)}, bf16[1040,128]{1,0:T(8,128)(2,1)S(1)}, u32[]{:S(2)}, u32[]{:S(2)}) %collective-permute-start.1) | collective-permute-done | bytes 266272 | tf_op jit(solution)/shard_map/ppermute | solution.py:343
  21.5 0.5 collective-permute-start.7
  22.0 3.4 %collective-permute-start.2 = (bf16[1040,128]{1,0:T(8,128)(2,1)S(1)}, bf16[1040,128]{1,0:T(8,128)(2,1)S(1)}, u32[]{:S(2)}, u32[]{:S(2)}) collective-permute-start(bf16[1040,128]{1,0:T(8,128)(2,1)S(1)} %collective-permute-done.1), channel_id=1, source_target_pairs={{0,8},{1,9},{2,10},{3,11},{4,12},{5,13},{6,14},{7,15},{8,24},{9,25... | collective-permute-start | bytes 798728 | tf_op jit(solution)/shard_map/ppermute | solution.py:343
  25.3 0.0 collective-permute-done.11.refs_1_
  25.3 1.5 %attend.7 = (f32[8,128]{1,0:T(8,128)S(1)}, f32[2,4,512,128]{3,2,1,0:T(8,128)S(1)}, f32[2,4,512,256]{3,2,1,0:T(8,128)S(1)}, bf16[2,24,512,128]{3,2,1,0:T(8,128)(2,1)S(1)}) custom-call(bf16[2,4,512,128]{3,2,1,0:T(8,128)(2,1)S(1)} %bitcast.10, ...), custom_call_target="tpu_custom_call", output_to_operand_aliasing={{0}: (3, {}), {1}: (4, {}), {2}: (5, {}), {3}: (6, {})} | custom-call | flops 402653184 | bytes 4194304 | tf_op jit(solution)/shard_map/attend/pallas_call | solution.py:285
  26.8 0.0 collective-permute-done.10
  26.9 0.2 collective-permute-start.14
  27.1 0.0 collective-permute-done.12.refs_2_
  27.1 2.2 %attend.8 = (f32[8,128]{1,0:T(8,128)S(1)}, f32[2,4,512,128]{3,2,1,0:T(8,128)S(1)}, f32[2,4,512,256]{3,2,1,0:T(8,128)S(1)}, bf16[2,24,512,128]{3,2,1,0:T(8,128)(2,1)S(1)}) custom-call(bf16[2,4,512,128]{3,2,1,0:T(8,128)(2,1)S(1)} %bitcast.11, ...), custom_call_target="tpu_custom_call", output_to_operand_aliasing={{0}: (4, {}), {1}: (5, {}), {2}: (6, {}), {3}: (7, {})} | custom-call | flops 805306368 | bytes 4194304 | tf_op jit(solution)/shard_map/attend/pallas_call | solution.py:285
  29.3 0.0 collective-permute-done.7
  29.4 1.4 %collective-permute-start.13 = (bf16[2080,128]{1,0:T(8,128)(2,1)S(1)}, bf16[2080,128]{1,0:T(8,128)(2,1)S(1)}, u32[]{:S(2)}, u32[]{:S(2)}) collective-permute-start(bf16[2080,128]{1,0:T(8,128)(2,1)S(1)} %constant_dynamic-update-slice_fusion.5.refs_2_), channel_id=1, source_target_pairs={{0,2},{1,3},{2,0},{3,1},{4,5},{5,4},{6,7},{7,6},{8,10},{9,11},{10,... | collective-permute-start | bytes 1597448 | tf_op jit(solution)/shard_map/ppermute | solution.py:343
  30.8 4.6 %collective-permute-done.14.refs_0_ = bf16[2080,128]{1,0:T(8,128)(2,1)S(1)} collective-permute-done((bf16[2080,128]{1,0:T(8,128)(2,1)S(1)}, bf16[2080,128]{1,0:T(8,128)(2,1)S(1)}, u32[]{:S(2)}, u32[]{:S(2)}) %collective-permute-start.14) | collective-permute-done | bytes 532512 | tf_op jit(solution)/shard_map/ppermute | solution.py:343
  35.4 0.1 pad_maximum_fusion.1
  35.4 1.6 %collective-permute-start.15 = (bf16[4160,128]{1,0:T(8,128)(2,1)S(1)}, bf16[4160,128]{1,0:T(8,128)(2,1)S(1)}, u32[]{:S(2)}, u32[]{:S(2)}) collective-permute-start(bf16[4160,128]{1,0:T(8,128)(2,1)S(1)} %pad_maximum_fusion.1), channel_id=1, source_target_pairs={{0,4},{1,5},{2,6},{3,7},{4,0},{5,1},{6,2},{7,3},{8,12},{9,13},{10,... | collective-permute-start | bytes 3194888 | tf_op jit(solution)/shard_map/ppermute | solution.py:343
  37.0 0.0 collective-permute-done.2
  37.0 0.2 collective-permute-start.3
  37.2 0.3 collective-permute-start.5
  37.5 4.3 %collective-permute-done.13.refs_0_ = bf16[2080,128]{1,0:T(8,128)(2,1)S(1)} collective-permute-done((bf16[2080,128]{1,0:T(8,128)(2,1)S(1)}, bf16[2080,128]{1,0:T(8,128)(2,1)S(1)}, u32[]{:S(2)}, u32[]{:S(2)}) %collective-permute-start.13) | collective-permute-done | bytes 532512 | tf_op jit(solution)/shard_map/ppermute | solution.py:343
  41.8 0.1 pad_maximum_fusion
  41.9 0.0 collective-permute-done.15.refs_1_
  41.9 2.5 %attend.9 = (f32[8,128]{1,0:T(8,128)S(1)}, f32[2,4,512,128]{3,2,1,0:T(8,128)S(1)}, f32[2,4,512,256]{3,2,1,0:T(8,128)S(1)}, bf16[2,24,512,128]{3,2,1,0:T(8,128)(2,1)S(1)}) custom-call(bf16[2,4,512,128]{3,2,1,0:T(8,128)(2,1)S(1)} %bitcast.12, ...), custom_call_target="tpu_custom_call", output_to_operand_aliasing={{0}: (4, {}), {1}: (5, {}), {2}: (6, {}), {3}: (7, {})} | custom-call | flops 1073741824 | bytes 4194304 | tf_op jit(solution)/shard_map/attend/pallas_call | solution.py:285
  44.4 2.7 %collective-permute-start.16 = (bf16[4160,128]{1,0:T(8,128)(2,1)S(1)}, bf16[4160,128]{1,0:T(8,128)(2,1)S(1)}, u32[]{:S(2)}, u32[]{:S(2)}) collective-permute-start(bf16[4160,128]{1,0:T(8,128)(2,1)S(1)} %pad_maximum_fusion), channel_id=1, source_target_pairs={{0,4},{1,5},{2,6},{3,7},{4,0},{5,1},{6,2},{7,3},{8,12},{9,13},{10,... | collective-permute-start | bytes 3194888 | tf_op jit(solution)/shard_map/ppermute | solution.py:343
  47.1 0.0 collective-permute-done.3
  47.1 0.0 collective-permute-done.5
  47.2 1.2 %collective-permute-start.6 = (bf16[3120,128]{1,0:T(8,128)(2,1)S(1)}, bf16[3120,128]{1,0:T(8,128)(2,1)S(1)}, u32[]{:S(2)}, u32[]{:S(2)}) collective-permute-start(bf16[3120,128]{1,0:T(8,128)(2,1)S(1)} %constant_dynamic-update-slice_fusion.refs_0_), channel_id=1, source_target_pairs={{0,4},{1,5},{2,6},{3,7},{4,0},{5,1},{6,2},{7,3},{8,12},{9,13},{10,... | collective-permute-start | bytes 2396168 | tf_op jit(solution)/shard_map/ppermute | solution.py:343
  48.4 0.3 collective-permute-start.4
  48.6 0.8 %collective-permute-done.16.refs_1_ = bf16[4160,128]{1,0:T(8,128)(2,1)S(1)} collective-permute-done((bf16[4160,128]{1,0:T(8,128)(2,1)S(1)}, bf16[4160,128]{1,0:T(8,128)(2,1)S(1)}, u32[]{:S(2)}, u32[]{:S(2)}) %collective-permute-start.16) | collective-permute-done | bytes 1064992 | tf_op jit(solution)/shard_map/ppermute | solution.py:343
  49.4 3.4 %attend.10 = (f32[8,128]{1,0:T(8,128)S(1)}, f32[2,4,512,128]{3,2,1,0:T(8,128)S(1)}, f32[2,4,512,256]{3,2,1,0:T(8,128)S(1)}, bf16[2,24,512,128]{3,2,1,0:T(8,128)(2,1)S(1)}) custom-call(bf16[2,4,512,128]{3,2,1,0:T(8,128)(2,1)S(1)} %bitcast.13, ...), custom_call_target="tpu_custom_call", output_to_operand_aliasing={{0}: (3, {}), {1}: (4, {}), {2}: (5, {}), {3}: (6, {})} | custom-call | flops 805306368 | bytes 4194304 | tf_op jit(solution)/shard_map/attend/pallas_call | solution.py:285
  52.9 1.7 %attend.11 = (f32[8,128]{1,0:T(8,128)S(1)}, f32[2,4,512,128]{3,2,1,0:T(8,128)S(1)}, f32[2,4,512,256]{3,2,1,0:T(8,128)S(1)}, bf16[2,24,512,128]{3,2,1,0:T(8,128)(2,1)S(1)}) custom-call(bf16[2,4,512,128]{3,2,1,0:T(8,128)(2,1)S(1)} %bitcast.14, ...), custom_call_target="tpu_custom_call", output_to_operand_aliasing={{0}: (3, {}), {1}: (4, {}), {2}: (5, {}), {3}: (6, {})} | custom-call | flops 805306368 | bytes 4194304 | tf_op jit(solution)/shard_map/attend/pallas_call | solution.py:285
  54.6 0.0 collective-permute-done.4.refs_0_
  54.6 0.3 collective-permute-start.17
  54.9 4.1 %attend.12 = (f32[8,128]{1,0:T(8,128)S(1)}, f32[2,4,512,128]{3,2,1,0:T(8,128)S(1)}, f32[2,4,512,256]{3,2,1,0:T(8,128)S(1)}, bf16[2,24,512,128]{3,2,1,0:T(8,128)(2,1)S(1)}) custom-call(bf16[2,4,512,128]{3,2,1,0:T(8,128)(2,1)S(1)} %bitcast.15, ...), custom_call_target="tpu_custom_call", output_to_operand_aliasing={{0}: (2, {}), {1}: (3, {}), {2}: (4, {}), {3}: (5, {})} | custom-call | flops 134217728 | bytes 4194304 | tf_op jit(solution)/shard_map/attend/pallas_call | solution.py:285
  59.0 0.0 collective-permute-done.17.refs_0_
  59.0 2.5 %attend.13 = (bf16[128,32,128]{2,1,0:T(8,128)(2,1)}, f32[8,128]{1,0:T(8,128)S(1)}, f32[2,4,512,128]{3,2,1,0:T(8,128)S(1)}, f32[2,4,512,256]{3,2,1,0:T(8,128)S(1)}, bf16[2,24,512,128]{3,2,1,0:T(8,128)(2,1)S(1)}) custom-call(bf16[2,4,512,128]{3,2,1,0:T(8,128)(2,1)S(1)} %bitcast.16, ...), custom_call_target="tpu_custom_call", output_to_operand_aliasing={{1}: (2, {}), {2}: (3, {}), {3}: (4, {}), {4}: (5, {})} | custom-call | flops 134217728 | bytes 4194304 | tf_op jit(solution)/shard_map/attend/pallas_call | solution.py:285
  (10 shorter events, 0.2 us)
Async XLA Ops:
  2.1 5.0 %copy-start = (bf16[1040,128]{1,0:T(8,128)(2,1)S(1)}, bf16[1040,128]{1,0:T(8,128)(2,1)}, u32[]{:S(2)}) copy-start(bf16[1040,128]{1,0:T(8,128)(2,1)} %pack.1.own_ref) | copy-start | bytes 798724
  2.1 6.5 %collective-permute-start.8 = (bf16[1040,128]{1,0:T(8,128)(2,1)}, bf16[1040,128]{1,0:T(8,128)(2,1)S(1)}, u32[]{:S(2)}, u32[]{:S(2)}) collective-permute-start(bf16[1040,128]{1,0:T(8,128)(2,1)} %pack.1.own_ref), channel_id=1, source_target_pairs={{0,1},{1,0},{2,3},{3,2},{4,6},{5,7},{6,4},{7,5},{8,9},{9,8},{10,11... | collective-permute-start | bytes 798728 | tf_op jit(solution)/shard_map/ppermute | solution.py:343
  3.4 7.4 %collective-permute-start = (bf16[1040,128]{1,0:T(8,128)(2,1)}, bf16[1040,128]{1,0:T(8,128)(2,1)S(1)}, u32[]{:S(2)}, u32[]{:S(2)}) collective-permute-start(bf16[1040,128]{1,0:T(8,128)(2,1)} %pack.1.own_ref), channel_id=1, source_target_pairs={{0,8},{1,9},{2,10},{3,11},{4,12},{5,13},{6,14},{7,15},{8,24},{9,25... | collective-permute-start | bytes 798728 | tf_op jit(solution)/shard_map/ppermute | solution.py:343
  8.7 8.5 %collective-permute-start.9 = (bf16[2080,128]{1,0:T(8,128)(2,1)S(1)}, bf16[2080,128]{1,0:T(8,128)(2,1)S(1)}, u32[]{:S(2)}, u32[]{:S(2)}) collective-permute-start(bf16[2080,128]{1,0:T(8,128)(2,1)S(1)} %pad_maximum_fusion.2.refs_0_), channel_id=1, source_target_pairs={{0,2},{1,3},{2,0},{3,1},{4,5},{5,4},{6,7},{7,6},{8,10},{9,11},{10,... | collective-permute-start | bytes 1597448 | tf_op jit(solution)/shard_map/ppermute | solution.py:343
  10.8 14.5 %collective-permute-start.11 = (bf16[2080,128]{1,0:T(8,128)(2,1)S(1)}, bf16[2080,128]{1,0:T(8,128)(2,1)S(1)}, u32[]{:S(2)}, u32[]{:S(2)}) collective-permute-start(bf16[2080,128]{1,0:T(8,128)(2,1)S(1)} %pad_maximum_fusion.2.refs_0_), channel_id=1, source_target_pairs={{0,4},{1,5},{2,6},{3,7},{4,0},{5,1},{6,2},{7,3},{8,12},{9,13},{10,... | collective-permute-start | bytes 1597448 | tf_op jit(solution)/shard_map/ppermute | solution.py:343
  12.6 8.8 %collective-permute-start.1 = (bf16[1040,128]{1,0:T(8,128)(2,1)S(1)}, bf16[1040,128]{1,0:T(8,128)(2,1)S(1)}, u32[]{:S(2)}, u32[]{:S(2)}) collective-permute-start(bf16[1040,128]{1,0:T(8,128)(2,1)S(1)} %collective-permute-done), channel_id=1, source_target_pairs={{0,8},{1,9},{2,10},{3,11},{4,12},{5,13},{6,14},{7,15},{8,24},{9,25... | collective-permute-start | bytes 798728 | tf_op jit(solution)/shard_map/ppermute | solution.py:343
  15.6 11.2 %collective-permute-start.10 = (bf16[1040,128]{1,0:T(8,128)(2,1)S(1)}, bf16[1040,128]{1,0:T(8,128)(2,1)S(1)}, u32[]{:S(2)}, u32[]{:S(2)}) collective-permute-start(bf16[1040,128]{1,0:T(8,128)(2,1)S(1)} %collective-permute-done), channel_id=1, source_target_pairs={{0,1},{1,0},{2,3},{3,2},{4,6},{5,7},{6,4},{7,5},{8,9},{9,8},{10,11... | collective-permute-start | bytes 798728 | tf_op jit(solution)/shard_map/ppermute | solution.py:343
  17.2 9.9 %collective-permute-start.12 = (bf16[2080,128]{1,0:T(8,128)(2,1)S(1)}, bf16[2080,128]{1,0:T(8,128)(2,1)S(1)}, u32[]{:S(2)}, u32[]{:S(2)}) collective-permute-start(bf16[2080,128]{1,0:T(8,128)(2,1)S(1)} %collective-permute-done.9.refs_0_), channel_id=1, source_target_pairs={{0,4},{1,5},{2,6},{3,7},{4,0},{5,1},{6,2},{7,3},{8,12},{9,13},{10,... | collective-permute-start | bytes 1597448 | tf_op jit(solution)/shard_map/ppermute | solution.py:343
  21.5 7.9 %collective-permute-start.7 = (bf16[1040,128]{1,0:T(8,128)(2,1)S(1)}, bf16[1040,128]{1,0:T(8,128)(2,1)S(1)}, u32[]{:S(2)}, u32[]{:S(2)}) collective-permute-start(bf16[1040,128]{1,0:T(8,128)(2,1)S(1)} %collective-permute-done.1), channel_id=1, source_target_pairs={{0,1},{1,0},{2,3},{3,2},{4,6},{5,7},{6,4},{7,5},{8,9},{9,8},{10,11... | collective-permute-start | bytes 798728 | tf_op jit(solution)/shard_map/ppermute | solution.py:343
  22.0 15.0 %collective-permute-start.2 = (bf16[1040,128]{1,0:T(8,128)(2,1)S(1)}, bf16[1040,128]{1,0:T(8,128)(2,1)S(1)}, u32[]{:S(2)}, u32[]{:S(2)}) collective-permute-start(bf16[1040,128]{1,0:T(8,128)(2,1)S(1)} %collective-permute-done.1), channel_id=1, source_target_pairs={{0,8},{1,9},{2,10},{3,11},{4,12},{5,13},{6,14},{7,15},{8,24},{9,25... | collective-permute-start | bytes 798728 | tf_op jit(solution)/shard_map/ppermute | solution.py:343
  26.9 8.5 %collective-permute-start.14 = (bf16[2080,128]{1,0:T(8,128)(2,1)S(1)}, bf16[2080,128]{1,0:T(8,128)(2,1)S(1)}, u32[]{:S(2)}, u32[]{:S(2)}) collective-permute-start(bf16[2080,128]{1,0:T(8,128)(2,1)S(1)} %constant_dynamic-update-slice_fusion.3.refs_1_), channel_id=1, source_target_pairs={{0,2},{1,3},{2,0},{3,1},{4,5},{5,4},{6,7},{7,6},{8,10},{9,11},{10,... | collective-permute-start | bytes 1597448 | tf_op jit(solution)/shard_map/ppermute | solution.py:343
  29.4 12.4 %collective-permute-start.13 = (bf16[2080,128]{1,0:T(8,128)(2,1)S(1)}, bf16[2080,128]{1,0:T(8,128)(2,1)S(1)}, u32[]{:S(2)}, u32[]{:S(2)}) collective-permute-start(bf16[2080,128]{1,0:T(8,128)(2,1)S(1)} %constant_dynamic-update-slice_fusion.5.refs_2_), channel_id=1, source_target_pairs={{0,2},{1,3},{2,0},{3,1},{4,5},{5,4},{6,7},{7,6},{8,10},{9,11},{10,... | collective-permute-start | bytes 1597448 | tf_op jit(solution)/shard_map/ppermute | solution.py:343
  35.4 6.5 %collective-permute-start.15 = (bf16[4160,128]{1,0:T(8,128)(2,1)S(1)}, bf16[4160,128]{1,0:T(8,128)(2,1)S(1)}, u32[]{:S(2)}, u32[]{:S(2)}) collective-permute-start(bf16[4160,128]{1,0:T(8,128)(2,1)S(1)} %pad_maximum_fusion.1), channel_id=1, source_target_pairs={{0,4},{1,5},{2,6},{3,7},{4,0},{5,1},{6,2},{7,3},{8,12},{9,13},{10,... | collective-permute-start | bytes 3194888 | tf_op jit(solution)/shard_map/ppermute | solution.py:343
  37.0 10.1 %collective-permute-start.3 = (bf16[1040,128]{1,0:T(8,128)(2,1)S(1)}, bf16[1040,128]{1,0:T(8,128)(2,1)S(1)}, u32[]{:S(2)}, u32[]{:S(2)}) collective-permute-start(bf16[1040,128]{1,0:T(8,128)(2,1)S(1)} %collective-permute-done.2), channel_id=1, source_target_pairs={{0,1},{1,0},{2,3},{3,2},{4,6},{5,7},{6,4},{7,5},{8,9},{9,8},{10,11... | collective-permute-start | bytes 798728 | tf_op jit(solution)/shard_map/ppermute | solution.py:343
  37.2 9.9 %collective-permute-start.5 = (bf16[1040,128]{1,0:T(8,128)(2,1)S(1)}, bf16[1040,128]{1,0:T(8,128)(2,1)S(1)}, u32[]{:S(2)}, u32[]{:S(2)}) collective-permute-start(bf16[1040,128]{1,0:T(8,128)(2,1)S(1)} %collective-permute-done.2), channel_id=1, source_target_pairs={{0,2},{1,3},{2,0},{3,1},{4,5},{5,4},{6,7},{7,6},{8,10},{9,11},{10,... | collective-permute-start | bytes 798728 | tf_op jit(solution)/shard_map/ppermute | solution.py:343
  44.4 5.0 %collective-permute-start.16 = (bf16[4160,128]{1,0:T(8,128)(2,1)S(1)}, bf16[4160,128]{1,0:T(8,128)(2,1)S(1)}, u32[]{:S(2)}, u32[]{:S(2)}) collective-permute-start(bf16[4160,128]{1,0:T(8,128)(2,1)S(1)} %pad_maximum_fusion), channel_id=1, source_target_pairs={{0,4},{1,5},{2,6},{3,7},{4,0},{5,1},{6,2},{7,3},{8,12},{9,13},{10,... | collective-permute-start | bytes 3194888 | tf_op jit(solution)/shard_map/ppermute | solution.py:343
  47.2 5.7 %collective-permute-start.6 = (bf16[3120,128]{1,0:T(8,128)(2,1)S(1)}, bf16[3120,128]{1,0:T(8,128)(2,1)S(1)}, u32[]{:S(2)}, u32[]{:S(2)}) collective-permute-start(bf16[3120,128]{1,0:T(8,128)(2,1)S(1)} %constant_dynamic-update-slice_fusion.refs_0_), channel_id=1, source_target_pairs={{0,4},{1,5},{2,6},{3,7},{4,0},{5,1},{6,2},{7,3},{8,12},{9,13},{10,... | collective-permute-start | bytes 2396168 | tf_op jit(solution)/shard_map/ppermute | solution.py:343
  48.4 6.2 %collective-permute-start.4 = (bf16[1040,128]{1,0:T(8,128)(2,1)S(1)}, bf16[1040,128]{1,0:T(8,128)(2,1)S(1)}, u32[]{:S(2)}, u32[]{:S(2)}) collective-permute-start(bf16[1040,128]{1,0:T(8,128)(2,1)S(1)} %collective-permute-done.3), channel_id=1, source_target_pairs={{0,2},{1,3},{2,0},{3,1},{4,5},{5,4},{6,7},{7,6},{8,10},{9,11},{10,... | collective-permute-start | bytes 798728 | tf_op jit(solution)/shard_map/ppermute | solution.py:343
  54.6 4.4 %collective-permute-start.17 = (bf16[1040,128]{1,0:T(8,128)(2,1)S(1)}, bf16[1040,128]{1,0:T(8,128)(2,1)S(1)}, u32[]{:S(2)}, u32[]{:S(2)}) collective-permute-start(bf16[1040,128]{1,0:T(8,128)(2,1)S(1)} %collective-permute-done.4.refs_0_), channel_id=1, source_target_pairs={{0,4},{1,5},{2,6},{3,7},{4,0},{5,1},{6,2},{7,3},{8,12},{9,13},{10,... | collective-permute-start | bytes 798728 | tf_op jit(solution)/shard_map/ppermute | solution.py:343

commit v2 on v1

--- a/solution.py
+++ b/solution.py
@@ -345,9 +345,10 @@
     def along_z(x):
         return permute(x, lambda z, core, place: (after[z], core, place))
 
-    def over_place(x, step):
+    def over_place(x, step, cross=0):
         def to(z, core, place):
-            return z, core, place ^ (1 << (bits - 1 - step if core else step))
+            bit = bits - 1 - step if core else step
+            return z, core ^ cross, place ^ (1 << bit)
 
         return permute(x, to)
 
@@ -418,15 +419,14 @@
     for step in range(bits):
         found += [over_place(x, step) for x in found]
     *most, final = found
+    crossed = over_place(found[inner // 2 - 1], bits - 1, cross=1)
     most = jnp.concatenate(most)
     their_most = other_core(most)
     state = attention.add(state, [halves[-1][1], theirs[-1][-1]])
     state = attention.add(state, [most, their_most])
-    final = tied(final, state[0])
-    theirs = other_core(final)
-    state = attention.add(state, [final], keep=1)
+    last = [tied(x, state[0]) for x in (final, crossed)]
     out = jax.ShapeDtypeStruct(queries.shape, queries.dtype)
-    return attention.add(state, [theirs], keep=1, out=out)
+    return attention.add(state, last, keep=1, out=out)
 
 
 def solution(mesh):

time: 62.7 us -> 63.3 us (level)
  the two profiles are of different devices: /device:TPU:9 before, /device:TPU:1 now
where the time goes in v2:
time: 63.3 us; the launch traced here: 63.9 us
  starting transfers between devices  28.1 us (44%)
  waiting for transfers between devices  18.7 us (30%)
  Pallas kernels  15 us (24%)
  local copies, waits for them, and re-layouts  1.62 us (3%)
    ppermute x18, starting transfers between devices, permute(): return lax.ppermute(x, AXES, pairs)  28.1 us
    ppermute x18, waiting for transfers between devices, permute(): return lax.ppermute(x, AXES, pairs)  18.7 us
    pallas_call x7, Pallas kernels, call(): pl.pallas_call(kernel, out_shape=shapes, in_specs=[vmem] * len(operands),...  12.9 us
    pallas_call x1, Pallas kernels, per_device(): pl.pallas_call(pack_kernel, out_shape=jax.ShapeDtypeStruct((2 * tokens *...  2.08 us
    reshape x1, local copies, waits for them, and re-layouts, per_device(): queries.reshape(2, RUN, heads_kv, group, head_dim).transpose(0, 2, 1, 3, 4)  1.41 us
  transfers between devices with their start and end apart: 18, of which 8 were waited for; matrix products, arithmetic and copies ran while one was open for 3% of the time, Pallas kernels for 15%

profile of v2, /device:TPU:1, one launch (start us, length us, event | category | flops | bytes accessed | tf_op | source)
XLA Modules:
  0.0 63.9 jit_solution(3407296955615019646)
XLA Ops:
  0.0 2.1 %pack.1.own_ref = bf16[1040,128]{1,0:T(8,128)(2,1)} custom-call(bf16[512,128]{1,0:T(8,128)(2,1)} %bitcast.17, bf16[512,128]{1,0:T(8,128)(2,1)} %bitcast.18, s32[1,128]{1,0:T(1,128)} %bitcast.19), custom_call_target="tpu_custom_call" | custom-call | tf_op jit(solution)/shard_map/pack/pallas_call | solution.py:362
  2.1 0.0 copy-start
  2.1 2.1 %collective-permute-start.8 = (bf16[1040,128]{1,0:T(8,128)(2,1)}, bf16[1040,128]{1,0:T(8,128)(2,1)S(1)}, u32[]{:S(2)}, u32[]{:S(2)}) collective-permute-start(bf16[1040,128]{1,0:T(8,128)(2,1)} %pack.1.own_ref), channel_id=1, source_target_pairs={{0,1},{1,0},{2,3},{3,2},{4,6},{5,7},{6,4},{7,5},{8,9},{9,8},{10,11... | collective-permute-start | bytes 798728 | tf_op jit(solution)/shard_map/ppermute | solution.py:343
  4.2 1.3 %collective-permute-start = (bf16[1040,128]{1,0:T(8,128)(2,1)}, bf16[1040,128]{1,0:T(8,128)(2,1)S(1)}, u32[]{:S(2)}, u32[]{:S(2)}) collective-permute-start(bf16[1040,128]{1,0:T(8,128)(2,1)} %pack.1.own_ref), channel_id=1, source_target_pairs={{0,8},{1,9},{2,10},{3,11},{4,12},{5,13},{6,14},{7,15},{8,24},{9,25... | collective-permute-start | bytes 798728 | tf_op jit(solution)/shard_map/ppermute | solution.py:343
  5.5 1.4 %copy.31 = bf16[2,64,4,8,128]{4,3,1,2,0:T(8,128)(2,1)S(1)} copy(bf16[2,64,4,8,128]{4,3,2,1,0:T(8,128)(2,1)} %bitcast.16) | data formatting | bytes 2097152 | tf_op jit(solution)/shard_map/reshape | solution.py:379
  7.0 1.5 %attend_own.1 = (f32[8,128]{1,0:T(8,128)S(1)}, f32[2,4,512,128]{3,2,1,0:T(8,128)S(1)}, f32[2,4,512,256]{3,2,1,0:T(8,128)S(1)}, bf16[2,24,512,128]{3,2,1,0:T(8,128)(2,1)S(1)}) custom-call(bf16[2,4,512,128]{3,2,1,0:T(8,128)(2,1)S(1)} %bitcast.9, bf16[1040,128]{1,0:T(8,128)(2,1)S(1)} %copy-done), custom_call_target="tpu_custom_call" | custom-call | flops 268435456 | bytes 4194304 | tf_op jit(solution)/shard_map/attend_own/pallas_call | solution.py:285
  8.4 0.1 collective-permute-done.8
  8.6 1.5 %collective-permute-start.9 = (bf16[2080,128]{1,0:T(8,128)(2,1)S(1)}, bf16[2080,128]{1,0:T(8,128)(2,1)S(1)}, u32[]{:S(2)}, u32[]{:S(2)}) collective-permute-start(bf16[2080,128]{1,0:T(8,128)(2,1)S(1)} %pad_maximum_fusion.2.refs_0_), channel_id=1, source_target_pairs={{0,2},{1,3},{2,0},{3,1},{4,5},{5,4},{6,7},{7,6},{8,10},{9,11},{10,... | collective-permute-start | bytes 1597448 | tf_op jit(solution)/shard_map/ppermute | solution.py:343
  10.1 2.3 %collective-permute-done = bf16[1040,128]{1,0:T(8,128)(2,1)S(1)} collective-permute-done((bf16[1040,128]{1,0:T(8,128)(2,1)}, bf16[1040,128]{1,0:T(8,128)(2,1)S(1)}, u32[]{:S(2)}, u32[]{:S(2)}) %collective-permute-start) | collective-permute-done | bytes 266272 | tf_op jit(solution)/shard_map/ppermute | solution.py:343
  12.4 1.8 %collective-permute-start.11 = (bf16[2080,128]{1,0:T(8,128)(2,1)S(1)}, bf16[2080,128]{1,0:T(8,128)(2,1)S(1)}, u32[]{:S(2)}, u32[]{:S(2)}) collective-permute-start(bf16[2080,128]{1,0:T(8,128)(2,1)S(1)} %pad_maximum_fusion.2.refs_0_), channel_id=1, source_target_pairs={{0,4},{1,5},{2,6},{3,7},{4,0},{5,1},{6,2},{7,3},{8,12},{9,13},{10,... | collective-permute-start | bytes 1597448 | tf_op jit(solution)/shard_map/ppermute | solution.py:343
  14.2 0.6 collective-permute-start.1
  14.8 0.2 collective-permute-start.10
  15.0 2.1 %collective-permute-done.9.refs_0_ = bf16[2080,128]{1,0:T(8,128)(2,1)S(1)} collective-permute-done((bf16[2080,128]{1,0:T(8,128)(2,1)S(1)}, bf16[2080,128]{1,0:T(8,128)(2,1)S(1)}, u32[]{:S(2)}, u32[]{:S(2)}) %collective-permute-start.9) | collective-permute-done | bytes 532512 | tf_op jit(solution)/shard_map/ppermute | solution.py:343
  17.1 4.4 %collective-permute-start.12 = (bf16[2080,128]{1,0:T(8,128)(2,1)S(1)}, bf16[2080,128]{1,0:T(8,128)(2,1)S(1)}, u32[]{:S(2)}, u32[]{:S(2)}) collective-permute-start(bf16[2080,128]{1,0:T(8,128)(2,1)S(1)} %collective-permute-done.9.refs_0_), channel_id=1, source_target_pairs={{0,4},{1,5},{2,6},{3,7},{4,0},{5,1},{6,2},{7,3},{8,12},{9,13},{10,... | collective-permute-start | bytes 1597448 | tf_op jit(solution)/shard_map/ppermute | solution.py:343
  21.5 1.6 %collective-permute-done.1 = bf16[1040,128]{1,0:T(8,128)(2,1)S(1)} collective-permute-done((bf16[1040,128]{1,0:T(8,128)(2,1)S(1)}, bf16[1040,128]{1,0:T(8,128)(2,1)S(1)}, u32[]{:S(2)}, u32[]{:S(2)}) %collective-permute-start.1) | collective-permute-done | bytes 266272 | tf_op jit(solution)/shard_map/ppermute | solution.py:343
  23.1 0.7 %collective-permute-start.7 = (bf16[1040,128]{1,0:T(8,128)(2,1)S(1)}, bf16[1040,128]{1,0:T(8,128)(2,1)S(1)}, u32[]{:S(2)}, u32[]{:S(2)}) collective-permute-start(bf16[1040,128]{1,0:T(8,128)(2,1)S(1)} %collective-permute-done.1), channel_id=1, source_target_pairs={{0,1},{1,0},{2,3},{3,2},{4,6},{5,7},{6,4},{7,5},{8,9},{9,8},{10,11... | collective-permute-start | bytes 798728 | tf_op jit(solution)/shard_map/ppermute | solution.py:343
  23.7 0.4 collective-permute-start.2
  24.1 0.0 collective-permute-done.11.refs_1_
  24.1 0.4 attend.6
  24.5 0.0 collective-permute-done.10
  24.5 2.1 %collective-permute-start.14 = (bf16[2080,128]{1,0:T(8,128)(2,1)S(1)}, bf16[2080,128]{1,0:T(8,128)(2,1)S(1)}, u32[]{:S(2)}, u32[]{:S(2)}) collective-permute-start(bf16[2080,128]{1,0:T(8,128)(2,1)S(1)} %constant_dynamic-update-slice_fusion.3.refs_1_), channel_id=1, source_target_pairs={{0,2},{1,3},{2,0},{3,1},{4,5},{5,4},{6,7},{7,6},{8,10},{9,11},{10,... | collective-permute-start | bytes 1597448 | tf_op jit(solution)/shard_map/ppermute | solution.py:343
  26.6 0.0 collective-permute-done.12.refs_2_
  26.6 2.2 %attend.7 = (f32[8,128]{1,0:T(8,128)S(1)}, f32[2,4,512,128]{3,2,1,0:T(8,128)S(1)}, f32[2,4,512,256]{3,2,1,0:T(8,128)S(1)}, bf16[2,24,512,128]{3,2,1,0:T(8,128)(2,1)S(1)}) custom-call(bf16[2,4,512,128]{3,2,1,0:T(8,128)(2,1)S(1)} %bitcast.11, ...), custom_call_target="tpu_custom_call", output_to_operand_aliasing={{0}: (4, {}), {1}: (5, {}), {2}: (6, {}), {3}: (7, {})} | custom-call | flops 805306368 | bytes 4194304 | tf_op jit(solution)/shard_map/attend/pallas_call | solution.py:285
  28.9 0.0 collective-permute-done.7
  28.9 1.0 %collective-permute-start.13 = (bf16[2080,128]{1,0:T(8,128)(2,1)S(1)}, bf16[2080,128]{1,0:T(8,128)(2,1)S(1)}, u32[]{:S(2)}, u32[]{:S(2)}) collective-permute-start(bf16[2080,128]{1,0:T(8,128)(2,1)S(1)} %constant_dynamic-update-slice_fusion.5.refs_2_), channel_id=1, source_target_pairs={{0,2},{1,3},{2,0},{3,1},{4,5},{5,4},{6,7},{7,6},{8,10},{9,11},{10,... | collective-permute-start | bytes 1597448 | tf_op jit(solution)/shard_map/ppermute | solution.py:343
  30.0 5.5 %collective-permute-done.14.refs_0_ = bf16[2080,128]{1,0:T(8,128)(2,1)S(1)} collective-permute-done((bf16[2080,128]{1,0:T(8,128)(2,1)S(1)}, bf16[2080,128]{1,0:T(8,128)(2,1)S(1)}, u32[]{:S(2)}, u32[]{:S(2)}) %collective-permute-start.14) | collective-permute-done | bytes 532512 | tf_op jit(solution)/shard_map/ppermute | solution.py:343
  35.5 0.1 pad_maximum_fusion.1
  35.5 0.5 collective-permute-start.15
  36.0 0.0 collective-permute-done.2
  36.0 0.2 collective-permute-start.3
  36.3 2.5 %collective-permute-start.5 = (bf16[1040,128]{1,0:T(8,128)(2,1)S(1)}, bf16[1040,128]{1,0:T(8,128)(2,1)S(1)}, u32[]{:S(2)}, u32[]{:S(2)}) collective-permute-start(bf16[1040,128]{1,0:T(8,128)(2,1)S(1)} %collective-permute-done.2), channel_id=1, source_target_pairs={{0,2},{1,3},{2,0},{3,1},{4,5},{5,4},{6,7},{7,6},{8,10},{9,11},{10,... | collective-permute-start | bytes 798728 | tf_op jit(solution)/shard_map/ppermute | solution.py:343
  38.7 3.6 %collective-permute-done.13.refs_0_ = bf16[2080,128]{1,0:T(8,128)(2,1)S(1)} collective-permute-done((bf16[2080,128]{1,0:T(8,128)(2,1)S(1)}, bf16[2080,128]{1,0:T(8,128)(2,1)S(1)}, u32[]{:S(2)}, u32[]{:S(2)}) %collective-permute-start.13) | collective-permute-done | bytes 532512 | tf_op jit(solution)/shard_map/ppermute | solution.py:343
  42.3 0.1 pad_maximum_fusion
  42.4 0.0 collective-permute-done.15.refs_1_
  42.4 2.6 %attend.8 = (f32[8,128]{1,0:T(8,128)S(1)}, f32[2,4,512,128]{3,2,1,0:T(8,128)S(1)}, f32[2,4,512,256]{3,2,1,0:T(8,128)S(1)}, bf16[2,24,512,128]{3,2,1,0:T(8,128)(2,1)S(1)}) custom-call(bf16[2,4,512,128]{3,2,1,0:T(8,128)(2,1)S(1)} %bitcast.12, ...), custom_call_target="tpu_custom_call", output_to_operand_aliasing={{0}: (4, {}), {1}: (5, {}), {2}: (6, {}), {3}: (7, {})} | custom-call | flops 1073741824 | bytes 4194304 | tf_op jit(solution)/shard_map/attend/pallas_call | solution.py:285
  45.0 2.0 %collective-permute-start.16 = (bf16[4160,128]{1,0:T(8,128)(2,1)S(1)}, bf16[4160,128]{1,0:T(8,128)(2,1)S(1)}, u32[]{:S(2)}, u32[]{:S(2)}) collective-permute-start(bf16[4160,128]{1,0:T(8,128)(2,1)S(1)} %pad_maximum_fusion), channel_id=1, source_target_pairs={{0,4},{1,5},{2,6},{3,7},{4,0},{5,1},{6,2},{7,3},{8,12},{9,13},{10,... | collective-permute-start | bytes 3194888 | tf_op jit(solution)/shard_map/ppermute | solution.py:343
  47.0 0.0 collective-permute-done.3
  47.1 0.0 collective-permute-done.5
  47.1 0.4 collective-permute-start.6
  47.5 6.4 %collective-permute-start.17 = (bf16[1040,128]{1,0:T(8,128)(2,1)S(1)}, bf16[1040,128]{1,0:T(8,128)(2,1)S(1)}, u32[]{:S(2)}, u32[]{:S(2)}) collective-permute-start(bf16[1040,128]{1,0:T(8,128)(2,1)S(1)} %collective-permute-done.3), channel_id=1, source_target_pairs={{0,6},{1,7},{2,4},{3,5},{4,1},{5,0},{6,3},{7,2},{8,14},{9,15},{10,... | collective-permute-start | bytes 798728 | tf_op jit(solution)/shard_map/ppermute | solution.py:343
  53.9 0.0 collective-permute-start.4
  54.0 0.0 collective-permute-done.16.refs_1_
  54.0 2.3 %attend.9 = (f32[8,128]{1,0:T(8,128)S(1)}, f32[2,4,512,128]{3,2,1,0:T(8,128)S(1)}, f32[2,4,512,256]{3,2,1,0:T(8,128)S(1)}, bf16[2,24,512,128]{3,2,1,0:T(8,128)(2,1)S(1)}) custom-call(bf16[2,4,512,128]{3,2,1,0:T(8,128)(2,1)S(1)} %bitcast.13, ...), custom_call_target="tpu_custom_call", output_to_operand_aliasing={{0}: (3, {}), {1}: (4, {}), {2}: (5, {}), {3}: (6, {})} | custom-call | flops 805306368 | bytes 4194304 | tf_op jit(solution)/shard_map/attend/pallas_call | solution.py:285
  56.3 0.0 collective-permute-done.6.refs_1_
  56.3 0.5 attend.10
  56.8 0.5 collective-permute-done.17.refs_1_
  57.3 3.0 %collective-permute-done.4.refs_0_ = bf16[1040,128]{1,0:T(8,128)(2,1)S(1)} collective-permute-done((bf16[1040,128]{1,0:T(8,128)(2,1)S(1)}, bf16[1040,128]{1,0:T(8,128)(2,1)S(1)}, u32[]{:S(2)}, u32[]{:S(2)}) %collective-permute-start.4) | collective-permute-done | bytes 266272 | tf_op jit(solution)/shard_map/ppermute | solution.py:343
  60.3 3.4 %attend.11 = (bf16[128,32,128]{2,1,0:T(8,128)(2,1)}, f32[8,128]{1,0:T(8,128)S(1)}, f32[2,4,512,128]{3,2,1,0:T(8,128)S(1)}, f32[2,4,512,256]{3,2,1,0:T(8,128)S(1)}, bf16[2,24,512,128]{3,2,1,0:T(8,128)(2,1)S(1)}) custom-call(bf16[2,4,512,128]{3,2,1,0:T(8,128)(2,1)S(1)} %bitcast.15, ...), custom_call_target="tpu_custom_call", output_to_operand_aliasing={{1}: (3, {}), {2}: (4, {}), {3}: (5, {}), {4}: (6, {})} | custom-call | flops 268435456 | bytes 4194304 | tf_op jit(solution)/shard_map/attend/pallas_call | solution.py:285
  (9 shorter events, 0.2 us)
Async XLA Ops:
  2.1 4.9 %copy-start = (bf16[1040,128]{1,0:T(8,128)(2,1)S(1)}, bf16[1040,128]{1,0:T(8,128)(2,1)}, u32[]{:S(2)}) copy-start(bf16[1040,128]{1,0:T(8,128)(2,1)} %pack.1.own_ref) | copy-start | bytes 798724
  2.1 6.4 %collective-permute-start.8 = (bf16[1040,128]{1,0:T(8,128)(2,1)}, bf16[1040,128]{1,0:T(8,128)(2,1)S(1)}, u32[]{:S(2)}, u32[]{:S(2)}) collective-permute-start(bf16[1040,128]{1,0:T(8,128)(2,1)} %pack.1.own_ref), channel_id=1, source_target_pairs={{0,1},{1,0},{2,3},{3,2},{4,6},{5,7},{6,4},{7,5},{8,9},{9,8},{10,11... | collective-permute-start | bytes 798728 | tf_op jit(solution)/shard_map/ppermute | solution.py:343
  4.2 8.1 %collective-permute-start = (bf16[1040,128]{1,0:T(8,128)(2,1)}, bf16[1040,128]{1,0:T(8,128)(2,1)S(1)}, u32[]{:S(2)}, u32[]{:S(2)}) collective-permute-start(bf16[1040,128]{1,0:T(8,128)(2,1)} %pack.1.own_ref), channel_id=1, source_target_pairs={{0,8},{1,9},{2,10},{3,11},{4,12},{5,13},{6,14},{7,15},{8,24},{9,25... | collective-permute-start | bytes 798728 | tf_op jit(solution)/shard_map/ppermute | solution.py:343
  8.6 8.5 %collective-permute-start.9 = (bf16[2080,128]{1,0:T(8,128)(2,1)S(1)}, bf16[2080,128]{1,0:T(8,128)(2,1)S(1)}, u32[]{:S(2)}, u32[]{:S(2)}) collective-permute-start(bf16[2080,128]{1,0:T(8,128)(2,1)S(1)} %pad_maximum_fusion.2.refs_0_), channel_id=1, source_target_pairs={{0,2},{1,3},{2,0},{3,1},{4,5},{5,4},{6,7},{7,6},{8,10},{9,11},{10,... | collective-permute-start | bytes 1597448 | tf_op jit(solution)/shard_map/ppermute | solution.py:343
  12.4 11.8 %collective-permute-start.11 = (bf16[2080,128]{1,0:T(8,128)(2,1)S(1)}, bf16[2080,128]{1,0:T(8,128)(2,1)S(1)}, u32[]{:S(2)}, u32[]{:S(2)}) collective-permute-start(bf16[2080,128]{1,0:T(8,128)(2,1)S(1)} %pad_maximum_fusion.2.refs_0_), channel_id=1, source_target_pairs={{0,4},{1,5},{2,6},{3,7},{4,0},{5,1},{6,2},{7,3},{8,12},{9,13},{10,... | collective-permute-start | bytes 1597448 | tf_op jit(solution)/shard_map/ppermute | solution.py:343
  14.2 8.9 %collective-permute-start.1 = (bf16[1040,128]{1,0:T(8,128)(2,1)S(1)}, bf16[1040,128]{1,0:T(8,128)(2,1)S(1)}, u32[]{:S(2)}, u32[]{:S(2)}) collective-permute-start(bf16[1040,128]{1,0:T(8,128)(2,1)S(1)} %collective-permute-done), channel_id=1, source_target_pairs={{0,8},{1,9},{2,10},{3,11},{4,12},{5,13},{6,14},{7,15},{8,24},{9,25... | collective-permute-start | bytes 798728 | tf_op jit(solution)/shard_map/ppermute | solution.py:343
  14.8 9.7 %collective-permute-start.10 = (bf16[1040,128]{1,0:T(8,128)(2,1)S(1)}, bf16[1040,128]{1,0:T(8,128)(2,1)S(1)}, u32[]{:S(2)}, u32[]{:S(2)}) collective-permute-start(bf16[1040,128]{1,0:T(8,128)(2,1)S(1)} %collective-permute-done), channel_id=1, source_target_pairs={{0,1},{1,0},{2,3},{3,2},{4,6},{5,7},{6,4},{7,5},{8,9},{9,8},{10,11... | collective-permute-start | bytes 798728 | tf_op jit(solution)/shard_map/ppermute | solution.py:343
  17.1 9.6 %collective-permute-start.12 = (bf16[2080,128]{1,0:T(8,128)(2,1)S(1)}, bf16[2080,128]{1,0:T(8,128)(2,1)S(1)}, u32[]{:S(2)}, u32[]{:S(2)}) collective-permute-start(bf16[2080,128]{1,0:T(8,128)(2,1)S(1)} %collective-permute-done.9.refs_0_), channel_id=1, source_target_pairs={{0,4},{1,5},{2,6},{3,7},{4,0},{5,1},{6,2},{7,3},{8,12},{9,13},{10,... | collective-permute-start | bytes 1597448 | tf_op jit(solution)/shard_map/ppermute | solution.py:343
  23.1 5.8 %collective-permute-start.7 = (bf16[1040,128]{1,0:T(8,128)(2,1)S(1)}, bf16[1040,128]{1,0:T(8,128)(2,1)S(1)}, u32[]{:S(2)}, u32[]{:S(2)}) collective-permute-start(bf16[1040,128]{1,0:T(8,128)(2,1)S(1)} %collective-permute-done.1), channel_id=1, source_target_pairs={{0,1},{1,0},{2,3},{3,2},{4,6},{5,7},{6,4},{7,5},{8,9},{9,8},{10,11... | collective-permute-start | bytes 798728 | tf_op jit(solution)/shard_map/ppermute | solution.py:343
  23.7 12.3 %collective-permute-start.2 = (bf16[1040,128]{1,0:T(8,128)(2,1)S(1)}, bf16[1040,128]{1,0:T(8,128)(2,1)S(1)}, u32[]{:S(2)}, u32[]{:S(2)}) collective-permute-start(bf16[1040,128]{1,0:T(8,128)(2,1)S(1)} %collective-permute-done.1), channel_id=1, source_target_pairs={{0,8},{1,9},{2,10},{3,11},{4,12},{5,13},{6,14},{7,15},{8,24},{9,25... | collective-permute-start | bytes 798728 | tf_op jit(solution)/shard_map/ppermute | solution.py:343
  24.5 10.9 %collective-permute-start.14 = (bf16[2080,128]{1,0:T(8,128)(2,1)S(1)}, bf16[2080,128]{1,0:T(8,128)(2,1)S(1)}, u32[]{:S(2)}, u32[]{:S(2)}) collective-permute-start(bf16[2080,128]{1,0:T(8,128)(2,1)S(1)} %constant_dynamic-update-slice_fusion.3.refs_1_), channel_id=1, source_target_pairs={{0,2},{1,3},{2,0},{3,1},{4,5},{5,4},{6,7},{7,6},{8,10},{9,11},{10,... | collective-permute-start | bytes 1597448 | tf_op jit(solution)/shard_map/ppermute | solution.py:343
  28.9 13.4 %collective-permute-start.13 = (bf16[2080,128]{1,0:T(8,128)(2,1)S(1)}, bf16[2080,128]{1,0:T(8,128)(2,1)S(1)}, u32[]{:S(2)}, u32[]{:S(2)}) collective-permute-start(bf16[2080,128]{1,0:T(8,128)(2,1)S(1)} %constant_dynamic-update-slice_fusion.5.refs_2_), channel_id=1, source_target_pairs={{0,2},{1,3},{2,0},{3,1},{4,5},{5,4},{6,7},{7,6},{8,10},{9,11},{10,... | collective-permute-start | bytes 1597448 | tf_op jit(solution)/shard_map/ppermute | solution.py:343
  35.5 6.9 %collective-permute-start.15 = (bf16[4160,128]{1,0:T(8,128)(2,1)S(1)}, bf16[4160,128]{1,0:T(8,128)(2,1)S(1)}, u32[]{:S(2)}, u32[]{:S(2)}) collective-permute-start(bf16[4160,128]{1,0:T(8,128)(2,1)S(1)} %pad_maximum_fusion.1), channel_id=1, source_target_pairs={{0,4},{1,5},{2,6},{3,7},{4,0},{5,1},{6,2},{7,3},{8,12},{9,13},{10,... | collective-permute-start | bytes 3194888 | tf_op jit(solution)/shard_map/ppermute | solution.py:343
  36.0 11.0 %collective-permute-start.3 = (bf16[1040,128]{1,0:T(8,128)(2,1)S(1)}, bf16[1040,128]{1,0:T(8,128)(2,1)S(1)}, u32[]{:S(2)}, u32[]{:S(2)}) collective-permute-start(bf16[1040,128]{1,0:T(8,128)(2,1)S(1)} %collective-permute-done.2), channel_id=1, source_target_pairs={{0,1},{1,0},{2,3},{3,2},{4,6},{5,7},{6,4},{7,5},{8,9},{9,8},{10,11... | collective-permute-start | bytes 798728 | tf_op jit(solution)/shard_map/ppermute | solution.py:343
  36.3 10.8 %collective-permute-start.5 = (bf16[1040,128]{1,0:T(8,128)(2,1)S(1)}, bf16[1040,128]{1,0:T(8,128)(2,1)S(1)}, u32[]{:S(2)}, u32[]{:S(2)}) collective-permute-start(bf16[1040,128]{1,0:T(8,128)(2,1)S(1)} %collective-permute-done.2), channel_id=1, source_target_pairs={{0,2},{1,3},{2,0},{3,1},{4,5},{5,4},{6,7},{7,6},{8,10},{9,11},{10,... | collective-permute-start | bytes 798728 | tf_op jit(solution)/shard_map/ppermute | solution.py:343
  45.0 8.9 %collective-permute-start.16 = (bf16[4160,128]{1,0:T(8,128)(2,1)S(1)}, bf16[4160,128]{1,0:T(8,128)(2,1)S(1)}, u32[]{:S(2)}, u32[]{:S(2)}) collective-permute-start(bf16[4160,128]{1,0:T(8,128)(2,1)S(1)} %pad_maximum_fusion), channel_id=1, source_target_pairs={{0,4},{1,5},{2,6},{3,7},{4,0},{5,1},{6,2},{7,3},{8,12},{9,13},{10,... | collective-permute-start | bytes 3194888 | tf_op jit(solution)/shard_map/ppermute | solution.py:343
  47.1 9.1 %collective-permute-start.6 = (bf16[3120,128]{1,0:T(8,128)(2,1)S(1)}, bf16[3120,128]{1,0:T(8,128)(2,1)S(1)}, u32[]{:S(2)}, u32[]{:S(2)}) collective-permute-start(bf16[3120,128]{1,0:T(8,128)(2,1)S(1)} %constant_dynamic-update-slice_fusion.refs_0_), channel_id=1, source_target_pairs={{0,4},{1,5},{2,6},{3,7},{4,0},{5,1},{6,2},{7,3},{8,12},{9,13},{10,... | collective-permute-start | bytes 2396168 | tf_op jit(solution)/shard_map/ppermute | solution.py:343
  47.5 9.8 %collective-permute-start.17 = (bf16[1040,128]{1,0:T(8,128)(2,1)S(1)}, bf16[1040,128]{1,0:T(8,128)(2,1)S(1)}, u32[]{:S(2)}, u32[]{:S(2)}) collective-permute-start(bf16[1040,128]{1,0:T(8,128)(2,1)S(1)} %collective-permute-done.3), channel_id=1, source_target_pairs={{0,6},{1,7},{2,4},{3,5},{4,1},{5,0},{6,3},{7,2},{8,14},{9,15},{10,... | collective-permute-start | bytes 798728 | tf_op jit(solution)/shard_map/ppermute | solution.py:343
  53.9 6.3 %collective-permute-start.4 = (bf16[1040,128]{1,0:T(8,128)(2,1)S(1)}, bf16[1040,128]{1,0:T(8,128)(2,1)S(1)}, u32[]{:S(2)}, u32[]{:S(2)}) collective-permute-start(bf16[1040,128]{1,0:T(8,128)(2,1)S(1)} %collective-permute-done.3), channel_id=1, source_target_pairs={{0,2},{1,3},{2,0},{3,1},{4,5},{5,4},{6,7},{7,6},{8,10},{9,11},{10,... | collective-permute-start | bytes 798728 | tf_op jit(solution)/shard_map/ppermute | solution.py:343

commit v3 on v2

--- a/solution.py
+++ b/solution.py
@@ -49,26 +49,34 @@
 
 
 def head_tile(q_ref, state_refs, a, keys, values, factor, live=None):
-    def scores(h):
+    heads_kv, rows = q_ref.shape[1:3]
+    pieces = [
+        (h, slice(start, start + rows // 2))
+        for h in range(heads_kv)
+        for start in (0, rows // 2)
+    ]
+
+    def scores(h, part):
         return lax.dot_general(
-            q_ref[a, h],
+            q_ref[a, h, part],
             keys(h),
             (((1,), (1,)), ((), ())),
             preferred_element_type=jnp.float32,
         )
 
-    heads_kv = q_ref.shape[1]
-    ahead = scores(0)
-    for h in range(heads_kv):
+    ahead = scores(*pieces[0])
+    for n, (h, part) in enumerate(pieces):
         score = ahead
-        if h + 1 < heads_kv:
-            ahead = scores(h + 1)
-        state = (None, None)
+        if n + 1 < len(pieces):
+            ahead = scores(*pieces[n + 1])
+        state, mask = (None, None), live
         if live is None or isinstance(live, int):
-            state = tuple(ref[a, h] for ref in state_refs)
-        state = flash(score, values(h), state, factor, live)
+            state = tuple(ref[a, h, part] for ref in state_refs)
+        else:
+            mask = live[part]
+        state = flash(score, values(h), state, factor, mask)
         for ref, value in zip(state_refs, state):
-            ref[a, h] = value
+            ref[a, h, part] = value
 
 
 def own_kernel(group, factor, half, q_ref, own_ref, meta_ref, *refs):

time: 63.3 us -> 63.3 us (level)
  the two profiles are of different devices: /device:TPU:1 before, /device:TPU:8 now
where the time goes in v3:
time: 63.3 us; the launch traced here: 63 us
  waiting for transfers between devices  21.6 us (34%)
  starting transfers between devices  20.2 us (32%)
  Pallas kernels  19 us (30%)
  local copies, waits for them, and re-layouts  1.62 us (3%)
    ppermute x18, waiting for transfers between devices, permute(): return lax.ppermute(x, AXES, pairs)  21.6 us
    ppermute x18, starting transfers between devices, permute(): return lax.ppermute(x, AXES, pairs)  20.2 us
    pallas_call x7, Pallas kernels, call(): pl.pallas_call(kernel, out_shape=shapes, in_specs=[vmem] * len(operands),...  17 us
    pallas_call x1, Pallas kernels, per_device(): pl.pallas_call(pack_kernel, out_shape=jax.ShapeDtypeStruct((2 * tokens *...  2.08 us
    reshape x1, local copies, waits for them, and re-layouts, per_device(): queries.reshape(2, RUN, heads_kv, group, head_dim).transpose(0, 2, 1, 3, 4)  1.41 us
  transfers between devices with their start and end apart: 18, of which 7 were waited for; matrix products, arithmetic and copies ran while one was open for 3% of the time, Pallas kernels for 20%

profile of v3, /device:TPU:8, one launch (start us, length us, event | category | flops | bytes accessed | tf_op | source)
XLA Modules:
  0.0 63.0 jit_solution(15196366088811357273)
XLA Ops:
  0.0 2.1 %pack.1.own_ref = bf16[1040,128]{1,0:T(8,128)(2,1)} custom-call(bf16[512,128]{1,0:T(8,128)(2,1)} %bitcast.17, bf16[512,128]{1,0:T(8,128)(2,1)} %bitcast.18, s32[1,128]{1,0:T(1,128)} %bitcast.19), custom_call_target="tpu_custom_call" | custom-call | tf_op jit(solution)/shard_map/pack/pallas_call | solution.py:370
  2.1 0.0 copy-start
  2.1 1.6 %collective-permute-start.8 = (bf16[1040,128]{1,0:T(8,128)(2,1)}, bf16[1040,128]{1,0:T(8,128)(2,1)S(1)}, u32[]{:S(2)}, u32[]{:S(2)}) collective-permute-start(bf16[1040,128]{1,0:T(8,128)(2,1)} %pack.1.own_ref), channel_id=1, source_target_pairs={{0,1},{1,0},{2,3},{3,2},{4,6},{5,7},{6,4},{7,5},{8,9},{9,8},{10,11... | collective-permute-start | bytes 798728 | tf_op jit(solution)/shard_map/ppermute | solution.py:351
  3.7 2.6 %collective-permute-start = (bf16[1040,128]{1,0:T(8,128)(2,1)}, bf16[1040,128]{1,0:T(8,128)(2,1)S(1)}, u32[]{:S(2)}, u32[]{:S(2)}) collective-permute-start(bf16[1040,128]{1,0:T(8,128)(2,1)} %pack.1.own_ref), channel_id=1, source_target_pairs={{0,8},{1,9},{2,10},{3,11},{4,12},{5,13},{6,14},{7,15},{8,24},{9,25... | collective-permute-start | bytes 798728 | tf_op jit(solution)/shard_map/ppermute | solution.py:351
  6.2 1.4 %copy.31 = bf16[2,64,4,8,128]{4,3,1,2,0:T(8,128)(2,1)S(1)} copy(bf16[2,64,4,8,128]{4,3,2,1,0:T(8,128)(2,1)} %bitcast.16) | data formatting | bytes 2097152 | tf_op jit(solution)/shard_map/reshape | solution.py:387
  7.7 2.0 %attend_own.1 = (f32[8,128]{1,0:T(8,128)S(1)}, f32[2,4,512,128]{3,2,1,0:T(8,128)S(1)}, f32[2,4,512,256]{3,2,1,0:T(8,128)S(1)}, bf16[2,24,512,128]{3,2,1,0:T(8,128)(2,1)S(1)}) custom-call(bf16[2,4,512,128]{3,2,1,0:T(8,128)(2,1)S(1)} %bitcast.9, bf16[1040,128]{1,0:T(8,128)(2,1)S(1)} %copy-done), custom_call_target="tpu_custom_call" | custom-call | flops 268435456 | bytes 4194304 | tf_op jit(solution)/shard_map/attend_own/pallas_call | solution.py:293
  9.7 0.0 collective-permute-done.8
  9.7 1.6 %collective-permute-start.9 = (bf16[2080,128]{1,0:T(8,128)(2,1)S(1)}, bf16[2080,128]{1,0:T(8,128)(2,1)S(1)}, u32[]{:S(2)}, u32[]{:S(2)}) collective-permute-start(bf16[2080,128]{1,0:T(8,128)(2,1)S(1)} %pad_maximum_fusion.2.refs_0_), channel_id=1, source_target_pairs={{0,2},{1,3},{2,0},{3,1},{4,5},{5,4},{6,7},{7,6},{8,10},{9,11},{10,... | collective-permute-start | bytes 1597448 | tf_op jit(solution)/shard_map/ppermute | solution.py:351
  11.3 0.7 %collective-permute-done = bf16[1040,128]{1,0:T(8,128)(2,1)S(1)} collective-permute-done((bf16[1040,128]{1,0:T(8,128)(2,1)}, bf16[1040,128]{1,0:T(8,128)(2,1)S(1)}, u32[]{:S(2)}, u32[]{:S(2)}) %collective-permute-start) | collective-permute-done | bytes 266272 | tf_op jit(solution)/shard_map/ppermute | solution.py:351
  12.0 0.0 collective-permute-start.11
  12.0 3.3 %collective-permute-start.1 = (bf16[1040,128]{1,0:T(8,128)(2,1)S(1)}, bf16[1040,128]{1,0:T(8,128)(2,1)S(1)}, u32[]{:S(2)}, u32[]{:S(2)}) collective-permute-start(bf16[1040,128]{1,0:T(8,128)(2,1)S(1)} %collective-permute-done), channel_id=1, source_target_pairs={{0,8},{1,9},{2,10},{3,11},{4,12},{5,13},{6,14},{7,15},{8,24},{9,25... | collective-permute-start | bytes 798728 | tf_op jit(solution)/shard_map/ppermute | solution.py:351
  15.2 1.5 %collective-permute-start.10 = (bf16[1040,128]{1,0:T(8,128)(2,1)S(1)}, bf16[1040,128]{1,0:T(8,128)(2,1)S(1)}, u32[]{:S(2)}, u32[]{:S(2)}) collective-permute-start(bf16[1040,128]{1,0:T(8,128)(2,1)S(1)} %collective-permute-done), channel_id=1, source_target_pairs={{0,1},{1,0},{2,3},{3,2},{4,6},{5,7},{6,4},{7,5},{8,9},{9,8},{10,11... | collective-permute-start | bytes 798728 | tf_op jit(solution)/shard_map/ppermute | solution.py:351
  16.7 3.3 %collective-permute-done.9.refs_0_ = bf16[2080,128]{1,0:T(8,128)(2,1)S(1)} collective-permute-done((bf16[2080,128]{1,0:T(8,128)(2,1)S(1)}, bf16[2080,128]{1,0:T(8,128)(2,1)S(1)}, u32[]{:S(2)}, u32[]{:S(2)}) %collective-permute-start.9) | collective-permute-done | bytes 532512 | tf_op jit(solution)/shard_map/ppermute | solution.py:351
  20.0 0.0 collective-permute-start.12
  20.1 1.5 %collective-permute-done.1 = bf16[1040,128]{1,0:T(8,128)(2,1)S(1)} collective-permute-done((bf16[1040,128]{1,0:T(8,128)(2,1)S(1)}, bf16[1040,128]{1,0:T(8,128)(2,1)S(1)}, u32[]{:S(2)}, u32[]{:S(2)}) %collective-permute-start.1) | collective-permute-done | bytes 266272 | tf_op jit(solution)/shard_map/ppermute | solution.py:351
  21.6 1.5 %collective-permute-start.7 = (bf16[1040,128]{1,0:T(8,128)(2,1)S(1)}, bf16[1040,128]{1,0:T(8,128)(2,1)S(1)}, u32[]{:S(2)}, u32[]{:S(2)}) collective-permute-start(bf16[1040,128]{1,0:T(8,128)(2,1)S(1)} %collective-permute-done.1), channel_id=1, source_target_pairs={{0,1},{1,0},{2,3},{3,2},{4,6},{5,7},{6,4},{7,5},{8,9},{9,8},{10,11... | collective-permute-start | bytes 798728 | tf_op jit(solution)/shard_map/ppermute | solution.py:351
  23.1 3.4 %collective-permute-start.2 = (bf16[1040,128]{1,0:T(8,128)(2,1)S(1)}, bf16[1040,128]{1,0:T(8,128)(2,1)S(1)}, u32[]{:S(2)}, u32[]{:S(2)}) collective-permute-start(bf16[1040,128]{1,0:T(8,128)(2,1)S(1)} %collective-permute-done.1), channel_id=1, source_target_pairs={{0,8},{1,9},{2,10},{3,11},{4,12},{5,13},{6,14},{7,15},{8,24},{9,25... | collective-permute-start | bytes 798728 | tf_op jit(solution)/shard_map/ppermute | solution.py:351
  26.4 0.0 collective-permute-done.11.refs_1_
  26.4 1.5 %attend.6 = (f32[8,128]{1,0:T(8,128)S(1)}, f32[2,4,512,128]{3,2,1,0:T(8,128)S(1)}, f32[2,4,512,256]{3,2,1,0:T(8,128)S(1)}, bf16[2,24,512,128]{3,2,1,0:T(8,128)(2,1)S(1)}) custom-call(bf16[2,4,512,128]{3,2,1,0:T(8,128)(2,1)S(1)} %bitcast.10, ...), custom_call_target="tpu_custom_call", output_to_operand_aliasing={{0}: (3, {}), {1}: (4, {}), {2}: (5, {}), {3}: (6, {})} | custom-call | flops 402653184 | bytes 4194304 | tf_op jit(solution)/shard_map/attend/pallas_call | solution.py:293
  27.9 0.0 collective-permute-done.10
  28.0 0.1 collective-permute-start.14
  28.1 0.0 collective-permute-done.12.refs_2_
  28.1 1.6 %attend.7 = (f32[8,128]{1,0:T(8,128)S(1)}, f32[2,4,512,128]{3,2,1,0:T(8,128)S(1)}, f32[2,4,512,256]{3,2,1,0:T(8,128)S(1)}, bf16[2,24,512,128]{3,2,1,0:T(8,128)(2,1)S(1)}) custom-call(bf16[2,4,512,128]{3,2,1,0:T(8,128)(2,1)S(1)} %bitcast.11, ...), custom_call_target="tpu_custom_call", output_to_operand_aliasing={{0}: (4, {}), {1}: (5, {}), {2}: (6, {}), {3}: (7, {})} | custom-call | flops 805306368 | bytes 4194304 | tf_op jit(solution)/shard_map/attend/pallas_call | solution.py:293
  29.7 0.0 collective-permute-done.7
  29.8 2.1 %collective-permute-start.13 = (bf16[2080,128]{1,0:T(8,128)(2,1)S(1)}, bf16[2080,128]{1,0:T(8,128)(2,1)S(1)}, u32[]{:S(2)}, u32[]{:S(2)}) collective-permute-start(bf16[2080,128]{1,0:T(8,128)(2,1)S(1)} %constant_dynamic-update-slice_fusion.5.refs_2_), channel_id=1, source_target_pairs={{0,2},{1,3},{2,0},{3,1},{4,5},{5,4},{6,7},{7,6},{8,10},{9,11},{10,... | collective-permute-start | bytes 1597448 | tf_op jit(solution)/shard_map/ppermute | solution.py:351
  31.8 5.5 %collective-permute-done.14.refs_0_ = bf16[2080,128]{1,0:T(8,128)(2,1)S(1)} collective-permute-done((bf16[2080,128]{1,0:T(8,128)(2,1)S(1)}, bf16[2080,128]{1,0:T(8,128)(2,1)S(1)}, u32[]{:S(2)}, u32[]{:S(2)}) %collective-permute-start.14) | collective-permute-done | bytes 532512 | tf_op jit(solution)/shard_map/ppermute | solution.py:351
  37.3 0.1 pad_maximum_fusion.1
  37.4 0.1 collective-permute-start.15
  37.5 0.0 collective-permute-done.2
  37.5 0.1 collective-permute-start.3
  37.5 0.3 collective-permute-start.5
  37.8 7.6 %collective-permute-done.13.refs_0_ = bf16[2080,128]{1,0:T(8,128)(2,1)S(1)} collective-permute-done((bf16[2080,128]{1,0:T(8,128)(2,1)S(1)}, bf16[2080,128]{1,0:T(8,128)(2,1)S(1)}, u32[]{:S(2)}, u32[]{:S(2)}) %collective-permute-start.13) | collective-permute-done | bytes 532512 | tf_op jit(solution)/shard_map/ppermute | solution.py:351
  45.4 0.1 pad_maximum_fusion
  45.5 0.0 collective-permute-done.15.refs_1_
  45.5 2.6 %attend.8 = (f32[8,128]{1,0:T(8,128)S(1)}, f32[2,4,512,128]{3,2,1,0:T(8,128)S(1)}, f32[2,4,512,256]{3,2,1,0:T(8,128)S(1)}, bf16[2,24,512,128]{3,2,1,0:T(8,128)(2,1)S(1)}) custom-call(bf16[2,4,512,128]{3,2,1,0:T(8,128)(2,1)S(1)} %bitcast.12, ...), custom_call_target="tpu_custom_call", output_to_operand_aliasing={{0}: (4, {}), {1}: (5, {}), {2}: (6, {}), {3}: (7, {})} | custom-call | flops 1073741824 | bytes 4194304 | tf_op jit(solution)/shard_map/attend/pallas_call | solution.py:293
  48.1 0.1 collective-permute-start.16
  48.2 0.0 collective-permute-done.3
  48.2 0.5 collective-permute-done.5
  48.7 0.1 collective-permute-start.6
  48.8 0.1 collective-permute-start.17
  48.9 2.0 %collective-permute-start.4 = (bf16[1040,128]{1,0:T(8,128)(2,1)S(1)}, bf16[1040,128]{1,0:T(8,128)(2,1)S(1)}, u32[]{:S(2)}, u32[]{:S(2)}) collective-permute-start(bf16[1040,128]{1,0:T(8,128)(2,1)S(1)} %collective-permute-done.3), channel_id=1, source_target_pairs={{0,2},{1,3},{2,0},{3,1},{4,5},{5,4},{6,7},{7,6},{8,10},{9,11},{10,... | collective-permute-start | bytes 798728 | tf_op jit(solution)/shard_map/ppermute | solution.py:351
  51.0 0.0 collective-permute-done.16.refs_1_
  51.0 1.7 %attend.9 = (f32[8,128]{1,0:T(8,128)S(1)}, f32[2,4,512,128]{3,2,1,0:T(8,128)S(1)}, f32[2,4,512,256]{3,2,1,0:T(8,128)S(1)}, bf16[2,24,512,128]{3,2,1,0:T(8,128)(2,1)S(1)}) custom-call(bf16[2,4,512,128]{3,2,1,0:T(8,128)(2,1)S(1)} %bitcast.13, ...), custom_call_target="tpu_custom_call", output_to_operand_aliasing={{0}: (3, {}), {1}: (4, {}), {2}: (5, {}), {3}: (6, {})} | custom-call | flops 805306368 | bytes 4194304 | tf_op jit(solution)/shard_map/attend/pallas_call | solution.py:293
  52.7 0.0 collective-permute-done.6.refs_1_
  52.7 2.9 %attend.10 = (f32[8,128]{1,0:T(8,128)S(1)}, f32[2,4,512,128]{3,2,1,0:T(8,128)S(1)}, f32[2,4,512,256]{3,2,1,0:T(8,128)S(1)}, bf16[2,24,512,128]{3,2,1,0:T(8,128)(2,1)S(1)}) custom-call(bf16[2,4,512,128]{3,2,1,0:T(8,128)(2,1)S(1)} %bitcast.14, ...), custom_call_target="tpu_custom_call", output_to_operand_aliasing={{0}: (3, {}), {1}: (4, {}), {2}: (5, {}), {3}: (6, {})} | custom-call | flops 805306368 | bytes 4194304 | tf_op jit(solution)/shard_map/attend/pallas_call | solution.py:293
  55.6 0.0 collective-permute-done.17.refs_1_
  55.6 2.6 %collective-permute-done.4.refs_0_ = bf16[1040,128]{1,0:T(8,128)(2,1)S(1)} collective-permute-done((bf16[1040,128]{1,0:T(8,128)(2,1)S(1)}, bf16[1040,128]{1,0:T(8,128)(2,1)S(1)}, u32[]{:S(2)}, u32[]{:S(2)}) %collective-permute-start.4) | collective-permute-done | bytes 266272 | tf_op jit(solution)/shard_map/ppermute | solution.py:351
  58.2 4.7 %attend.11 = (bf16[128,32,128]{2,1,0:T(8,128)(2,1)}, f32[8,128]{1,0:T(8,128)S(1)}, f32[2,4,512,128]{3,2,1,0:T(8,128)S(1)}, f32[2,4,512,256]{3,2,1,0:T(8,128)S(1)}, bf16[2,24,512,128]{3,2,1,0:T(8,128)(2,1)S(1)}) custom-call(bf16[2,4,512,128]{3,2,1,0:T(8,128)(2,1)S(1)} %bitcast.15, ...), custom_call_target="tpu_custom_call", output_to_operand_aliasing={{1}: (3, {}), {2}: (4, {}), {3}: (5, {}), {4}: (6, {})} | custom-call | flops 268435456 | bytes 4194304 | tf_op jit(solution)/shard_map/attend/pallas_call | solution.py:293
  (9 shorter events, 0.2 us)
Async XLA Ops:
  2.1 5.6 %copy-start = (bf16[1040,128]{1,0:T(8,128)(2,1)S(1)}, bf16[1040,128]{1,0:T(8,128)(2,1)}, u32[]{:S(2)}) copy-start(bf16[1040,128]{1,0:T(8,128)(2,1)} %pack.1.own_ref) | copy-start | bytes 798724
  2.1 7.6 %collective-permute-start.8 = (bf16[1040,128]{1,0:T(8,128)(2,1)}, bf16[1040,128]{1,0:T(8,128)(2,1)S(1)}, u32[]{:S(2)}, u32[]{:S(2)}) collective-permute-start(bf16[1040,128]{1,0:T(8,128)(2,1)} %pack.1.own_ref), channel_id=1, source_target_pairs={{0,1},{1,0},{2,3},{3,2},{4,6},{5,7},{6,4},{7,5},{8,9},{9,8},{10,11... | collective-permute-start | bytes 798728 | tf_op jit(solution)/shard_map/ppermute | solution.py:351
  3.7 8.3 %collective-permute-start = (bf16[1040,128]{1,0:T(8,128)(2,1)}, bf16[1040,128]{1,0:T(8,128)(2,1)S(1)}, u32[]{:S(2)}, u32[]{:S(2)}) collective-permute-start(bf16[1040,128]{1,0:T(8,128)(2,1)} %pack.1.own_ref), channel_id=1, source_target_pairs={{0,8},{1,9},{2,10},{3,11},{4,12},{5,13},{6,14},{7,15},{8,24},{9,25... | collective-permute-start | bytes 798728 | tf_op jit(solution)/shard_map/ppermute | solution.py:351
  9.7 10.3 %collective-permute-start.9 = (bf16[2080,128]{1,0:T(8,128)(2,1)S(1)}, bf16[2080,128]{1,0:T(8,128)(2,1)S(1)}, u32[]{:S(2)}, u32[]{:S(2)}) collective-permute-start(bf16[2080,128]{1,0:T(8,128)(2,1)S(1)} %pad_maximum_fusion.2.refs_0_), channel_id=1, source_target_pairs={{0,2},{1,3},{2,0},{3,1},{4,5},{5,4},{6,7},{7,6},{8,10},{9,11},{10,... | collective-permute-start | bytes 1597448 | tf_op jit(solution)/shard_map/ppermute | solution.py:351
  12.0 14.5 %collective-permute-start.11 = (bf16[2080,128]{1,0:T(8,128)(2,1)S(1)}, bf16[2080,128]{1,0:T(8,128)(2,1)S(1)}, u32[]{:S(2)}, u32[]{:S(2)}) collective-permute-start(bf16[2080,128]{1,0:T(8,128)(2,1)S(1)} %pad_maximum_fusion.2.refs_0_), channel_id=1, source_target_pairs={{0,4},{1,5},{2,6},{3,7},{4,0},{5,1},{6,2},{7,3},{8,12},{9,13},{10,... | collective-permute-start | bytes 1597448 | tf_op jit(solution)/shard_map/ppermute | solution.py:351
  12.0 9.6 %collective-permute-start.1 = (bf16[1040,128]{1,0:T(8,128)(2,1)S(1)}, bf16[1040,128]{1,0:T(8,128)(2,1)S(1)}, u32[]{:S(2)}, u32[]{:S(2)}) collective-permute-start(bf16[1040,128]{1,0:T(8,128)(2,1)S(1)} %collective-permute-done), channel_id=1, source_target_pairs={{0,8},{1,9},{2,10},{3,11},{4,12},{5,13},{6,14},{7,15},{8,24},{9,25... | collective-permute-start | bytes 798728 | tf_op jit(solution)/shard_map/ppermute | solution.py:351
  15.2 12.7 %collective-permute-start.10 = (bf16[1040,128]{1,0:T(8,128)(2,1)S(1)}, bf16[1040,128]{1,0:T(8,128)(2,1)S(1)}, u32[]{:S(2)}, u32[]{:S(2)}) collective-permute-start(bf16[1040,128]{1,0:T(8,128)(2,1)S(1)} %collective-permute-done), channel_id=1, source_target_pairs={{0,1},{1,0},{2,3},{3,2},{4,6},{5,7},{6,4},{7,5},{8,9},{9,8},{10,11... | collective-permute-start | bytes 798728 | tf_op jit(solution)/shard_map/ppermute | solution.py:351
  20.0 8.0 %collective-permute-start.12 = (bf16[2080,128]{1,0:T(8,128)(2,1)S(1)}, bf16[2080,128]{1,0:T(8,128)(2,1)S(1)}, u32[]{:S(2)}, u32[]{:S(2)}) collective-permute-start(bf16[2080,128]{1,0:T(8,128)(2,1)S(1)} %collective-permute-done.9.refs_0_), channel_id=1, source_target_pairs={{0,4},{1,5},{2,6},{3,7},{4,0},{5,1},{6,2},{7,3},{8,12},{9,13},{10,... | collective-permute-start | bytes 1597448 | tf_op jit(solution)/shard_map/ppermute | solution.py:351
  21.6 8.2 %collective-permute-start.7 = (bf16[1040,128]{1,0:T(8,128)(2,1)S(1)}, bf16[1040,128]{1,0:T(8,128)(2,1)S(1)}, u32[]{:S(2)}, u32[]{:S(2)}) collective-permute-start(bf16[1040,128]{1,0:T(8,128)(2,1)S(1)} %collective-permute-done.1), channel_id=1, source_target_pairs={{0,1},{1,0},{2,3},{3,2},{4,6},{5,7},{6,4},{7,5},{8,9},{9,8},{10,11... | collective-permute-start | bytes 798728 | tf_op jit(solution)/shard_map/ppermute | solution.py:351
  23.1 14.4 %collective-permute-start.2 = (bf16[1040,128]{1,0:T(8,128)(2,1)S(1)}, bf16[1040,128]{1,0:T(8,128)(2,1)S(1)}, u32[]{:S(2)}, u32[]{:S(2)}) collective-permute-start(bf16[1040,128]{1,0:T(8,128)(2,1)S(1)} %collective-permute-done.1), channel_id=1, source_target_pairs={{0,8},{1,9},{2,10},{3,11},{4,12},{5,13},{6,14},{7,15},{8,24},{9,25... | collective-permute-start | bytes 798728 | tf_op jit(solution)/shard_map/ppermute | solution.py:351
  28.0 9.3 %collective-permute-start.14 = (bf16[2080,128]{1,0:T(8,128)(2,1)S(1)}, bf16[2080,128]{1,0:T(8,128)(2,1)S(1)}, u32[]{:S(2)}, u32[]{:S(2)}) collective-permute-start(bf16[2080,128]{1,0:T(8,128)(2,1)S(1)} %constant_dynamic-update-slice_fusion.3.refs_1_), channel_id=1, source_target_pairs={{0,2},{1,3},{2,0},{3,1},{4,5},{5,4},{6,7},{7,6},{8,10},{9,11},{10,... | collective-permute-start | bytes 1597448 | tf_op jit(solution)/shard_map/ppermute | solution.py:351
  29.8 15.6 %collective-permute-start.13 = (bf16[2080,128]{1,0:T(8,128)(2,1)S(1)}, bf16[2080,128]{1,0:T(8,128)(2,1)S(1)}, u32[]{:S(2)}, u32[]{:S(2)}) collective-permute-start(bf16[2080,128]{1,0:T(8,128)(2,1)S(1)} %constant_dynamic-update-slice_fusion.5.refs_2_), channel_id=1, source_target_pairs={{0,2},{1,3},{2,0},{3,1},{4,5},{5,4},{6,7},{7,6},{8,10},{9,11},{10,... | collective-permute-start | bytes 1597448 | tf_op jit(solution)/shard_map/ppermute | solution.py:351
  37.4 8.1 %collective-permute-start.15 = (bf16[4160,128]{1,0:T(8,128)(2,1)S(1)}, bf16[4160,128]{1,0:T(8,128)(2,1)S(1)}, u32[]{:S(2)}, u32[]{:S(2)}) collective-permute-start(bf16[4160,128]{1,0:T(8,128)(2,1)S(1)} %pad_maximum_fusion.1), channel_id=1, source_target_pairs={{0,4},{1,5},{2,6},{3,7},{4,0},{5,1},{6,2},{7,3},{8,12},{9,13},{10,... | collective-permute-start | bytes 3194888 | tf_op jit(solution)/shard_map/ppermute | solution.py:351
  37.5 10.7 %collective-permute-start.3 = (bf16[1040,128]{1,0:T(8,128)(2,1)S(1)}, bf16[1040,128]{1,0:T(8,128)(2,1)S(1)}, u32[]{:S(2)}, u32[]{:S(2)}) collective-permute-start(bf16[1040,128]{1,0:T(8,128)(2,1)S(1)} %collective-permute-done.2), channel_id=1, source_target_pairs={{0,1},{1,0},{2,3},{3,2},{4,6},{5,7},{6,4},{7,5},{8,9},{9,8},{10,11... | collective-permute-start | bytes 798728 | tf_op jit(solution)/shard_map/ppermute | solution.py:351
  37.5 11.2 %collective-permute-start.5 = (bf16[1040,128]{1,0:T(8,128)(2,1)S(1)}, bf16[1040,128]{1,0:T(8,128)(2,1)S(1)}, u32[]{:S(2)}, u32[]{:S(2)}) collective-permute-start(bf16[1040,128]{1,0:T(8,128)(2,1)S(1)} %collective-permute-done.2), channel_id=1, source_target_pairs={{0,2},{1,3},{2,0},{3,1},{4,5},{5,4},{6,7},{7,6},{8,10},{9,11},{10,... | collective-permute-start | bytes 798728 | tf_op jit(solution)/shard_map/ppermute | solution.py:351
  48.1 2.9 %collective-permute-start.16 = (bf16[4160,128]{1,0:T(8,128)(2,1)S(1)}, bf16[4160,128]{1,0:T(8,128)(2,1)S(1)}, u32[]{:S(2)}, u32[]{:S(2)}) collective-permute-start(bf16[4160,128]{1,0:T(8,128)(2,1)S(1)} %pad_maximum_fusion), channel_id=1, source_target_pairs={{0,4},{1,5},{2,6},{3,7},{4,0},{5,1},{6,2},{7,3},{8,12},{9,13},{10,... | collective-permute-start | bytes 3194888 | tf_op jit(solution)/shard_map/ppermute | solution.py:351
  48.7 3.9 %collective-permute-start.6 = (bf16[3120,128]{1,0:T(8,128)(2,1)S(1)}, bf16[3120,128]{1,0:T(8,128)(2,1)S(1)}, u32[]{:S(2)}, u32[]{:S(2)}) collective-permute-start(bf16[3120,128]{1,0:T(8,128)(2,1)S(1)} %constant_dynamic-update-slice_fusion.refs_0_), channel_id=1, source_target_pairs={{0,4},{1,5},{2,6},{3,7},{4,0},{5,1},{6,2},{7,3},{8,12},{9,13},{10,... | collective-permute-start | bytes 2396168 | tf_op jit(solution)/shard_map/ppermute | solution.py:351
  48.8 6.7 %collective-permute-start.17 = (bf16[1040,128]{1,0:T(8,128)(2,1)S(1)}, bf16[1040,128]{1,0:T(8,128)(2,1)S(1)}, u32[]{:S(2)}, u32[]{:S(2)}) collective-permute-start(bf16[1040,128]{1,0:T(8,128)(2,1)S(1)} %collective-permute-done.3), channel_id=1, source_target_pairs={{0,6},{1,7},{2,4},{3,5},{4,1},{5,0},{6,3},{7,2},{8,14},{9,15},{10,... | collective-permute-start | bytes 798728 | tf_op jit(solution)/shard_map/ppermute | solution.py:351
  48.9 9.3 %collective-permute-start.4 = (bf16[1040,128]{1,0:T(8,128)(2,1)S(1)}, bf16[1040,128]{1,0:T(8,128)(2,1)S(1)}, u32[]{:S(2)}, u32[]{:S(2)}) collective-permute-start(bf16[1040,128]{1,0:T(8,128)(2,1)S(1)} %collective-permute-done.3), channel_id=1, source_target_pairs={{0,2},{1,3},{2,0},{3,1},{4,5},{5,4},{6,7},{7,6},{8,10},{9,11},{10,... | collective-permute-start | bytes 798728 | tf_op jit(solution)/shard_map/ppermute | solution.py:351

commit v4 on v2

--- a/solution.py
+++ b/solution.py
@@ -381,7 +381,7 @@
         .reshape(2, heads_kv, RUN * group, head_dim)
     )
 
-    attention = Attention(q, group, half, 2 * inner)
+    attention = Attention(q, group, half, 3 * inner if inner <= 4 else 2 * inner)
     state = attention.start(own)
 
     stage = own
@@ -422,8 +422,9 @@
     crossed = over_place(found[inner // 2 - 1], bits - 1, cross=1)
     most = jnp.concatenate(most)
     their_most = other_core(most)
-    state = attention.add(state, [halves[-1][1], theirs[-1][-1]])
-    state = attention.add(state, [most, their_most])
+    rest = [halves[-1][1], theirs[-1][-1], most, their_most]
+    for kvs in [rest] if inner <= 4 else [rest[:2], rest[2:]]:
+        state = attention.add(state, kvs)
     last = [tied(x, state[0]) for x in (final, crossed)]
     out = jax.ShapeDtypeStruct(queries.shape, queries.dtype)
     return attention.add(state, last, keep=1, out=out)

time: 63.3 us -> 63.9 us (level)
  the two profiles are of different devices: /device:TPU:1 before, /device:TPU:14 now
where the time goes in v4:
time: 63.9 us; the launch traced here: 63.3 us
  starting transfers between devices  23 us (36%)
  waiting for transfers between devices  22.2 us (35%)
  Pallas kernels  15.9 us (25%)
  local copies, waits for them, and re-layouts  1.62 us (3%)
    ppermute x18, starting transfers between devices, permute(): return lax.ppermute(x, AXES, pairs)  23 us
    ppermute x18, waiting for transfers between devices, permute(): return lax.ppermute(x, AXES, pairs)  22.2 us
    pallas_call x6, Pallas kernels, call(): pl.pallas_call(kernel, out_shape=shapes, in_specs=[vmem] * len(operands),...  13.9 us
    pallas_call x1, Pallas kernels, per_device(): pl.pallas_call(pack_kernel, out_shape=jax.ShapeDtypeStruct((2 * tokens *...  2.07 us
    reshape x1, local copies, waits for them, and re-layouts, per_device(): queries.reshape(2, RUN, heads_kv, group, head_dim).transpose(0, 2, 1, 3, 4)  1.41 us
  transfers between devices with their start and end apart: 18, of which 9 were waited for; matrix products, arithmetic and copies ran while one was open for 3% of the time, Pallas kernels for 14%

profile of v4, /device:TPU:14, one launch (start us, length us, event | category | flops | bytes accessed | tf_op | source)
XLA Modules:
  0.0 63.3 jit_solution(11021862766659761172)
XLA Ops:
  0.0 2.1 %pack.1.own_ref = bf16[1040,128]{1,0:T(8,128)(2,1)} custom-call(bf16[512,128]{1,0:T(8,128)(2,1)} %bitcast.16, bf16[512,128]{1,0:T(8,128)(2,1)} %bitcast.17, s32[1,128]{1,0:T(1,128)} %bitcast.18), custom_call_target="tpu_custom_call" | custom-call | tf_op jit(solution)/shard_map/pack/pallas_call | solution.py:362
  2.1 0.0 copy-start
  2.1 0.6 collective-permute-start.6
  2.7 2.6 %collective-permute-start = (bf16[1040,128]{1,0:T(8,128)(2,1)}, bf16[1040,128]{1,0:T(8,128)(2,1)S(1)}, u32[]{:S(2)}, u32[]{:S(2)}) collective-permute-start(bf16[1040,128]{1,0:T(8,128)(2,1)} %pack.1.own_ref), channel_id=1, source_target_pairs={{0,8},{1,9},{2,10},{3,11},{4,12},{5,13},{6,14},{7,15},{8,24},{9,25... | collective-permute-start | bytes 798728 | tf_op jit(solution)/shard_map/ppermute | solution.py:343
  5.3 1.4 %copy.27 = bf16[2,64,4,8,128]{4,3,1,2,0:T(8,128)(2,1)S(1)} copy(bf16[2,64,4,8,128]{4,3,2,1,0:T(8,128)(2,1)} %bitcast.15) | data formatting | bytes 2097152 | tf_op jit(solution)/shard_map/reshape | solution.py:379
  6.7 0.0 copy-done
  6.7 1.5 %attend_own.1 = (f32[8,128]{1,0:T(8,128)S(1)}, f32[2,4,512,128]{3,2,1,0:T(8,128)S(1)}, f32[2,4,512,256]{3,2,1,0:T(8,128)S(1)}, bf16[2,32,512,128]{3,2,1,0:T(8,128)(2,1)S(1)}) custom-call(bf16[2,4,512,128]{3,2,1,0:T(8,128)(2,1)S(1)} %bitcast.9, bf16[1040,128]{1,0:T(8,128)(2,1)S(1)} %copy-done), custom_call_target="tpu_custom_call" | custom-call | flops 268435456 | bytes 4194304 | tf_op jit(solution)/shard_map/attend_own/pallas_call | solution.py:285
  8.2 0.6 collective-permute-done.6
  8.8 0.6 collective-permute-start.7
  9.4 1.5 %collective-permute-done = bf16[1040,128]{1,0:T(8,128)(2,1)S(1)} collective-permute-done((bf16[1040,128]{1,0:T(8,128)(2,1)}, bf16[1040,128]{1,0:T(8,128)(2,1)S(1)}, u32[]{:S(2)}, u32[]{:S(2)}) %collective-permute-start) | collective-permute-done | bytes 266272 | tf_op jit(solution)/shard_map/ppermute | solution.py:343
  10.9 0.0 collective-permute-start.9
  11.0 3.3 %collective-permute-start.1 = (bf16[1040,128]{1,0:T(8,128)(2,1)S(1)}, bf16[1040,128]{1,0:T(8,128)(2,1)S(1)}, u32[]{:S(2)}, u32[]{:S(2)}) collective-permute-start(bf16[1040,128]{1,0:T(8,128)(2,1)S(1)} %collective-permute-done), channel_id=1, source_target_pairs={{0,8},{1,9},{2,10},{3,11},{4,12},{5,13},{6,14},{7,15},{8,24},{9,25... | collective-permute-start | bytes 798728 | tf_op jit(solution)/shard_map/ppermute | solution.py:343
  14.2 0.5 collective-permute-start.8
  14.8 4.4 %collective-permute-done.7.refs_0_ = bf16[2080,128]{1,0:T(8,128)(2,1)S(1)} collective-permute-done((bf16[2080,128]{1,0:T(8,128)(2,1)S(1)}, bf16[2080,128]{1,0:T(8,128)(2,1)S(1)}, u32[]{:S(2)}, u32[]{:S(2)}) %collective-permute-start.7) | collective-permute-done | bytes 532512 | tf_op jit(solution)/shard_map/ppermute | solution.py:343
  19.2 0.0 collective-permute-start.10
  19.2 1.3 %collective-permute-done.1 = bf16[1040,128]{1,0:T(8,128)(2,1)S(1)} collective-permute-done((bf16[1040,128]{1,0:T(8,128)(2,1)S(1)}, bf16[1040,128]{1,0:T(8,128)(2,1)S(1)}, u32[]{:S(2)}, u32[]{:S(2)}) %collective-permute-start.1) | collective-permute-done | bytes 266272 | tf_op jit(solution)/shard_map/ppermute | solution.py:343
  20.6 0.5 collective-permute-start.5
  21.1 3.4 %collective-permute-start.2 = (bf16[1040,128]{1,0:T(8,128)(2,1)S(1)}, bf16[1040,128]{1,0:T(8,128)(2,1)S(1)}, u32[]{:S(2)}, u32[]{:S(2)}) collective-permute-start(bf16[1040,128]{1,0:T(8,128)(2,1)S(1)} %collective-permute-done.1), channel_id=1, source_target_pairs={{0,8},{1,9},{2,10},{3,11},{4,12},{5,13},{6,14},{7,15},{8,24},{9,25... | collective-permute-start | bytes 798728 | tf_op jit(solution)/shard_map/ppermute | solution.py:343
  24.5 0.0 collective-permute-done.9.refs_1_
  24.5 0.4 attend.5
  24.8 0.0 collective-permute-done.8
  24.9 2.7 %collective-permute-start.12 = (bf16[2080,128]{1,0:T(8,128)(2,1)S(1)}, bf16[2080,128]{1,0:T(8,128)(2,1)S(1)}, u32[]{:S(2)}, u32[]{:S(2)}) collective-permute-start(bf16[2080,128]{1,0:T(8,128)(2,1)S(1)} %constant_dynamic-update-slice_fusion.refs_1_), channel_id=1, source_target_pairs={{0,2},{1,3},{2,0},{3,1},{4,5},{5,4},{6,7},{7,6},{8,10},{9,11},{10,... | collective-permute-start | bytes 1597448 | tf_op jit(solution)/shard_map/ppermute | solution.py:343
  27.6 0.0 collective-permute-done.10.refs_2_
  27.6 2.2 %attend.6 = (f32[8,128]{1,0:T(8,128)S(1)}, f32[2,4,512,128]{3,2,1,0:T(8,128)S(1)}, f32[2,4,512,256]{3,2,1,0:T(8,128)S(1)}, bf16[2,32,512,128]{3,2,1,0:T(8,128)(2,1)S(1)}) custom-call(bf16[2,4,512,128]{3,2,1,0:T(8,128)(2,1)S(1)} %bitcast.11, ...), custom_call_target="tpu_custom_call", output_to_operand_aliasing={{0}: (4, {}), {1}: (5, {}), {2}: (6, {}), {3}: (7, {})} | custom-call | flops 805306368 | bytes 4194304 | tf_op jit(solution)/shard_map/attend/pallas_call | solution.py:285
  29.8 0.0 collective-permute-done.5
  29.9 1.3 %collective-permute-start.11 = (bf16[2080,128]{1,0:T(8,128)(2,1)S(1)}, bf16[2080,128]{1,0:T(8,128)(2,1)S(1)}, u32[]{:S(2)}, u32[]{:S(2)}) collective-permute-start(bf16[2080,128]{1,0:T(8,128)(2,1)S(1)} %constant_dynamic-update-slice_fusion.2.refs_2_), channel_id=1, source_target_pairs={{0,2},{1,3},{2,0},{3,1},{4,5},{5,4},{6,7},{7,6},{8,10},{9,11},{10,... | collective-permute-start | bytes 1597448 | tf_op jit(solution)/shard_map/ppermute | solution.py:343
  31.2 3.6 %collective-permute-done.12.refs_0_ = bf16[2080,128]{1,0:T(8,128)(2,1)S(1)} collective-permute-done((bf16[2080,128]{1,0:T(8,128)(2,1)S(1)}, bf16[2080,128]{1,0:T(8,128)(2,1)S(1)}, u32[]{:S(2)}, u32[]{:S(2)}) %collective-permute-start.12) | collective-permute-done | bytes 532512 | tf_op jit(solution)/shard_map/ppermute | solution.py:343
  34.8 0.1 pad_maximum_fusion.1
  34.9 0.1 collective-permute-start.13
  35.0 0.0 collective-permute-done.2
  35.0 0.9 %collective-permute-start.3 = (bf16[1040,128]{1,0:T(8,128)(2,1)S(1)}, bf16[1040,128]{1,0:T(8,128)(2,1)S(1)}, u32[]{:S(2)}, u32[]{:S(2)}) collective-permute-start(bf16[1040,128]{1,0:T(8,128)(2,1)S(1)} %collective-permute-done.2), channel_id=1, source_target_pairs={{0,1},{1,0},{2,3},{3,2},{4,6},{5,7},{6,4},{7,5},{8,9},{9,8},{10,11... | collective-permute-start | bytes 798728 | tf_op jit(solution)/shard_map/ppermute | solution.py:343
  35.9 1.5 %collective-permute-start.15 = (bf16[1040,128]{1,0:T(8,128)(2,1)S(1)}, bf16[1040,128]{1,0:T(8,128)(2,1)S(1)}, u32[]{:S(2)}, u32[]{:S(2)}) collective-permute-start(bf16[1040,128]{1,0:T(8,128)(2,1)S(1)} %collective-permute-done.2), channel_id=1, source_target_pairs={{0,2},{1,3},{2,0},{3,1},{4,5},{5,4},{6,7},{7,6},{8,10},{9,11},{10,... | collective-permute-start | bytes 798728 | tf_op jit(solution)/shard_map/ppermute | solution.py:343
  37.5 5.2 %collective-permute-done.11.refs_0_ = bf16[2080,128]{1,0:T(8,128)(2,1)S(1)} collective-permute-done((bf16[2080,128]{1,0:T(8,128)(2,1)S(1)}, bf16[2080,128]{1,0:T(8,128)(2,1)S(1)}, u32[]{:S(2)}, u32[]{:S(2)}) %collective-permute-start.11) | collective-permute-done | bytes 532512 | tf_op jit(solution)/shard_map/ppermute | solution.py:343
  42.7 0.1 pad_maximum_fusion
  42.7 0.0 collective-permute-done.13.refs_1_
  42.7 2.5 %attend.7 = (f32[8,128]{1,0:T(8,128)S(1)}, f32[2,4,512,128]{3,2,1,0:T(8,128)S(1)}, f32[2,4,512,256]{3,2,1,0:T(8,128)S(1)}, bf16[2,32,512,128]{3,2,1,0:T(8,128)(2,1)S(1)}) custom-call(bf16[2,4,512,128]{3,2,1,0:T(8,128)(2,1)S(1)} %bitcast.12, ...), custom_call_target="tpu_custom_call", output_to_operand_aliasing={{0}: (4, {}), {1}: (5, {}), {2}: (6, {}), {3}: (7, {})} | custom-call | flops 1073741824 | bytes 4194304 | tf_op jit(solution)/shard_map/attend/pallas_call | solution.py:285
  45.3 0.6 %collective-permute-start.14 = (bf16[4160,128]{1,0:T(8,128)(2,1)S(1)}, bf16[4160,128]{1,0:T(8,128)(2,1)S(1)}, u32[]{:S(2)}, u32[]{:S(2)}) collective-permute-start(bf16[4160,128]{1,0:T(8,128)(2,1)S(1)} %pad_maximum_fusion), channel_id=1, source_target_pairs={{0,4},{1,5},{2,6},{3,7},{4,0},{5,1},{6,2},{7,3},{8,12},{9,13},{10,... | collective-permute-start | bytes 3194888 | tf_op jit(solution)/shard_map/ppermute | solution.py:343
  45.9 0.0 collective-permute-done.3
  45.9 0.3 collective-permute-done.15
  46.3 0.1 collective-permute-start.16
  46.4 3.9 %collective-permute-start.17 = (bf16[1040,128]{1,0:T(8,128)(2,1)S(1)}, bf16[1040,128]{1,0:T(8,128)(2,1)S(1)}, u32[]{:S(2)}, u32[]{:S(2)}) collective-permute-start(bf16[1040,128]{1,0:T(8,128)(2,1)S(1)} %collective-permute-done.3), channel_id=1, source_target_pairs={{0,6},{1,7},{2,4},{3,5},{4,1},{5,0},{6,3},{7,2},{8,14},{9,15},{10,... | collective-permute-start | bytes 798728 | tf_op jit(solution)/shard_map/ppermute | solution.py:343
  50.3 0.3 collective-permute-start.4
  50.6 0.0 collective-permute-done.16.refs_3_
  50.6 0.0 collective-permute-done.14.refs_1_
  50.6 2.0 %attend.8 = (f32[8,128]{1,0:T(8,128)S(1)}, f32[2,4,512,128]{3,2,1,0:T(8,128)S(1)}, f32[2,4,512,256]{3,2,1,0:T(8,128)S(1)}, bf16[2,32,512,128]{3,2,1,0:T(8,128)(2,1)S(1)}) custom-call(bf16[2,4,512,128]{3,2,1,0:T(8,128)(2,1)S(1)} %bitcast.13, ...), custom_call_target="tpu_custom_call", output_to_operand_aliasing={{0}: (5, {}), {1}: (6, {}), {2}: (7, {}), {3}: (8, {})} | custom-call | flops 1610612736 | bytes 4194304 | tf_op jit(solution)/shard_map/attend/pallas_call | solution.py:285
  52.7 1.6 %collective-permute-done.17.refs_1_ = bf16[1040,128]{1,0:T(8,128)(2,1)S(1)} collective-permute-done((bf16[1040,128]{1,0:T(8,128)(2,1)S(1)}, bf16[1040,128]{1,0:T(8,128)(2,1)S(1)}, u32[]{:S(2)}, u32[]{:S(2)}) %collective-permute-start.17) | collective-permute-done | bytes 266272 | tf_op jit(solution)/shard_map/ppermute | solution.py:343
  54.2 3.6 %collective-permute-done.4.refs_0_ = bf16[1040,128]{1,0:T(8,128)(2,1)S(1)} collective-permute-done((bf16[1040,128]{1,0:T(8,128)(2,1)S(1)}, bf16[1040,128]{1,0:T(8,128)(2,1)S(1)}, u32[]{:S(2)}, u32[]{:S(2)}) %collective-permute-start.4) | collective-permute-done | bytes 266272 | tf_op jit(solution)/shard_map/ppermute | solution.py:343
  57.9 5.3 %attend.9 = (bf16[128,32,128]{2,1,0:T(8,128)(2,1)}, f32[8,128]{1,0:T(8,128)S(1)}, f32[2,4,512,128]{3,2,1,0:T(8,128)S(1)}, f32[2,4,512,256]{3,2,1,0:T(8,128)S(1)}, bf16[2,32,512,128]{3,2,1,0:T(8,128)(2,1)S(1)}) custom-call(bf16[2,4,512,128]{3,2,1,0:T(8,128)(2,1)S(1)} %bitcast.14, ...), custom_call_target="tpu_custom_call", output_to_operand_aliasing={{1}: (3, {}), {2}: (4, {}), {3}: (5, {}), {4}: (6, {})} | custom-call | flops 268435456 | bytes 4194304 | tf_op jit(solution)/shard_map/attend/pallas_call | solution.py:285
  (8 shorter events, 0.2 us)
Async XLA Ops:
  2.1 4.6 %copy-start = (bf16[1040,128]{1,0:T(8,128)(2,1)S(1)}, bf16[1040,128]{1,0:T(8,128)(2,1)}, u32[]{:S(2)}) copy-start(bf16[1040,128]{1,0:T(8,128)(2,1)} %pack.1.own_ref) | copy-start | bytes 798724
  2.1 6.7 %collective-permute-start.6 = (bf16[1040,128]{1,0:T(8,128)(2,1)}, bf16[1040,128]{1,0:T(8,128)(2,1)S(1)}, u32[]{:S(2)}, u32[]{:S(2)}) collective-permute-start(bf16[1040,128]{1,0:T(8,128)(2,1)} %pack.1.own_ref), channel_id=1, source_target_pairs={{0,1},{1,0},{2,3},{3,2},{4,6},{5,7},{6,4},{7,5},{8,9},{9,8},{10,11... | collective-permute-start | bytes 798728 | tf_op jit(solution)/shard_map/ppermute | solution.py:343
  2.7 8.3 %collective-permute-start = (bf16[1040,128]{1,0:T(8,128)(2,1)}, bf16[1040,128]{1,0:T(8,128)(2,1)S(1)}, u32[]{:S(2)}, u32[]{:S(2)}) collective-permute-start(bf16[1040,128]{1,0:T(8,128)(2,1)} %pack.1.own_ref), channel_id=1, source_target_pairs={{0,8},{1,9},{2,10},{3,11},{4,12},{5,13},{6,14},{7,15},{8,24},{9,25... | collective-permute-start | bytes 798728 | tf_op jit(solution)/shard_map/ppermute | solution.py:343
  8.8 10.4 %collective-permute-start.7 = (bf16[2080,128]{1,0:T(8,128)(2,1)S(1)}, bf16[2080,128]{1,0:T(8,128)(2,1)S(1)}, u32[]{:S(2)}, u32[]{:S(2)}) collective-permute-start(bf16[2080,128]{1,0:T(8,128)(2,1)S(1)} %pad_maximum_fusion.2.refs_0_), channel_id=1, source_target_pairs={{0,2},{1,3},{2,0},{3,1},{4,5},{5,4},{6,7},{7,6},{8,10},{9,11},{10,... | collective-permute-start | bytes 1597448 | tf_op jit(solution)/shard_map/ppermute | solution.py:343
  10.9 13.5 %collective-permute-start.9 = (bf16[2080,128]{1,0:T(8,128)(2,1)S(1)}, bf16[2080,128]{1,0:T(8,128)(2,1)S(1)}, u32[]{:S(2)}, u32[]{:S(2)}) collective-permute-start(bf16[2080,128]{1,0:T(8,128)(2,1)S(1)} %pad_maximum_fusion.2.refs_0_), channel_id=1, source_target_pairs={{0,4},{1,5},{2,6},{3,7},{4,0},{5,1},{6,2},{7,3},{8,12},{9,13},{10,... | collective-permute-start | bytes 1597448 | tf_op jit(solution)/shard_map/ppermute | solution.py:343
  11.0 9.6 %collective-permute-start.1 = (bf16[1040,128]{1,0:T(8,128)(2,1)S(1)}, bf16[1040,128]{1,0:T(8,128)(2,1)S(1)}, u32[]{:S(2)}, u32[]{:S(2)}) collective-permute-start(bf16[1040,128]{1,0:T(8,128)(2,1)S(1)} %collective-permute-done), channel_id=1, source_target_pairs={{0,8},{1,9},{2,10},{3,11},{4,12},{5,13},{6,14},{7,15},{8,24},{9,25... | collective-permute-start | bytes 798728 | tf_op jit(solution)/shard_map/ppermute | solution.py:343
  14.2 10.6 %collective-permute-start.8 = (bf16[1040,128]{1,0:T(8,128)(2,1)S(1)}, bf16[1040,128]{1,0:T(8,128)(2,1)S(1)}, u32[]{:S(2)}, u32[]{:S(2)}) collective-permute-start(bf16[1040,128]{1,0:T(8,128)(2,1)S(1)} %collective-permute-done), channel_id=1, source_target_pairs={{0,1},{1,0},{2,3},{3,2},{4,6},{5,7},{6,4},{7,5},{8,9},{9,8},{10,11... | collective-permute-start | bytes 798728 | tf_op jit(solution)/shard_map/ppermute | solution.py:343
  19.2 8.4 %collective-permute-start.10 = (bf16[2080,128]{1,0:T(8,128)(2,1)S(1)}, bf16[2080,128]{1,0:T(8,128)(2,1)S(1)}, u32[]{:S(2)}, u32[]{:S(2)}) collective-permute-start(bf16[2080,128]{1,0:T(8,128)(2,1)S(1)} %collective-permute-done.7.refs_0_), channel_id=1, source_target_pairs={{0,4},{1,5},{2,6},{3,7},{4,0},{5,1},{6,2},{7,3},{8,12},{9,13},{10,... | collective-permute-start | bytes 1597448 | tf_op jit(solution)/shard_map/ppermute | solution.py:343
  20.6 9.3 %collective-permute-start.5 = (bf16[1040,128]{1,0:T(8,128)(2,1)S(1)}, bf16[1040,128]{1,0:T(8,128)(2,1)S(1)}, u32[]{:S(2)}, u32[]{:S(2)}) collective-permute-start(bf16[1040,128]{1,0:T(8,128)(2,1)S(1)} %collective-permute-done.1), channel_id=1, source_target_pairs={{0,1},{1,0},{2,3},{3,2},{4,6},{5,7},{6,4},{7,5},{8,9},{9,8},{10,11... | collective-permute-start | bytes 798728 | tf_op jit(solution)/shard_map/ppermute | solution.py:343
  21.1 13.9 %collective-permute-start.2 = (bf16[1040,128]{1,0:T(8,128)(2,1)S(1)}, bf16[1040,128]{1,0:T(8,128)(2,1)S(1)}, u32[]{:S(2)}, u32[]{:S(2)}) collective-permute-start(bf16[1040,128]{1,0:T(8,128)(2,1)S(1)} %collective-permute-done.1), channel_id=1, source_target_pairs={{0,8},{1,9},{2,10},{3,11},{4,12},{5,13},{6,14},{7,15},{8,24},{9,25... | collective-permute-start | bytes 798728 | tf_op jit(solution)/shard_map/ppermute | solution.py:343
  24.9 9.9 %collective-permute-start.12 = (bf16[2080,128]{1,0:T(8,128)(2,1)S(1)}, bf16[2080,128]{1,0:T(8,128)(2,1)S(1)}, u32[]{:S(2)}, u32[]{:S(2)}) collective-permute-start(bf16[2080,128]{1,0:T(8,128)(2,1)S(1)} %constant_dynamic-update-slice_fusion.refs_1_), channel_id=1, source_target_pairs={{0,2},{1,3},{2,0},{3,1},{4,5},{5,4},{6,7},{7,6},{8,10},{9,11},{10,... | collective-permute-start | bytes 1597448 | tf_op jit(solution)/shard_map/ppermute | solution.py:343
  29.9 12.8 %collective-permute-start.11 = (bf16[2080,128]{1,0:T(8,128)(2,1)S(1)}, bf16[2080,128]{1,0:T(8,128)(2,1)S(1)}, u32[]{:S(2)}, u32[]{:S(2)}) collective-permute-start(bf16[2080,128]{1,0:T(8,128)(2,1)S(1)} %constant_dynamic-update-slice_fusion.2.refs_2_), channel_id=1, source_target_pairs={{0,2},{1,3},{2,0},{3,1},{4,5},{5,4},{6,7},{7,6},{8,10},{9,11},{10,... | collective-permute-start | bytes 1597448 | tf_op jit(solution)/shard_map/ppermute | solution.py:343
  34.9 7.8 %collective-permute-start.13 = (bf16[4160,128]{1,0:T(8,128)(2,1)S(1)}, bf16[4160,128]{1,0:T(8,128)(2,1)S(1)}, u32[]{:S(2)}, u32[]{:S(2)}) collective-permute-start(bf16[4160,128]{1,0:T(8,128)(2,1)S(1)} %pad_maximum_fusion.1), channel_id=1, source_target_pairs={{0,4},{1,5},{2,6},{3,7},{4,0},{5,1},{6,2},{7,3},{8,12},{9,13},{10,... | collective-permute-start | bytes 3194888 | tf_op jit(solution)/shard_map/ppermute | solution.py:343
  35.0 10.9 %collective-permute-start.3 = (bf16[1040,128]{1,0:T(8,128)(2,1)S(1)}, bf16[1040,128]{1,0:T(8,128)(2,1)S(1)}, u32[]{:S(2)}, u32[]{:S(2)}) collective-permute-start(bf16[1040,128]{1,0:T(8,128)(2,1)S(1)} %collective-permute-done.2), channel_id=1, source_target_pairs={{0,1},{1,0},{2,3},{3,2},{4,6},{5,7},{6,4},{7,5},{8,9},{9,8},{10,11... | collective-permute-start | bytes 798728 | tf_op jit(solution)/shard_map/ppermute | solution.py:343
  35.9 10.3 %collective-permute-start.15 = (bf16[1040,128]{1,0:T(8,128)(2,1)S(1)}, bf16[1040,128]{1,0:T(8,128)(2,1)S(1)}, u32[]{:S(2)}, u32[]{:S(2)}) collective-permute-start(bf16[1040,128]{1,0:T(8,128)(2,1)S(1)} %collective-permute-done.2), channel_id=1, source_target_pairs={{0,2},{1,3},{2,0},{3,1},{4,5},{5,4},{6,7},{7,6},{8,10},{9,11},{10,... | collective-permute-start | bytes 798728 | tf_op jit(solution)/shard_map/ppermute | solution.py:343
  45.3 5.4 %collective-permute-start.14 = (bf16[4160,128]{1,0:T(8,128)(2,1)S(1)}, bf16[4160,128]{1,0:T(8,128)(2,1)S(1)}, u32[]{:S(2)}, u32[]{:S(2)}) collective-permute-start(bf16[4160,128]{1,0:T(8,128)(2,1)S(1)} %pad_maximum_fusion), channel_id=1, source_target_pairs={{0,4},{1,5},{2,6},{3,7},{4,0},{5,1},{6,2},{7,3},{8,12},{9,13},{10,... | collective-permute-start | bytes 3194888 | tf_op jit(solution)/shard_map/ppermute | solution.py:343
  46.3 4.3 %collective-permute-start.16 = (bf16[3120,128]{1,0:T(8,128)(2,1)S(1)}, bf16[3120,128]{1,0:T(8,128)(2,1)S(1)}, u32[]{:S(2)}, u32[]{:S(2)}) collective-permute-start(bf16[3120,128]{1,0:T(8,128)(2,1)S(1)} %constant_dynamic-update-slice_fusion.4.refs_2_), channel_id=1, source_target_pairs={{0,4},{1,5},{2,6},{3,7},{4,0},{5,1},{6,2},{7,3},{8,12},{9,13},{10,... | collective-permute-start | bytes 2396168 | tf_op jit(solution)/shard_map/ppermute | solution.py:343
  46.4 7.9 %collective-permute-start.17 = (bf16[1040,128]{1,0:T(8,128)(2,1)S(1)}, bf16[1040,128]{1,0:T(8,128)(2,1)S(1)}, u32[]{:S(2)}, u32[]{:S(2)}) collective-permute-start(bf16[1040,128]{1,0:T(8,128)(2,1)S(1)} %collective-permute-done.3), channel_id=1, source_target_pairs={{0,6},{1,7},{2,4},{3,5},{4,1},{5,0},{6,3},{7,2},{8,14},{9,15},{10,... | collective-permute-start | bytes 798728 | tf_op jit(solution)/shard_map/ppermute | solution.py:343
  50.3 7.6 %collective-permute-start.4 = (bf16[1040,128]{1,0:T(8,128)(2,1)S(1)}, bf16[1040,128]{1,0:T(8,128)(2,1)S(1)}, u32[]{:S(2)}, u32[]{:S(2)}) collective-permute-start(bf16[1040,128]{1,0:T(8,128)(2,1)S(1)} %collective-permute-done.3), channel_id=1, source_target_pairs={{0,2},{1,3},{2,0},{3,1},{4,5},{5,4},{6,7},{7,6},{8,10},{9,11},{10,... | collective-permute-start | bytes 798728 | tf_op jit(solution)/shard_map/ppermute | solution.py:343

commit v5 on v4

--- a/solution.py
+++ b/solution.py
@@ -228,7 +228,9 @@
         copy.wait()
 
 
-def pack_kernel(k_any, v_any, positions_any, own_ref, k_ref, v_ref, positions_ref, sems):
+def pack_kernel(
+    k_any, v_any, positions_any, own_any, k_ref, v_ref, positions_ref, own_ref, sems
+):
     pairs = ((k_any, k_ref), (v_any, v_ref), (positions_any, positions_ref))
     copies = [
         pltpu.make_async_copy(source, target, sems.at[n])
@@ -252,10 +254,23 @@
             )
             start = (2 * r + n) * rows
             own_ref[start : start + rows] = moved.astype(own_ref.dtype)
+            place = slice(start, start + rows)
+            copy = pltpu.make_async_copy(
+                own_ref.at[place], own_any.at[place], sems.at[len(copies)]
+            )
+            copy.start()
+            copies.append(copy)
     copies[2].wait()
     numbers = (positions_ref[...] // RUN).astype(jnp.float32)
     numbers = jnp.broadcast_to(numbers, (16, numbers.shape[1]))
     own_ref[4 * rows :] = numbers.astype(own_ref.dtype)
+    place = slice(4 * rows, 4 * rows + 16)
+    copy = pltpu.make_async_copy(
+        own_ref.at[place], own_any.at[place], sems.at[len(copies)]
+    )
+    copy.start()
+    for copy in copies[3:] + [copy]:
+        copy.wait()
 
 
 class Attention:
@@ -365,12 +380,13 @@
             (2 * tokens * heads_kv + 16, head_dim), keys.dtype
         ),
         in_specs=[pl.BlockSpec(memory_space=pltpu.HBM)] * 3,
-        out_specs=pl.BlockSpec(memory_space=pltpu.VMEM),
+        out_specs=pl.BlockSpec(memory_space=pltpu.HBM),
         scratch_shapes=[
             pltpu.VMEM(flat.shape, flat.dtype),
             pltpu.VMEM(flat.shape, flat.dtype),
             pltpu.VMEM((1, tokens), jnp.int32),
-            pltpu.SemaphoreType.DMA((3,)),
+            pltpu.VMEM((2 * tokens * heads_kv + 16, head_dim), keys.dtype),
+            pltpu.SemaphoreType.DMA((8,)),
         ],
         compiler_params=pltpu.CompilerParams(vmem_limit_bytes=60 * 1024 * 1024),
         name="pack",
@@ -424,7 +440,7 @@
     their_most = other_core(most)
     rest = [halves[-1][1], theirs[-1][-1], most, their_most]
     for kvs in [rest] if inner <= 4 else [rest[:2], rest[2:]]:
-        state = attention.add(state, kvs)
+        state = attention.add(state, kvs, keep=2)
     last = [tied(x, state[0]) for x in (final, crossed)]
     out = jax.ShapeDtypeStruct(queries.shape, queries.dtype)
     return attention.add(state, last, keep=1, out=out)

time: 63.9 us -> 64.1 us (level)
  the two profiles are of different devices: /device:TPU:14 before, /device:TPU:8 now
where the time goes in v5:
time: 64.1 us; the launch traced here: 62.9 us
  Pallas kernels  22.3 us (35%)
  starting transfers between devices  20.6 us (32%)
  waiting for transfers between devices  17.9 us (28%)
  local copies, waits for them, and re-layouts  1.62 us (3%)
    ppermute x18, starting transfers between devices, permute(): return lax.ppermute(x, AXES, pairs)  20.6 us
    pallas_call x6, Pallas kernels, call(): pl.pallas_call(kernel, out_shape=shapes, in_specs=[vmem] * len(operands),...  20.3 us
    ppermute x18, waiting for transfers between devices, permute(): return lax.ppermute(x, AXES, pairs)  17.9 us
    pallas_call x1, Pallas kernels, per_device(): pl.pallas_call(pack_kernel, out_shape=jax.ShapeDtypeStruct((2 * tokens *...  2.05 us
    reshape x1, local copies, waits for them, and re-layouts, per_device(): queries.reshape(2, RUN, heads_kv, group, head_dim).transpose(0, 2, 1, 3, 4)  1.41 us
  transfers between devices with their start and end apart: 18, of which 6 were waited for; matrix products, arithmetic and copies ran while one was open for 3% of the time, Pallas kernels for 25%

profile of v5, /device:TPU:8, one launch (start us, length us, event | category | flops | bytes accessed | tf_op | source)
XLA Modules:
  0.0 62.9 jit_solution(459904629606390078)
XLA Ops:
  0.0 2.1 %pack.1.own_ref = bf16[1040,128]{1,0:T(8,128)(2,1)} custom-call(bf16[512,128]{1,0:T(8,128)(2,1)} %bitcast.16, bf16[512,128]{1,0:T(8,128)(2,1)} %bitcast.17, s32[1,128]{1,0:T(1,128)} %bitcast.18), custom_call_target="tpu_custom_call" | custom-call | tf_op jit(solution)/shard_map/pack/pallas_call | solution.py:377
  2.1 0.0 copy-start
  2.1 1.6 %collective-permute-start.6 = (bf16[1040,128]{1,0:T(8,128)(2,1)}, bf16[1040,128]{1,0:T(8,128)(2,1)S(1)}, u32[]{:S(2)}, u32[]{:S(2)}) collective-permute-start(bf16[1040,128]{1,0:T(8,128)(2,1)} %pack.1.own_ref), channel_id=1, source_target_pairs={{0,1},{1,0},{2,3},{3,2},{4,6},{5,7},{6,4},{7,5},{8,9},{9,8},{10,11... | collective-permute-start | bytes 798728 | tf_op jit(solution)/shard_map/ppermute | solution.py:358
  3.6 2.6 %collective-permute-start = (bf16[1040,128]{1,0:T(8,128)(2,1)}, bf16[1040,128]{1,0:T(8,128)(2,1)S(1)}, u32[]{:S(2)}, u32[]{:S(2)}) collective-permute-start(bf16[1040,128]{1,0:T(8,128)(2,1)} %pack.1.own_ref), channel_id=1, source_target_pairs={{0,8},{1,9},{2,10},{3,11},{4,12},{5,13},{6,14},{7,15},{8,24},{9,25... | collective-permute-start | bytes 798728 | tf_op jit(solution)/shard_map/ppermute | solution.py:358
  6.2 1.4 %copy.27 = bf16[2,64,4,8,128]{4,3,1,2,0:T(8,128)(2,1)S(1)} copy(bf16[2,64,4,8,128]{4,3,2,1,0:T(8,128)(2,1)} %bitcast.15) | data formatting | bytes 2097152 | tf_op jit(solution)/shard_map/reshape | solution.py:395
  7.6 0.0 copy-done
  7.7 1.5 %attend_own.1 = (f32[8,128]{1,0:T(8,128)S(1)}, f32[2,4,512,128]{3,2,1,0:T(8,128)S(1)}, f32[2,4,512,256]{3,2,1,0:T(8,128)S(1)}, bf16[2,32,512,128]{3,2,1,0:T(8,128)(2,1)S(1)}) custom-call(bf16[2,4,512,128]{3,2,1,0:T(8,128)(2,1)S(1)} %bitcast.9, bf16[1040,128]{1,0:T(8,128)(2,1)S(1)} %copy-done), custom_call_target="tpu_custom_call" | custom-call | flops 268435456 | bytes 4194304 | tf_op jit(solution)/shard_map/attend_own/pallas_call | solution.py:300
  9.1 0.0 collective-permute-done.6
  9.2 1.6 %collective-permute-start.7 = (bf16[2080,128]{1,0:T(8,128)(2,1)S(1)}, bf16[2080,128]{1,0:T(8,128)(2,1)S(1)}, u32[]{:S(2)}, u32[]{:S(2)}) collective-permute-start(bf16[2080,128]{1,0:T(8,128)(2,1)S(1)} %pad_maximum_fusion.2.refs_0_), channel_id=1, source_target_pairs={{0,2},{1,3},{2,0},{3,1},{4,5},{5,4},{6,7},{7,6},{8,10},{9,11},{10,... | collective-permute-start | bytes 1597448 | tf_op jit(solution)/shard_map/ppermute | solution.py:358
  10.8 1.2 %collective-permute-done = bf16[1040,128]{1,0:T(8,128)(2,1)S(1)} collective-permute-done((bf16[1040,128]{1,0:T(8,128)(2,1)}, bf16[1040,128]{1,0:T(8,128)(2,1)S(1)}, u32[]{:S(2)}, u32[]{:S(2)}) %collective-permute-start) | collective-permute-done | bytes 266272 | tf_op jit(solution)/shard_map/ppermute | solution.py:358
  11.9 0.0 collective-permute-start.9
  11.9 3.3 %collective-permute-start.1 = (bf16[1040,128]{1,0:T(8,128)(2,1)S(1)}, bf16[1040,128]{1,0:T(8,128)(2,1)S(1)}, u32[]{:S(2)}, u32[]{:S(2)}) collective-permute-start(bf16[1040,128]{1,0:T(8,128)(2,1)S(1)} %collective-permute-done), channel_id=1, source_target_pairs={{0,8},{1,9},{2,10},{3,11},{4,12},{5,13},{6,14},{7,15},{8,24},{9,25... | collective-permute-start | bytes 798728 | tf_op jit(solution)/shard_map/ppermute | solution.py:358
  15.2 1.5 %collective-permute-start.8 = (bf16[1040,128]{1,0:T(8,128)(2,1)S(1)}, bf16[1040,128]{1,0:T(8,128)(2,1)S(1)}, u32[]{:S(2)}, u32[]{:S(2)}) collective-permute-start(bf16[1040,128]{1,0:T(8,128)(2,1)S(1)} %collective-permute-done), channel_id=1, source_target_pairs={{0,1},{1,0},{2,3},{3,2},{4,6},{5,7},{6,4},{7,5},{8,9},{9,8},{10,11... | collective-permute-start | bytes 798728 | tf_op jit(solution)/shard_map/ppermute | solution.py:358
  16.7 2.3 %collective-permute-done.7.refs_0_ = bf16[2080,128]{1,0:T(8,128)(2,1)S(1)} collective-permute-done((bf16[2080,128]{1,0:T(8,128)(2,1)S(1)}, bf16[2080,128]{1,0:T(8,128)(2,1)S(1)}, u32[]{:S(2)}, u32[]{:S(2)}) %collective-permute-start.7) | collective-permute-done | bytes 532512 | tf_op jit(solution)/shard_map/ppermute | solution.py:358
  19.0 0.0 collective-permute-start.10
  19.0 2.5 %collective-permute-done.1 = bf16[1040,128]{1,0:T(8,128)(2,1)S(1)} collective-permute-done((bf16[1040,128]{1,0:T(8,128)(2,1)S(1)}, bf16[1040,128]{1,0:T(8,128)(2,1)S(1)}, u32[]{:S(2)}, u32[]{:S(2)}) %collective-permute-start.1) | collective-permute-done | bytes 266272 | tf_op jit(solution)/shard_map/ppermute | solution.py:358
  21.5 1.5 %collective-permute-start.5 = (bf16[1040,128]{1,0:T(8,128)(2,1)S(1)}, bf16[1040,128]{1,0:T(8,128)(2,1)S(1)}, u32[]{:S(2)}, u32[]{:S(2)}) collective-permute-start(bf16[1040,128]{1,0:T(8,128)(2,1)S(1)} %collective-permute-done.1), channel_id=1, source_target_pairs={{0,1},{1,0},{2,3},{3,2},{4,6},{5,7},{6,4},{7,5},{8,9},{9,8},{10,11... | collective-permute-start | bytes 798728 | tf_op jit(solution)/shard_map/ppermute | solution.py:358
  23.0 3.4 %collective-permute-start.2 = (bf16[1040,128]{1,0:T(8,128)(2,1)S(1)}, bf16[1040,128]{1,0:T(8,128)(2,1)S(1)}, u32[]{:S(2)}, u32[]{:S(2)}) collective-permute-start(bf16[1040,128]{1,0:T(8,128)(2,1)S(1)} %collective-permute-done.1), channel_id=1, source_target_pairs={{0,8},{1,9},{2,10},{3,11},{4,12},{5,13},{6,14},{7,15},{8,24},{9,25... | collective-permute-start | bytes 798728 | tf_op jit(solution)/shard_map/ppermute | solution.py:358
  26.4 0.0 collective-permute-done.9.refs_1_
  26.4 0.4 attend.5
  26.8 0.0 collective-permute-done.8
  26.9 0.6 collective-permute-start.12
  27.5 0.0 collective-permute-done.10.refs_2_
  27.5 4.0 %attend.6 = (f32[8,128]{1,0:T(8,128)S(1)}, f32[2,4,512,128]{3,2,1,0:T(8,128)S(1)}, f32[2,4,512,256]{3,2,1,0:T(8,128)S(1)}, bf16[2,32,512,128]{3,2,1,0:T(8,128)(2,1)S(1)}) custom-call(bf16[2,4,512,128]{3,2,1,0:T(8,128)(2,1)S(1)} %bitcast.11, ...), custom_call_target="tpu_custom_call", output_to_operand_aliasing={{0}: (4, {}), {1}: (5, {}), {2}: (6, {}), {3}: (7, {})} | custom-call | flops 805306368 | bytes 4194304 | tf_op jit(solution)/shard_map/attend/pallas_call | solution.py:300
  31.4 0.0 collective-permute-done.5
  31.5 1.2 %collective-permute-start.11 = (bf16[2080,128]{1,0:T(8,128)(2,1)S(1)}, bf16[2080,128]{1,0:T(8,128)(2,1)S(1)}, u32[]{:S(2)}, u32[]{:S(2)}) collective-permute-start(bf16[2080,128]{1,0:T(8,128)(2,1)S(1)} %constant_dynamic-update-slice_fusion.2.refs_2_), channel_id=1, source_target_pairs={{0,2},{1,3},{2,0},{3,1},{4,5},{5,4},{6,7},{7,6},{8,10},{9,11},{10,... | collective-permute-start | bytes 1597448 | tf_op jit(solution)/shard_map/ppermute | solution.py:358
  32.6 3.6 %collective-permute-done.12.refs_0_ = bf16[2080,128]{1,0:T(8,128)(2,1)S(1)} collective-permute-done((bf16[2080,128]{1,0:T(8,128)(2,1)S(1)}, bf16[2080,128]{1,0:T(8,128)(2,1)S(1)}, u32[]{:S(2)}, u32[]{:S(2)}) %collective-permute-start.12) | collective-permute-done | bytes 532512 | tf_op jit(solution)/shard_map/ppermute | solution.py:358
  36.2 0.1 pad_maximum_fusion.1
  36.3 0.1 collective-permute-start.13
  36.3 0.0 collective-permute-done.2
  36.4 0.6 collective-permute-start.3
  37.0 0.5 collective-permute-start.15
  37.4 6.8 %collective-permute-done.11.refs_0_ = bf16[2080,128]{1,0:T(8,128)(2,1)S(1)} collective-permute-done((bf16[2080,128]{1,0:T(8,128)(2,1)S(1)}, bf16[2080,128]{1,0:T(8,128)(2,1)S(1)}, u32[]{:S(2)}, u32[]{:S(2)}) %collective-permute-start.11) | collective-permute-done | bytes 532512 | tf_op jit(solution)/shard_map/ppermute | solution.py:358
  44.3 0.1 pad_maximum_fusion
  44.4 0.0 collective-permute-done.13.refs_1_
  44.4 3.2 %attend.7 = (f32[8,128]{1,0:T(8,128)S(1)}, f32[2,4,512,128]{3,2,1,0:T(8,128)S(1)}, f32[2,4,512,256]{3,2,1,0:T(8,128)S(1)}, bf16[2,32,512,128]{3,2,1,0:T(8,128)(2,1)S(1)}) custom-call(bf16[2,4,512,128]{3,2,1,0:T(8,128)(2,1)S(1)} %bitcast.12, ...), custom_call_target="tpu_custom_call", output_to_operand_aliasing={{0}: (4, {}), {1}: (5, {}), {2}: (6, {}), {3}: (7, {})} | custom-call | flops 1073741824 | bytes 4194304 | tf_op jit(solution)/shard_map/attend/pallas_call | solution.py:300
  47.6 0.1 collective-permute-start.14
  47.7 0.0 collective-permute-done.3
  47.7 0.0 collective-permute-done.15
  47.8 0.5 collective-permute-start.16
  48.3 0.7 %collective-permute-start.17 = (bf16[1040,128]{1,0:T(8,128)(2,1)S(1)}, bf16[1040,128]{1,0:T(8,128)(2,1)S(1)}, u32[]{:S(2)}, u32[]{:S(2)}) collective-permute-start(bf16[1040,128]{1,0:T(8,128)(2,1)S(1)} %collective-permute-done.3), channel_id=1, source_target_pairs={{0,6},{1,7},{2,4},{3,5},{4,1},{5,0},{6,3},{7,2},{8,14},{9,15},{10,... | collective-permute-start | bytes 798728 | tf_op jit(solution)/shard_map/ppermute | solution.py:358
  49.1 1.0 %collective-permute-start.4 = (bf16[1040,128]{1,0:T(8,128)(2,1)S(1)}, bf16[1040,128]{1,0:T(8,128)(2,1)S(1)}, u32[]{:S(2)}, u32[]{:S(2)}) collective-permute-start(bf16[1040,128]{1,0:T(8,128)(2,1)S(1)} %collective-permute-done.3), channel_id=1, source_target_pairs={{0,2},{1,3},{2,0},{3,1},{4,5},{5,4},{6,7},{7,6},{8,10},{9,11},{10,... | collective-permute-start | bytes 798728 | tf_op jit(solution)/shard_map/ppermute | solution.py:358
  50.0 1.5 %collective-permute-done.16.refs_3_ = bf16[3120,128]{1,0:T(8,128)(2,1)S(1)} collective-permute-done((bf16[3120,128]{1,0:T(8,128)(2,1)S(1)}, bf16[3120,128]{1,0:T(8,128)(2,1)S(1)}, u32[]{:S(2)}, u32[]{:S(2)}) %collective-permute-start.16) | collective-permute-done | bytes 798752 | tf_op jit(solution)/shard_map/ppermute | solution.py:358
  51.5 0.0 collective-permute-done.14.refs_1_
  51.5 7.0 %attend.8 = (f32[8,128]{1,0:T(8,128)S(1)}, f32[2,4,512,128]{3,2,1,0:T(8,128)S(1)}, f32[2,4,512,256]{3,2,1,0:T(8,128)S(1)}, bf16[2,32,512,128]{3,2,1,0:T(8,128)(2,1)S(1)}) custom-call(bf16[2,4,512,128]{3,2,1,0:T(8,128)(2,1)S(1)} %bitcast.13, ...), custom_call_target="tpu_custom_call", output_to_operand_aliasing={{0}: (5, {}), {1}: (6, {}), {2}: (7, {}), {3}: (8, {})} | custom-call | flops 1610612736 | bytes 4194304 | tf_op jit(solution)/shard_map/attend/pallas_call | solution.py:300
  58.5 0.0 collective-permute-done.17.refs_1_
  58.5 0.0 collective-permute-done.4.refs_0_
  58.5 4.2 %attend.9 = (bf16[128,32,128]{2,1,0:T(8,128)(2,1)}, f32[8,128]{1,0:T(8,128)S(1)}, f32[2,4,512,128]{3,2,1,0:T(8,128)S(1)}, f32[2,4,512,256]{3,2,1,0:T(8,128)S(1)}, bf16[2,32,512,128]{3,2,1,0:T(8,128)(2,1)S(1)}) custom-call(bf16[2,4,512,128]{3,2,1,0:T(8,128)(2,1)S(1)} %bitcast.14, ...), custom_call_target="tpu_custom_call", output_to_operand_aliasing={{1}: (3, {}), {2}: (4, {}), {3}: (5, {}), {4}: (6, {})} | custom-call | flops 268435456 | bytes 4194304 | tf_op jit(solution)/shard_map/attend/pallas_call | solution.py:300
  (8 shorter events, 0.2 us)
Async XLA Ops:
  2.1 5.6 %copy-start = (bf16[1040,128]{1,0:T(8,128)(2,1)S(1)}, bf16[1040,128]{1,0:T(8,128)(2,1)}, u32[]{:S(2)}) copy-start(bf16[1040,128]{1,0:T(8,128)(2,1)} %pack.1.own_ref) | copy-start | bytes 798724
  2.1 7.1 %collective-permute-start.6 = (bf16[1040,128]{1,0:T(8,128)(2,1)}, bf16[1040,128]{1,0:T(8,128)(2,1)S(1)}, u32[]{:S(2)}, u32[]{:S(2)}) collective-permute-start(bf16[1040,128]{1,0:T(8,128)(2,1)} %pack.1.own_ref), channel_id=1, source_target_pairs={{0,1},{1,0},{2,3},{3,2},{4,6},{5,7},{6,4},{7,5},{8,9},{9,8},{10,11... | collective-permute-start | bytes 798728 | tf_op jit(solution)/shard_map/ppermute | solution.py:358
  3.6 8.3 %collective-permute-start = (bf16[1040,128]{1,0:T(8,128)(2,1)}, bf16[1040,128]{1,0:T(8,128)(2,1)S(1)}, u32[]{:S(2)}, u32[]{:S(2)}) collective-permute-start(bf16[1040,128]{1,0:T(8,128)(2,1)} %pack.1.own_ref), channel_id=1, source_target_pairs={{0,8},{1,9},{2,10},{3,11},{4,12},{5,13},{6,14},{7,15},{8,24},{9,25... | collective-permute-start | bytes 798728 | tf_op jit(solution)/shard_map/ppermute | solution.py:358
  9.2 9.8 %collective-permute-start.7 = (bf16[2080,128]{1,0:T(8,128)(2,1)S(1)}, bf16[2080,128]{1,0:T(8,128)(2,1)S(1)}, u32[]{:S(2)}, u32[]{:S(2)}) collective-permute-start(bf16[2080,128]{1,0:T(8,128)(2,1)S(1)} %pad_maximum_fusion.2.refs_0_), channel_id=1, source_target_pairs={{0,2},{1,3},{2,0},{3,1},{4,5},{5,4},{6,7},{7,6},{8,10},{9,11},{10,... | collective-permute-start | bytes 1597448 | tf_op jit(solution)/shard_map/ppermute | solution.py:358
  11.9 14.5 %collective-permute-start.9 = (bf16[2080,128]{1,0:T(8,128)(2,1)S(1)}, bf16[2080,128]{1,0:T(8,128)(2,1)S(1)}, u32[]{:S(2)}, u32[]{:S(2)}) collective-permute-start(bf16[2080,128]{1,0:T(8,128)(2,1)S(1)} %pad_maximum_fusion.2.refs_0_), channel_id=1, source_target_pairs={{0,4},{1,5},{2,6},{3,7},{4,0},{5,1},{6,2},{7,3},{8,12},{9,13},{10,... | collective-permute-start | bytes 1597448 | tf_op jit(solution)/shard_map/ppermute | solution.py:358
  11.9 9.6 %collective-permute-start.1 = (bf16[1040,128]{1,0:T(8,128)(2,1)S(1)}, bf16[1040,128]{1,0:T(8,128)(2,1)S(1)}, u32[]{:S(2)}, u32[]{:S(2)}) collective-permute-start(bf16[1040,128]{1,0:T(8,128)(2,1)S(1)} %collective-permute-done), channel_id=1, source_target_pairs={{0,8},{1,9},{2,10},{3,11},{4,12},{5,13},{6,14},{7,15},{8,24},{9,25... | collective-permute-start | bytes 798728 | tf_op jit(solution)/shard_map/ppermute | solution.py:358
  15.2 11.6 %collective-permute-start.8 = (bf16[1040,128]{1,0:T(8,128)(2,1)S(1)}, bf16[1040,128]{1,0:T(8,128)(2,1)S(1)}, u32[]{:S(2)}, u32[]{:S(2)}) collective-permute-start(bf16[1040,128]{1,0:T(8,128)(2,1)S(1)} %collective-permute-done), channel_id=1, source_target_pairs={{0,1},{1,0},{2,3},{3,2},{4,6},{5,7},{6,4},{7,5},{8,9},{9,8},{10,11... | collective-permute-start | bytes 798728 | tf_op jit(solution)/shard_map/ppermute | solution.py:358
  19.0 8.5 %collective-permute-start.10 = (bf16[2080,128]{1,0:T(8,128)(2,1)S(1)}, bf16[2080,128]{1,0:T(8,128)(2,1)S(1)}, u32[]{:S(2)}, u32[]{:S(2)}) collective-permute-start(bf16[2080,128]{1,0:T(8,128)(2,1)S(1)} %collective-permute-done.7.refs_0_), channel_id=1, source_target_pairs={{0,4},{1,5},{2,6},{3,7},{4,0},{5,1},{6,2},{7,3},{8,12},{9,13},{10,... | collective-permute-start | bytes 1597448 | tf_op jit(solution)/shard_map/ppermute | solution.py:358
  21.5 9.9 %collective-permute-start.5 = (bf16[1040,128]{1,0:T(8,128)(2,1)S(1)}, bf16[1040,128]{1,0:T(8,128)(2,1)S(1)}, u32[]{:S(2)}, u32[]{:S(2)}) collective-permute-start(bf16[1040,128]{1,0:T(8,128)(2,1)S(1)} %collective-permute-done.1), channel_id=1, source_target_pairs={{0,1},{1,0},{2,3},{3,2},{4,6},{5,7},{6,4},{7,5},{8,9},{9,8},{10,11... | collective-permute-start | bytes 798728 | tf_op jit(solution)/shard_map/ppermute | solution.py:358
  23.0 13.3 %collective-permute-start.2 = (bf16[1040,128]{1,0:T(8,128)(2,1)S(1)}, bf16[1040,128]{1,0:T(8,128)(2,1)S(1)}, u32[]{:S(2)}, u32[]{:S(2)}) collective-permute-start(bf16[1040,128]{1,0:T(8,128)(2,1)S(1)} %collective-permute-done.1), channel_id=1, source_target_pairs={{0,8},{1,9},{2,10},{3,11},{4,12},{5,13},{6,14},{7,15},{8,24},{9,25... | collective-permute-start | bytes 798728 | tf_op jit(solution)/shard_map/ppermute | solution.py:358
  26.9 9.3 %collective-permute-start.12 = (bf16[2080,128]{1,0:T(8,128)(2,1)S(1)}, bf16[2080,128]{1,0:T(8,128)(2,1)S(1)}, u32[]{:S(2)}, u32[]{:S(2)}) collective-permute-start(bf16[2080,128]{1,0:T(8,128)(2,1)S(1)} %constant_dynamic-update-slice_fusion.refs_1_), channel_id=1, source_target_pairs={{0,2},{1,3},{2,0},{3,1},{4,5},{5,4},{6,7},{7,6},{8,10},{9,11},{10,... | collective-permute-start | bytes 1597448 | tf_op jit(solution)/shard_map/ppermute | solution.py:358
  31.5 12.8 %collective-permute-start.11 = (bf16[2080,128]{1,0:T(8,128)(2,1)S(1)}, bf16[2080,128]{1,0:T(8,128)(2,1)S(1)}, u32[]{:S(2)}, u32[]{:S(2)}) collective-permute-start(bf16[2080,128]{1,0:T(8,128)(2,1)S(1)} %constant_dynamic-update-slice_fusion.2.refs_2_), channel_id=1, source_target_pairs={{0,2},{1,3},{2,0},{3,1},{4,5},{5,4},{6,7},{7,6},{8,10},{9,11},{10,... | collective-permute-start | bytes 1597448 | tf_op jit(solution)/shard_map/ppermute | solution.py:358
  36.3 8.1 %collective-permute-start.13 = (bf16[4160,128]{1,0:T(8,128)(2,1)S(1)}, bf16[4160,128]{1,0:T(8,128)(2,1)S(1)}, u32[]{:S(2)}, u32[]{:S(2)}) collective-permute-start(bf16[4160,128]{1,0:T(8,128)(2,1)S(1)} %pad_maximum_fusion.1), channel_id=1, source_target_pairs={{0,4},{1,5},{2,6},{3,7},{4,0},{5,1},{6,2},{7,3},{8,12},{9,13},{10,... | collective-permute-start | bytes 3194888 | tf_op jit(solution)/shard_map/ppermute | solution.py:358
  36.4 11.3 %collective-permute-start.3 = (bf16[1040,128]{1,0:T(8,128)(2,1)S(1)}, bf16[1040,128]{1,0:T(8,128)(2,1)S(1)}, u32[]{:S(2)}, u32[]{:S(2)}) collective-permute-start(bf16[1040,128]{1,0:T(8,128)(2,1)S(1)} %collective-permute-done.2), channel_id=1, source_target_pairs={{0,1},{1,0},{2,3},{3,2},{4,6},{5,7},{6,4},{7,5},{8,9},{9,8},{10,11... | collective-permute-start | bytes 798728 | tf_op jit(solution)/shard_map/ppermute | solution.py:358
  37.0 10.8 %collective-permute-start.15 = (bf16[1040,128]{1,0:T(8,128)(2,1)S(1)}, bf16[1040,128]{1,0:T(8,128)(2,1)S(1)}, u32[]{:S(2)}, u32[]{:S(2)}) collective-permute-start(bf16[1040,128]{1,0:T(8,128)(2,1)S(1)} %collective-permute-done.2), channel_id=1, source_target_pairs={{0,2},{1,3},{2,0},{3,1},{4,5},{5,4},{6,7},{7,6},{8,10},{9,11},{10,... | collective-permute-start | bytes 798728 | tf_op jit(solution)/shard_map/ppermute | solution.py:358
  47.6 3.9 %collective-permute-start.14 = (bf16[4160,128]{1,0:T(8,128)(2,1)S(1)}, bf16[4160,128]{1,0:T(8,128)(2,1)S(1)}, u32[]{:S(2)}, u32[]{:S(2)}) collective-permute-start(bf16[4160,128]{1,0:T(8,128)(2,1)S(1)} %pad_maximum_fusion), channel_id=1, source_target_pairs={{0,4},{1,5},{2,6},{3,7},{4,0},{5,1},{6,2},{7,3},{8,12},{9,13},{10,... | collective-permute-start | bytes 3194888 | tf_op jit(solution)/shard_map/ppermute | solution.py:358
  47.8 3.7 %collective-permute-start.16 = (bf16[3120,128]{1,0:T(8,128)(2,1)S(1)}, bf16[3120,128]{1,0:T(8,128)(2,1)S(1)}, u32[]{:S(2)}, u32[]{:S(2)}) collective-permute-start(bf16[3120,128]{1,0:T(8,128)(2,1)S(1)} %constant_dynamic-update-slice_fusion.4.refs_2_), channel_id=1, source_target_pairs={{0,4},{1,5},{2,6},{3,7},{4,0},{5,1},{6,2},{7,3},{8,12},{9,13},{10,... | collective-permute-start | bytes 2396168 | tf_op jit(solution)/shard_map/ppermute | solution.py:358
  48.3 10.2 %collective-permute-start.17 = (bf16[1040,128]{1,0:T(8,128)(2,1)S(1)}, bf16[1040,128]{1,0:T(8,128)(2,1)S(1)}, u32[]{:S(2)}, u32[]{:S(2)}) collective-permute-start(bf16[1040,128]{1,0:T(8,128)(2,1)S(1)} %collective-permute-done.3), channel_id=1, source_target_pairs={{0,6},{1,7},{2,4},{3,5},{4,1},{5,0},{6,3},{7,2},{8,14},{9,15},{10,... | collective-permute-start | bytes 798728 | tf_op jit(solution)/shard_map/ppermute | solution.py:358
  49.1 9.4 %collective-permute-start.4 = (bf16[1040,128]{1,0:T(8,128)(2,1)S(1)}, bf16[1040,128]{1,0:T(8,128)(2,1)S(1)}, u32[]{:S(2)}, u32[]{:S(2)}) collective-permute-start(bf16[1040,128]{1,0:T(8,128)(2,1)S(1)} %collective-permute-done.3), channel_id=1, source_target_pairs={{0,2},{1,3},{2,0},{3,1},{4,5},{5,4},{6,7},{7,6},{8,10},{9,11},{10,... | collective-permute-start | bytes 798728 | tf_op jit(solution)/shard_map/ppermute | solution.py:358
